TPU v7x, 32 devices: a whole 2x2x4 slice. The times are simulated.
32 devices in a mesh: facet: 8 (over y, x, core), sub: 4 (over z).
Axes of the slice: x: 2, y: 2, z: 4, core: 2. Of those that a mesh axis runs over, the one named last changes fastest.
Arguments:
- strips: bfloat16 [8, 32, 8192], P('facet', 'sub'), may hold values from -6 to 6
- facet_offset: int32 [8], replicated, may hold values from 0 to 448
- subgrid_offset: int32 [32], replicated, may hold values from 0 to 4095
- owner: int32 [32], replicated, may hold values from 0 to 31, as said below
- screen_index: int32 [32], replicated, may hold values from 0 to 15
- screens: bfloat16 [16, 32, 1024], replicated, may hold values from -1 to 1, as said below
- grid_weight: float32 [128, 512], P(('facet', 'sub')), may hold values from 0.3 to 3
Outputs:
- facet_out: float32 [8, 32, 8192], P('facet', 'sub')
Inputs may be any that keep to these rules, and one draw needn't show every extreme that they name: `owner`: device number i * 4 + k is the device at index i of facet and k of sub. No device owns more than 4 subgrids, and some device owns exactly 4. `screens`: element g and element 512 + g of a row are the cosine and sine of one phase.
All inputs are finite; a program needn't handle non-finite values.
Results may differ from a plain program's by a relative error of at most 0.0059.
Values may be sent and summed in bfloat16 or wider, within the bound.
No kernel may reach another device: no remote copies, remote signals or barrier semaphores. Data moves between devices by JAX's collectives and lax.ppermute only.
A program may use at most 64 MiB of HBM per device.

v0:
```python
import math

import jax
import jax.numpy as jnp
from jax import lax
from jax.sharding import PartitionSpec as P

FL = 4096
M = 64
SG = 512
W = 8
CAP = 4


def table_block(start, length, count):
    points = jnp.arange(length, dtype=jnp.int32)
    orders = start + jnp.arange(count, dtype=jnp.int32)
    turn_counts = points[:, None] * orders[None, :] % length
    angles = turn_counts.astype(jnp.float32) * (2.0 * math.pi / length)
    factor = 1.0 / math.sqrt(length)
    cosine = jnp.cos(angles) * factor
    sine_part = jnp.sin(angles) * factor
    upper = jnp.concatenate([cosine, -sine_part], axis=1)
    lower = jnp.concatenate([sine_part, cosine], axis=1)
    return jnp.concatenate([upper, lower], axis=0).astype(jnp.bfloat16)


def full_spectrum(rows):
    width = min(FL, 512)
    blocks = FL // width
    row_count = rows.shape[0]

    def one_block(index):
        block = table_block(index * width, FL, width)
        product = jnp.dot(rows, block, preferred_element_type=jnp.float32)
        return product.astype(jnp.bfloat16).reshape(row_count, 2, width)

    pieces = lax.map(one_block, jnp.arange(blocks, dtype=jnp.int32))
    return jnp.transpose(pieces, (1, 2, 0, 3)).reshape(row_count, 2 * FL)


def synthesize(spectrum):
    width = min(FL, 512)
    blocks = FL // width
    row_count = spectrum.shape[0]
    shaped = spectrum.reshape(row_count, 2, blocks, width)

    def add_block(index, accumulated):
        block = table_block(index * width, FL, width)
        piece = lax.dynamic_index_in_dim(shaped, index, 2, keepdims=False).reshape(
            row_count, 2 * width
        )
        return accumulated + lax.dot_general(
            piece, block, (((1,), (1,)), ((), ())), preferred_element_type=jnp.float32
        )

    return lax.fori_loop(
        jnp.int32(0), jnp.int32(blocks), add_block, jnp.zeros((row_count, 2 * FL), jnp.float32)
    )


def send_forward(buffer):
    return lax.all_to_all(buffer, ("facet", "sub"), split_axis=0, concat_axis=0, tiled=True)


def send_back(buffer):
    return lax.all_to_all(buffer, ("facet", "sub"), split_axis=0, concat_axis=0, tiled=True)


def serve_subgrids(arrived, placement, screen_rows, weight_rows, facet_count, strip_count):
    slot_count = weight_rows.shape[0]
    shaped = arrived.reshape(facet_count, strip_count, slot_count, W, 2, M)
    subgrid_sum = jnp.einsum(
        "fskwrm,fmg->kswrg", shaped, placement, preferred_element_type=jnp.float32
    )
    screen_f = screen_rows.reshape(slot_count, strip_count, W, 2, SG).astype(jnp.float32)
    weighting = weight_rows[:, None, None, :]
    real_part = (
        subgrid_sum[:, :, :, 0] * screen_f[:, :, :, 0]
        - subgrid_sum[:, :, :, 1] * screen_f[:, :, :, 1]
    ) * weighting
    imag_part = (
        subgrid_sum[:, :, :, 0] * screen_f[:, :, :, 1]
        + subgrid_sum[:, :, :, 1] * screen_f[:, :, :, 0]
    ) * weighting
    processed = jnp.stack([real_part, imag_part], axis=3).astype(jnp.bfloat16)
    extracted = jnp.einsum(
        "kswrg,fmg->fskwrm", processed, placement, preferred_element_type=jnp.float32
    )
    return extracted.astype(jnp.bfloat16).reshape(facet_count * strip_count, slot_count, W, 2 * M)


def local(strips, facet_offset, subgrid_offset, owner, screen_index, screens, grid_weight):
    facet_count = lax.axis_size("facet")
    strip_count = lax.axis_size("sub")
    subgrid_total = owner.shape[0]
    facet_here = lax.axis_index("facet")
    my_index = facet_here * strip_count + lax.axis_index("sub")
    my_offset = facet_offset[facet_here]
    order_ids = jnp.arange(M, dtype=jnp.int32)
    chosen_freq = (subgrid_offset[:, None] + my_offset + order_ids[None, :]) % FL
    spectrum = full_spectrum(strips[0])
    real_part = spectrum[:, chosen_freq]
    imag_part = spectrum[:, FL + chosen_freq]
    contributions = jnp.transpose(jnp.concatenate([real_part, imag_part], axis=2), (1, 0, 2))
    frequency_ids = jnp.arange(SG, dtype=jnp.int32)
    placement = (
        frequency_ids[None, None, :] == facet_offset[:, None, None] + order_ids[None, :, None]
    ).astype(jnp.bfloat16)
    device_ids = jnp.arange(subgrid_total, dtype=jnp.int32)
    onehot = (owner[:, None] == device_ids[None, :]).astype(jnp.int32)
    before = jnp.cumsum(onehot, axis=0) - onehot
    slot = jnp.sum(before * onehot, axis=1)
    target = owner * CAP + slot
    outgoing = (
        jnp.zeros((subgrid_total * CAP, W, 2 * M), jnp.bfloat16).at[target].set(contributions)
    )
    arrived = send_forward(outgoing.reshape(subgrid_total, CAP, W, 2 * M))
    slot_ids = jnp.arange(CAP, dtype=jnp.int32)
    picked = ((owner == my_index)[None, :] & (slot[None, :] == slot_ids[:, None])).astype(jnp.int32)
    held_subgrid = jnp.sum(picked * device_ids[None, :], axis=1)
    screen_rows = screens[screen_index[held_subgrid]]
    answer = serve_subgrids(arrived, placement, screen_rows, grid_weight, facet_count, strip_count)
    coming_back = send_back(answer)
    returned = coming_back.reshape(subgrid_total * CAP, W, 2 * M)[target]
    rows_f = jnp.transpose(returned.astype(jnp.float32), (1, 0, 2))
    back = jnp.zeros((W, 2, FL), jnp.float32)
    back = back.at[:, 0, chosen_freq].add(rows_f[:, :, :M])
    back = back.at[:, 1, chosen_freq].add(rows_f[:, :, M:])
    accumulated = synthesize(back.reshape(W, 2 * FL).astype(jnp.bfloat16))
    return accumulated[None]


def solution(mesh):
    in_specs = (P("facet", "sub", None), P(), P(), P(), P(), P(), P(("facet", "sub"), None))
    out_specs = P("facet", "sub", None)
    return jax.shard_map(local, mesh=mesh, in_specs=in_specs, out_specs=out_specs, check_vma=False)
```

profile of v0, /device:TPU:0, one launch (start us, length us, event | category | flops | bytes accessed | tf_op | source)
XLA Modules:
  0.0 1106.2 jit_solution(15575434909648798933)
XLA Ops:
  2.4 1.2 dynamic_slice.17
  3.6 1.3 broadcast_add_fusion
  5.2 432.5 %while.25 = (s32[]{:T(128)}, bf16[8,8,2,512]{3,1,2,0:T(8,128)(2,1)S(1)}, s32[8]{0:T(128)S(1)}, bf16[8,8192]{1,0:T(8,128)(2,1)}, s32[]{:T(128)}, /*index=5*/s32[1]{0:T(128)}) while((s32[]{:T(128)}, bf16[8,8,2,512]{3,1,2,0:T(8,128)(2,1)S(1)}, s32[8]{0:T(128)S(1)}, bf16[8,8192]{1,0:T(8,128)(2,1)}, s32[]{:T(128)}, /*index=5*/s32[1]{0:T(128)}) %tuple.77), condition=%wide.region_3.4_spmd, body=%wide.region_2.3_spmd.sunk | while | flops 243278336 | bytes 25874568 | solution.py:38
  6.4 37.2 %negate_convert_fusion.4 = (bf16[4096,512]{1,0:T(8,128)(2,1)}, bf16[4096,512]{1,0:T(8,128)(2,1)}, bf16[4096,512]{1,0:T(8,128)(2,1)}) fusion(s32[512]{0:T(512)S(1)} %iota_add_fusion.5), kind=kLoop, calls=%fused_computation.22.clone.1 | loop fusion | flops 41943040 | bytes 12584960 | tf_op jit(solution)/shard_map/convert.5
  43.7 15.5 %fusion.75 = bf16[1024,8]{0,1:T(8,128)(2,1)S(1)} fusion(bf16[8,8192]{1,0:T(8,128)(2,1)S(1)} %copy-done.7, bf16[4096,512]{1,0:T(8,128)(2,1)} %get-tuple-element.209, bf16[4096,512]{1,0:T(8,128)(2,1)} %get-tuple-element.210, bf16[4096,512]{1,0:T(8,128)(2,1)} %get-tuple-element.211), kind=kOutput, calls=%fused_computation.29.clone.1 | convolution fusion | flops 201334784 | bytes 12730368 | tf_op jit(solution)/shard_map/while/body/eval_jaxpr/dot_general | solution.py:35
  60.5 37.2 %negate_convert_fusion.4 = (bf16[4096,512]{1,0:T(8,128)(2,1)}, bf16[4096,512]{1,0:T(8,128)(2,1)}, bf16[4096,512]{1,0:T(8,128)(2,1)}) fusion(s32[512]{0:T(512)S(1)} %iota_add_fusion.5), kind=kLoop, calls=%fused_computation.22.clone.1 | loop fusion | flops 41943040 | bytes 12584960 | tf_op jit(solution)/shard_map/convert.5
  97.7 15.5 %fusion.75 = bf16[1024,8]{0,1:T(8,128)(2,1)S(1)} fusion(bf16[8,8192]{1,0:T(8,128)(2,1)S(1)} %copy-done.7, bf16[4096,512]{1,0:T(8,128)(2,1)} %get-tuple-element.209, bf16[4096,512]{1,0:T(8,128)(2,1)} %get-tuple-element.210, bf16[4096,512]{1,0:T(8,128)(2,1)} %get-tuple-element.211), kind=kOutput, calls=%fused_computation.29.clone.1 | convolution fusion | flops 201334784 | bytes 12730368 | tf_op jit(solution)/shard_map/while/body/eval_jaxpr/dot_general | solution.py:35
  114.6 37.2 %negate_convert_fusion.4 = (bf16[4096,512]{1,0:T(8,128)(2,1)}, bf16[4096,512]{1,0:T(8,128)(2,1)}, bf16[4096,512]{1,0:T(8,128)(2,1)}) fusion(s32[512]{0:T(512)S(1)} %iota_add_fusion.5), kind=kLoop, calls=%fused_computation.22.clone.1 | loop fusion | flops 41943040 | bytes 12584960 | tf_op jit(solution)/shard_map/convert.5
  151.8 15.5 %fusion.75 = bf16[1024,8]{0,1:T(8,128)(2,1)S(1)} fusion(bf16[8,8192]{1,0:T(8,128)(2,1)S(1)} %copy-done.7, bf16[4096,512]{1,0:T(8,128)(2,1)} %get-tuple-element.209, bf16[4096,512]{1,0:T(8,128)(2,1)} %get-tuple-element.210, bf16[4096,512]{1,0:T(8,128)(2,1)} %get-tuple-element.211), kind=kOutput, calls=%fused_computation.29.clone.1 | convolution fusion | flops 201334784 | bytes 12730368 | tf_op jit(solution)/shard_map/while/body/eval_jaxpr/dot_general | solution.py:35
  168.6 37.2 %negate_convert_fusion.4 = (bf16[4096,512]{1,0:T(8,128)(2,1)}, bf16[4096,512]{1,0:T(8,128)(2,1)}, bf16[4096,512]{1,0:T(8,128)(2,1)}) fusion(s32[512]{0:T(512)S(1)} %iota_add_fusion.5), kind=kLoop, calls=%fused_computation.22.clone.1 | loop fusion | flops 41943040 | bytes 12584960 | tf_op jit(solution)/shard_map/convert.5
  205.8 15.5 %fusion.75 = bf16[1024,8]{0,1:T(8,128)(2,1)S(1)} fusion(bf16[8,8192]{1,0:T(8,128)(2,1)S(1)} %copy-done.7, bf16[4096,512]{1,0:T(8,128)(2,1)} %get-tuple-element.209, bf16[4096,512]{1,0:T(8,128)(2,1)} %get-tuple-element.210, bf16[4096,512]{1,0:T(8,128)(2,1)} %get-tuple-element.211), kind=kOutput, calls=%fused_computation.29.clone.1 | convolution fusion | flops 201334784 | bytes 12730368 | tf_op jit(solution)/shard_map/while/body/eval_jaxpr/dot_general | solution.py:35
  222.7 37.2 %negate_convert_fusion.4 = (bf16[4096,512]{1,0:T(8,128)(2,1)}, bf16[4096,512]{1,0:T(8,128)(2,1)}, bf16[4096,512]{1,0:T(8,128)(2,1)}) fusion(s32[512]{0:T(512)S(1)} %iota_add_fusion.5), kind=kLoop, calls=%fused_computation.22.clone.1 | loop fusion | flops 41943040 | bytes 12584960 | tf_op jit(solution)/shard_map/convert.5
  259.9 15.5 %fusion.75 = bf16[1024,8]{0,1:T(8,128)(2,1)S(1)} fusion(bf16[8,8192]{1,0:T(8,128)(2,1)S(1)} %copy-done.7, bf16[4096,512]{1,0:T(8,128)(2,1)} %get-tuple-element.209, bf16[4096,512]{1,0:T(8,128)(2,1)} %get-tuple-element.210, bf16[4096,512]{1,0:T(8,128)(2,1)} %get-tuple-element.211), kind=kOutput, calls=%fused_computation.29.clone.1 | convolution fusion | flops 201334784 | bytes 12730368 | tf_op jit(solution)/shard_map/while/body/eval_jaxpr/dot_general | solution.py:35
  276.7 37.2 %negate_convert_fusion.4 = (bf16[4096,512]{1,0:T(8,128)(2,1)}, bf16[4096,512]{1,0:T(8,128)(2,1)}, bf16[4096,512]{1,0:T(8,128)(2,1)}) fusion(s32[512]{0:T(512)S(1)} %iota_add_fusion.5), kind=kLoop, calls=%fused_computation.22.clone.1 | loop fusion | flops 41943040 | bytes 12584960 | tf_op jit(solution)/shard_map/convert.5
  314.0 15.5 %fusion.75 = bf16[1024,8]{0,1:T(8,128)(2,1)S(1)} fusion(bf16[8,8192]{1,0:T(8,128)(2,1)S(1)} %copy-done.7, bf16[4096,512]{1,0:T(8,128)(2,1)} %get-tuple-element.209, bf16[4096,512]{1,0:T(8,128)(2,1)} %get-tuple-element.210, bf16[4096,512]{1,0:T(8,128)(2,1)} %get-tuple-element.211), kind=kOutput, calls=%fused_computation.29.clone.1 | convolution fusion | flops 201334784 | bytes 12730368 | tf_op jit(solution)/shard_map/while/body/eval_jaxpr/dot_general | solution.py:35
  330.8 37.2 %negate_convert_fusion.4 = (bf16[4096,512]{1,0:T(8,128)(2,1)}, bf16[4096,512]{1,0:T(8,128)(2,1)}, bf16[4096,512]{1,0:T(8,128)(2,1)}) fusion(s32[512]{0:T(512)S(1)} %iota_add_fusion.5), kind=kLoop, calls=%fused_computation.22.clone.1 | loop fusion | flops 41943040 | bytes 12584960 | tf_op jit(solution)/shard_map/convert.5
  368.0 15.5 %fusion.75 = bf16[1024,8]{0,1:T(8,128)(2,1)S(1)} fusion(bf16[8,8192]{1,0:T(8,128)(2,1)S(1)} %copy-done.7, bf16[4096,512]{1,0:T(8,128)(2,1)} %get-tuple-element.209, bf16[4096,512]{1,0:T(8,128)(2,1)} %get-tuple-element.210, bf16[4096,512]{1,0:T(8,128)(2,1)} %get-tuple-element.211), kind=kOutput, calls=%fused_computation.29.clone.1 | convolution fusion | flops 201334784 | bytes 12730368 | tf_op jit(solution)/shard_map/while/body/eval_jaxpr/dot_general | solution.py:35
  384.8 37.2 %negate_convert_fusion.4 = (bf16[4096,512]{1,0:T(8,128)(2,1)}, bf16[4096,512]{1,0:T(8,128)(2,1)}, bf16[4096,512]{1,0:T(8,128)(2,1)}) fusion(s32[512]{0:T(512)S(1)} %iota_add_fusion.5), kind=kLoop, calls=%fused_computation.22.clone.1 | loop fusion | flops 41943040 | bytes 12584960 | tf_op jit(solution)/shard_map/convert.5
  422.1 15.5 %fusion.75 = bf16[1024,8]{0,1:T(8,128)(2,1)S(1)} fusion(bf16[8,8192]{1,0:T(8,128)(2,1)S(1)} %copy-done.7, bf16[4096,512]{1,0:T(8,128)(2,1)} %get-tuple-element.209, bf16[4096,512]{1,0:T(8,128)(2,1)} %get-tuple-element.210, bf16[4096,512]{1,0:T(8,128)(2,1)} %get-tuple-element.211), kind=kOutput, calls=%fused_computation.29.clone.1 | convolution fusion | flops 201334784 | bytes 12730368 | tf_op jit(solution)/shard_map/while/body/eval_jaxpr/dot_general | solution.py:35
  438.8 8.0 gather_fusion.1
  446.7 8.0 gather_fusion
  454.7 1.2 copy.36
  455.9 1.2 copy.37
  458.0 3.7 scatter_fusion
  461.8 7.3 all-to-all-start
  471.6 7.6 all-to-all-done
  482.2 2.9 all-to-all-start.1
  485.5 9.7 all-to-all-done.1
  496.6 13.6 %scatter_custom_fusion.1 = f32[8,8192]{0,1:T(8,128)} fusion(s32[2048]{0:T(1024)S(1)} %reshape.296, f32[2048,8]{1,0:T(8,128)S(1)} %bitcast.83, f32[]{:T(128)} %constant.147.clone.1), kind=kCustom, calls=%fused_computation.58 | custom fusion | flops 16384 | bytes 262148
  510.2 14.4 %scatter_fusion.1 = f32[8,8192]{0,1:T(8,128)} fusion(f32[8,8192]{0,1:T(8,128)} %scatter_custom_fusion.1, s32[2048]{0:T(1024)S(1)} %reshape.302, f32[2048,8]{1,0:T(8,128)S(1)} %bitcast.82), kind=kCustom, calls=%fused_computation.7 | custom fusion | flops 16384 | bytes 204800
  524.6 2.4 convert_element_type.72
  527.9 577.7 %while.26 = (s32[]{:T(128)}, f32[8,8192]{1,0:T(8,128)S(1)}, bf16[8,2,8,512]{3,1,0,2:T(2,128)(2,1)S(1)}, s32[]{:T(128)}, s32[]{:T(128)}, /*index=5*/s32[]{:T(128)}) while((s32[]{:T(128)}, f32[8,8192]{1,0:T(8,128)S(1)}, bf16[8,2,8,512]{3,1,0,2:T(2,128)(2,1)S(1)}, s32[]{:T(128)}, s32[]{:T(128)}, /*index=5*/s32[]{:T(128)}) %tuple.78), condition=%wide.region_9.10_spmd.clone, body=%wide.region_8.9_spmd.clone.sunk | while | flops 243401216 | bytes 25776236 | solution.py:57
  527.9 35.7 %negate_convert_fusion.5 = (bf16[4096,512]{1,0:T(8,128)(2,1)S(1)}, bf16[4096,512]{1,0:T(8,128)(2,1)S(1)}, bf16[4096,512]{1,0:T(8,128)(2,1)}) fusion(s32[512]{0:T(512)S(1)} %iota_add_fusion.6), kind=kLoop, calls=%fused_computation.48.clone.1 | loop fusion | flops 41943040 | bytes 12584960 | tf_op jit(solution)/shard_map/convert.11
  563.6 36.5 %fusion.78 = f32[8,8192]{1,0:T(8,128)S(1)} fusion(bf16[8,1024]{1,0:T(8,128)(2,1)S(1)} %bitcast.87, bf16[4096,512]{1,0:T(8,128)(2,1)} %get-tuple-element.215, bf16[4096,512]{1,0:T(8,128)(2,1)S(1)} %get-tuple-element.216, bf16[4096,512]{1,0:T(8,128)(2,1)S(1)} %get-tuple-element.217, f32[8,8192]{1,0:T(8,128)S(1)} %get-tuple-element.243, pred[]{:T(512)S(6)} %compare.40), kind=kOutput, calls=%fused_computation.44.clone.1 | convolution fusion | flops 201457664 | bytes 13123585 | tf_op jit(solution)/shard_map/while/body/dot_general | solution.py:53
  600.1 35.7 %negate_convert_fusion.5 = (bf16[4096,512]{1,0:T(8,128)(2,1)S(1)}, bf16[4096,512]{1,0:T(8,128)(2,1)S(1)}, bf16[4096,512]{1,0:T(8,128)(2,1)}) fusion(s32[512]{0:T(512)S(1)} %iota_add_fusion.6), kind=kLoop, calls=%fused_computation.48.clone.1 | loop fusion | flops 41943040 | bytes 12584960 | tf_op jit(solution)/shard_map/convert.11
  635.8 36.5 %fusion.78 = f32[8,8192]{1,0:T(8,128)S(1)} fusion(bf16[8,1024]{1,0:T(8,128)(2,1)S(1)} %bitcast.87, bf16[4096,512]{1,0:T(8,128)(2,1)} %get-tuple-element.215, bf16[4096,512]{1,0:T(8,128)(2,1)S(1)} %get-tuple-element.216, bf16[4096,512]{1,0:T(8,128)(2,1)S(1)} %get-tuple-element.217, f32[8,8192]{1,0:T(8,128)S(1)} %get-tuple-element.243, pred[]{:T(512)S(6)} %compare.40), kind=kOutput, calls=%fused_computation.44.clone.1 | convolution fusion | flops 201457664 | bytes 13123585 | tf_op jit(solution)/shard_map/while/body/dot_general | solution.py:53
  672.3 35.7 %negate_convert_fusion.5 = (bf16[4096,512]{1,0:T(8,128)(2,1)S(1)}, bf16[4096,512]{1,0:T(8,128)(2,1)S(1)}, bf16[4096,512]{1,0:T(8,128)(2,1)}) fusion(s32[512]{0:T(512)S(1)} %iota_add_fusion.6), kind=kLoop, calls=%fused_computation.48.clone.1 | loop fusion | flops 41943040 | bytes 12584960 | tf_op jit(solution)/shard_map/convert.11
  708.0 36.5 %fusion.78 = f32[8,8192]{1,0:T(8,128)S(1)} fusion(bf16[8,1024]{1,0:T(8,128)(2,1)S(1)} %bitcast.87, bf16[4096,512]{1,0:T(8,128)(2,1)} %get-tuple-element.215, bf16[4096,512]{1,0:T(8,128)(2,1)S(1)} %get-tuple-element.216, bf16[4096,512]{1,0:T(8,128)(2,1)S(1)} %get-tuple-element.217, f32[8,8192]{1,0:T(8,128)S(1)} %get-tuple-element.243, pred[]{:T(512)S(6)} %compare.40), kind=kOutput, calls=%fused_computation.44.clone.1 | convolution fusion | flops 201457664 | bytes 13123585 | tf_op jit(solution)/shard_map/while/body/dot_general | solution.py:53
  744.5 35.7 %negate_convert_fusion.5 = (bf16[4096,512]{1,0:T(8,128)(2,1)S(1)}, bf16[4096,512]{1,0:T(8,128)(2,1)S(1)}, bf16[4096,512]{1,0:T(8,128)(2,1)}) fusion(s32[512]{0:T(512)S(1)} %iota_add_fusion.6), kind=kLoop, calls=%fused_computation.48.clone.1 | loop fusion | flops 41943040 | bytes 12584960 | tf_op jit(solution)/shard_map/convert.11
  780.2 36.5 %fusion.78 = f32[8,8192]{1,0:T(8,128)S(1)} fusion(bf16[8,1024]{1,0:T(8,128)(2,1)S(1)} %bitcast.87, bf16[4096,512]{1,0:T(8,128)(2,1)} %get-tuple-element.215, bf16[4096,512]{1,0:T(8,128)(2,1)S(1)} %get-tuple-element.216, bf16[4096,512]{1,0:T(8,128)(2,1)S(1)} %get-tuple-element.217, f32[8,8192]{1,0:T(8,128)S(1)} %get-tuple-element.243, pred[]{:T(512)S(6)} %compare.40), kind=kOutput, calls=%fused_computation.44.clone.1 | convolution fusion | flops 201457664 | bytes 13123585 | tf_op jit(solution)/shard_map/while/body/dot_general | solution.py:53
  816.8 35.7 %negate_convert_fusion.5 = (bf16[4096,512]{1,0:T(8,128)(2,1)S(1)}, bf16[4096,512]{1,0:T(8,128)(2,1)S(1)}, bf16[4096,512]{1,0:T(8,128)(2,1)}) fusion(s32[512]{0:T(512)S(1)} %iota_add_fusion.6), kind=kLoop, calls=%fused_computation.48.clone.1 | loop fusion | flops 41943040 | bytes 12584960 | tf_op jit(solution)/shard_map/convert.11
  852.4 36.5 %fusion.78 = f32[8,8192]{1,0:T(8,128)S(1)} fusion(bf16[8,1024]{1,0:T(8,128)(2,1)S(1)} %bitcast.87, bf16[4096,512]{1,0:T(8,128)(2,1)} %get-tuple-element.215, bf16[4096,512]{1,0:T(8,128)(2,1)S(1)} %get-tuple-element.216, bf16[4096,512]{1,0:T(8,128)(2,1)S(1)} %get-tuple-element.217, f32[8,8192]{1,0:T(8,128)S(1)} %get-tuple-element.243, pred[]{:T(512)S(6)} %compare.40), kind=kOutput, calls=%fused_computation.44.clone.1 | convolution fusion | flops 201457664 | bytes 13123585 | tf_op jit(solution)/shard_map/while/body/dot_general | solution.py:53
  889.0 35.7 %negate_convert_fusion.5 = (bf16[4096,512]{1,0:T(8,128)(2,1)S(1)}, bf16[4096,512]{1,0:T(8,128)(2,1)S(1)}, bf16[4096,512]{1,0:T(8,128)(2,1)}) fusion(s32[512]{0:T(512)S(1)} %iota_add_fusion.6), kind=kLoop, calls=%fused_computation.48.clone.1 | loop fusion | flops 41943040 | bytes 12584960 | tf_op jit(solution)/shard_map/convert.11
  924.6 36.5 %fusion.78 = f32[8,8192]{1,0:T(8,128)S(1)} fusion(bf16[8,1024]{1,0:T(8,128)(2,1)S(1)} %bitcast.87, bf16[4096,512]{1,0:T(8,128)(2,1)} %get-tuple-element.215, bf16[4096,512]{1,0:T(8,128)(2,1)S(1)} %get-tuple-element.216, bf16[4096,512]{1,0:T(8,128)(2,1)S(1)} %get-tuple-element.217, f32[8,8192]{1,0:T(8,128)S(1)} %get-tuple-element.243, pred[]{:T(512)S(6)} %compare.40), kind=kOutput, calls=%fused_computation.44.clone.1 | convolution fusion | flops 201457664 | bytes 13123585 | tf_op jit(solution)/shard_map/while/body/dot_general | solution.py:53
  961.2 35.7 %negate_convert_fusion.5 = (bf16[4096,512]{1,0:T(8,128)(2,1)S(1)}, bf16[4096,512]{1,0:T(8,128)(2,1)S(1)}, bf16[4096,512]{1,0:T(8,128)(2,1)}) fusion(s32[512]{0:T(512)S(1)} %iota_add_fusion.6), kind=kLoop, calls=%fused_computation.48.clone.1 | loop fusion | flops 41943040 | bytes 12584960 | tf_op jit(solution)/shard_map/convert.11
  996.8 36.5 %fusion.78 = f32[8,8192]{1,0:T(8,128)S(1)} fusion(bf16[8,1024]{1,0:T(8,128)(2,1)S(1)} %bitcast.87, bf16[4096,512]{1,0:T(8,128)(2,1)} %get-tuple-element.215, bf16[4096,512]{1,0:T(8,128)(2,1)S(1)} %get-tuple-element.216, bf16[4096,512]{1,0:T(8,128)(2,1)S(1)} %get-tuple-element.217, f32[8,8192]{1,0:T(8,128)S(1)} %get-tuple-element.243, pred[]{:T(512)S(6)} %compare.40), kind=kOutput, calls=%fused_computation.44.clone.1 | convolution fusion | flops 201457664 | bytes 13123585 | tf_op jit(solution)/shard_map/while/body/dot_general | solution.py:53
  1033.4 35.7 %negate_convert_fusion.5 = (bf16[4096,512]{1,0:T(8,128)(2,1)S(1)}, bf16[4096,512]{1,0:T(8,128)(2,1)S(1)}, bf16[4096,512]{1,0:T(8,128)(2,1)}) fusion(s32[512]{0:T(512)S(1)} %iota_add_fusion.6), kind=kLoop, calls=%fused_computation.48.clone.1 | loop fusion | flops 41943040 | bytes 12584960 | tf_op jit(solution)/shard_map/convert.11
  1069.0 36.5 %fusion.78 = f32[8,8192]{1,0:T(8,128)S(1)} fusion(bf16[8,1024]{1,0:T(8,128)(2,1)S(1)} %bitcast.87, bf16[4096,512]{1,0:T(8,128)(2,1)} %get-tuple-element.215, bf16[4096,512]{1,0:T(8,128)(2,1)S(1)} %get-tuple-element.216, bf16[4096,512]{1,0:T(8,128)(2,1)S(1)} %get-tuple-element.217, f32[8,8192]{1,0:T(8,128)S(1)} %get-tuple-element.243, pred[]{:T(512)S(6)} %compare.40), kind=kOutput, calls=%fused_computation.44.clone.1 | convolution fusion | flops 201457664 | bytes 13123585 | tf_op jit(solution)/shard_map/while/body/dot_general | solution.py:53
  (126 shorter events, 18.2 us)
Async XLA Ops:
  0.0 469.9 %copy-start = (bf16[16,32,1024]{2,1,0:T(8,128)(2,1)S(1)}, bf16[16,32,1024]{2,1,0:T(8,128)(2,1)}, u32[]{:S(2)}) copy-start(bf16[16,32,1024]{2,1,0:T(8,128)(2,1)} %param.16) | copy-start | bytes 3145732
  6.4 37.2 %copy-start.7 = (bf16[8,8192]{1,0:T(8,128)(2,1)S(1)}, bf16[8,8192]{1,0:T(8,128)(2,1)}, u32[]{:S(2)}) copy-start(bf16[8,8192]{1,0:T(8,128)(2,1)} %get-tuple-element.233) | copy-start | bytes 393220 | tf_op jit(solution)/shard_map/while
  60.5 37.2 %copy-start.7 = (bf16[8,8192]{1,0:T(8,128)(2,1)S(1)}, bf16[8,8192]{1,0:T(8,128)(2,1)}, u32[]{:S(2)}) copy-start(bf16[8,8192]{1,0:T(8,128)(2,1)} %get-tuple-element.233) | copy-start | bytes 393220 | tf_op jit(solution)/shard_map/while
  114.5 37.2 %copy-start.7 = (bf16[8,8192]{1,0:T(8,128)(2,1)S(1)}, bf16[8,8192]{1,0:T(8,128)(2,1)}, u32[]{:S(2)}) copy-start(bf16[8,8192]{1,0:T(8,128)(2,1)} %get-tuple-element.233) | copy-start | bytes 393220 | tf_op jit(solution)/shard_map/while
  168.6 37.2 %copy-start.7 = (bf16[8,8192]{1,0:T(8,128)(2,1)S(1)}, bf16[8,8192]{1,0:T(8,128)(2,1)}, u32[]{:S(2)}) copy-start(bf16[8,8192]{1,0:T(8,128)(2,1)} %get-tuple-element.233) | copy-start | bytes 393220 | tf_op jit(solution)/shard_map/while
  222.7 37.2 %copy-start.7 = (bf16[8,8192]{1,0:T(8,128)(2,1)S(1)}, bf16[8,8192]{1,0:T(8,128)(2,1)}, u32[]{:S(2)}) copy-start(bf16[8,8192]{1,0:T(8,128)(2,1)} %get-tuple-element.233) | copy-start | bytes 393220 | tf_op jit(solution)/shard_map/while
  276.7 37.2 %copy-start.7 = (bf16[8,8192]{1,0:T(8,128)(2,1)S(1)}, bf16[8,8192]{1,0:T(8,128)(2,1)}, u32[]{:S(2)}) copy-start(bf16[8,8192]{1,0:T(8,128)(2,1)} %get-tuple-element.233) | copy-start | bytes 393220 | tf_op jit(solution)/shard_map/while
  330.8 37.2 %copy-start.7 = (bf16[8,8192]{1,0:T(8,128)(2,1)S(1)}, bf16[8,8192]{1,0:T(8,128)(2,1)}, u32[]{:S(2)}) copy-start(bf16[8,8192]{1,0:T(8,128)(2,1)} %get-tuple-element.233) | copy-start | bytes 393220 | tf_op jit(solution)/shard_map/while
  384.8 37.2 %copy-start.7 = (bf16[8,8192]{1,0:T(8,128)(2,1)S(1)}, bf16[8,8192]{1,0:T(8,128)(2,1)}, u32[]{:S(2)}) copy-start(bf16[8,8192]{1,0:T(8,128)(2,1)} %get-tuple-element.233) | copy-start | bytes 393220 | tf_op jit(solution)/shard_map/while
  437.6 31.4 %copy-start.3 = (s32[32]{0:T(128)S(1)}, s32[32]{0:T(128)}, u32[]{:S(2)}) copy-start(s32[32]{0:T(128)} %param.14) | copy-start | bytes 388
  437.7 31.6 %copy-start.1 = (s32[32]{0:T(128)S(1)}, s32[32]{0:T(128)}, u32[]{:S(2)}) copy-start(s32[32]{0:T(128)} %param.15) | copy-start | bytes 388
  437.7 33.3 %copy-start.5 = (s32[8]{0:T(128)S(1)}, s32[8]{0:T(128)}, u32[]{:S(2)}) copy-start(s32[8]{0:T(128)} %param.12) | copy-start | bytes 100
  461.8 17.5 %all-to-all-start = ((bf16[32,4,8,128]{3,2,1,0:T(8,128)(2,1)}), bf16[32,4,8,128]{3,2,1,0:T(8,128)(2,1)S(1)}, u32[]{:S(2)}, u32[]{:S(2)}) async-start(bf16[32,4,8,128]{3,2,1,0:T(8,128)(2,1)} %bitcast.15), calls=%async_computation | async-start | bytes 524288 | tf_op jit(solution)/shard_map/all_to_all | solution.py:63
  471.6 8.4 copy-start.2
  480.0 5.1 copy-start.4
  480.0 5.2 copy-start.6
  482.2 12.9 %all-to-all-start.1 = ((bf16[32,4,8,128]{3,2,1,0:T(8,128)(2,1)}), bf16[32,4,8,128]{3,2,1,0:T(8,128)(2,1)S(1)}, u32[]{:S(2)}, u32[]{:S(2)}) async-start(bf16[32,4,8,128]{3,2,1,0:T(8,128)(2,1)} %reshape.234), calls=%async_computation.1 | async-start | bytes 524288 | tf_op jit(solution)/shard_map/all_to_all | solution.py:67
  524.6 3.3 copy-start.8
  1105.5 0.7 copy-start.9
where the time goes:
time: 1110 us
  other arithmetic  618 us (56%)
  matrix products  417 us (38%)
  local copies, waits for them, and re-layouts  37.4 us (3%)
  waiting for transfers between devices  17.3 us (2%)
    another operation x17, other arithmetic  583 us
    dot_general x8, matrix products, add_block(): lax.dot_general(piece, block, (((1,), (1,)), ((), ())), preferred_element...  292 us
    dot_general x8, matrix products, one_block(): product = jnp.dot(rows, block, preferred_element_type=jnp.float32)  124 us
    unnamed x6, other arithmetic  28.2 us
  transfers between devices with their start and end apart: 2, of which 2 were waited for; matrix products, arithmetic and copies ran while one was open for 0% of the time, Pallas kernels for 0%

commit v1 on v0

v1 whole, which is shorter than its diff:
```python
import functools
import math

import jax
import jax.numpy as jnp
import numpy as np
from jax import lax
from jax.experimental import pallas as pl
from jax.experimental.pallas import tpu as pltpu
from jax.sharding import PartitionSpec as P

M = 64
CAP = 4
LANES = 128

BF = jnp.bfloat16
F32 = jnp.float32


def split(table):
    high = table.astype(BF).astype(np.float64)
    return high, table - high


def tables(length):
    chunks = length // LANES
    blocks = length // M
    g = np.arange(LANES)
    v = np.arange(LANES)
    u = np.arange(chunks)
    a = np.arange(blocks)
    outer = 2 * math.pi * ((u[:, None] * u[None, :]) % chunks) / chunks
    co, so = np.cos(outer), np.sin(outer)
    fwd = np.block([[co, so], [-so, co]])
    high, low = split(fwd)
    fwd2 = np.concatenate([high, low], axis=1)
    wide = 2 * math.pi * ((u[:, None] * g[None, :]) % chunks) / chunks
    cw, sw = np.cos(wide), np.sin(wide)
    inv = np.block([[cw, -sw], [sw, cw]])
    high, low = split(inv)
    inv2 = np.concatenate([high, low], axis=0)
    twist = 2 * math.pi * ((g[:, None] * v[None, :]) % length) / length
    turn = np.concatenate([np.cos(twist), np.sin(twist)], axis=0)
    coarse = 2 * math.pi * ((a[:, None] * v[None, :]) % blocks) / blocks
    ca, sa = np.cos(coarse) / math.sqrt(length), np.sin(coarse) / math.sqrt(length)
    chigh, clow = split(ca)
    shigh, slow = split(sa)
    pick = np.concatenate(
        [
            np.concatenate([chigh, shigh], axis=1),
            np.concatenate([-shigh, chigh], axis=1),
            np.concatenate([clow, slow], axis=1),
            np.concatenate([-slow, clow], axis=1),
        ],
        axis=0,
    )
    half = [t[:, :M].T for t in (chigh, shigh, clow, slow)]
    back = np.concatenate(
        [
            np.concatenate([half[0], -half[1], half[2], -half[3]], axis=1),
            np.concatenate([half[1], half[0], half[3], half[2]], axis=1),
        ],
        axis=0,
    )
    as_bf = lambda t: np.asarray(t, dtype=BF)
    return as_bf(fwd2), as_bf(inv2), np.asarray(turn, np.float32), as_bf(pick), as_bf(back)


def dot(x, y):
    return jnp.dot(x, y, preferred_element_type=F32)


def dot_t(x, y):
    return lax.dot_general(x, y, (((1,), (1,)), ((), ())), preferred_element_type=F32)


def start_of(where_ref, sub_ref, off_ref, j, length):
    return (sub_ref[j] + off_ref[where_ref[0]]) & (length - 1)


def choose(where_ref, sub_ref, off_ref, length):
    count = sub_ref.shape[0]
    blocks = length // M
    groups = []
    row = lax.broadcasted_iota(jnp.int32, (8, 4 * blocks), 0)
    for group in range(count // 8):
        value = jnp.zeros((8, 4 * blocks), jnp.int32)
        for r in range(8):
            block = start_of(where_ref, sub_ref, off_ref, group * 8 + r, length) // M
            value = jnp.where(row == r, block, value)
        groups.append(value)
    value = jnp.concatenate(groups, axis=0)
    lane = lax.broadcasted_iota(jnp.int32, value.shape, 1)
    return jnp.concatenate(
        [jnp.where(lane == value + q * blocks, 1.0, 0.0) for q in range(4)], axis=0
    ).astype(BF)


def forward_kernel(
    where_ref, sub_ref, off_ref, strips_ref, fwd_ref, turn_ref, pick_ref, out_ref, in_scr, out_scr
):
    rows = strips_ref.shape[1]
    length = strips_ref.shape[2] // 2
    chunks = length // LANES
    count = sub_ref.shape[0]
    for c in range(2 * chunks):
        piece = strips_ref[0, :, c * LANES : (c + 1) * LANES].astype(F32)
        in_scr[pl.ds(c, rows, stride=2 * chunks), :] = piece
    points = jnp.concatenate(
        [in_scr[r * 2 * chunks : (r + 1) * 2 * chunks, :].astype(BF) for r in range(rows)], axis=1
    )
    inner = dot(fwd_ref[...], jnp.concatenate([points, points], axis=0))
    twisted = []
    for r in range(rows):
        re = inner[:chunks, r * LANES : (r + 1) * LANES]
        im = inner[chunks:, r * LANES : (r + 1) * LANES]
        for q in range(LANES // chunks):
            cos = turn_ref[q * chunks : (q + 1) * chunks, :]
            sin = turn_ref[LANES + q * chunks : LANES + (q + 1) * chunks, :]
            both = jnp.concatenate([re * cos + im * sin, im * cos - re * sin], axis=1)
            twisted.append(both.astype(BF))
    twisted = jnp.concatenate(twisted, axis=0)
    chosen = choose(where_ref, sub_ref, off_ref, length)
    coarse = dot(chosen, pick_ref[...]).astype(BF)
    window = dot_t(coarse, twisted)
    window = window[: 2 * count] + window[2 * count :]
    for r in range(rows):
        out_scr[pl.ds(r, 2 * count, stride=rows), :] = window[:, r * LANES : (r + 1) * LANES]
    lane = lax.broadcasted_iota(jnp.int32, (rows, LANES), 1)

    def emit(j):
        shift = start_of(where_ref, sub_ref, off_ref, j, length) % M
        re = out_scr[j * rows : (j + 1) * rows, :]
        im = out_scr[(count + j) * rows : (count + j + 1) * rows, :]
        re = pltpu.roll(re, (LANES - shift) % LANES, 1)
        im = pltpu.roll(im, M - shift, 1)
        return jnp.where(lane < M, re, im)

    for j in range(0, count, 2):
        out_ref[j * rows : (j + 2) * rows, :] = jnp.concatenate([emit(j), emit(j + 1)], axis=0).astype(BF)


def backward_kernel(
    facets,
    subs,
    where_ref,
    sub_ref,
    off_ref,
    owner_ref,
    index_ref,
    *refs,
):
    arrived = refs[:facets]
    screens_ref, inv_ref, turn_ref, back_ref, out_ref = refs[facets : facets + 5]
    place_scr, cos_scr, sin_scr, weight_scr, re_scr, im_scr, out_scr, seen = refs[facets + 5 :]
    rows = out_ref.shape[1]
    length = out_ref.shape[2] // 2
    chunks = length // LANES
    count = sub_ref.shape[0]
    span = screens_ref.shape[2] // 2
    held = subs * CAP
    windows = count * rows
    mine = where_ref[0]
    my_sub = where_ref[1]
    my_off = off_ref[mine]

    shape = (LANES, 2 * LANES)
    row = lax.broadcasted_iota(jnp.int32, shape, 0)
    lane = lax.broadcasted_iota(jnp.int32, shape, 1)
    lane_part = jnp.where((lane // M == 1) | (lane // M == 2), 1, 0)
    apart = (lane_part - row // M) * 8192 + (lane % M - row % M)
    for s in range(facets):
        delta = off_ref[mine ^ s] - my_off
        place_scr[s * LANES : (s + 1) * LANES, :] = jnp.where(apart == delta, 1.0, 0.0).astype(BF)
    total = dot(arrived[0][:windows, :], place_scr[:LANES, :])
    for s in range(1, facets):
        total = total + dot(arrived[s][:windows, :], place_scr[s * LANES : (s + 1) * LANES, :])

    shape = (span, LANES)
    row = lax.broadcasted_iota(jnp.int32, shape, 0)
    lane = lax.broadcasted_iota(jnp.int32, shape, 1)
    hit = row == my_off + lane % M
    both = jnp.where(hit, 1.0, 0.0).astype(BF)
    signed = jnp.where(hit, jnp.where(lane < M, -1.0, 1.0), 0.0).astype(BF)
    kinds = screens_ref.shape[0]
    cosines = screens_ref[:, :, :span].reshape(kinds * rows, span)
    sines = screens_ref[:, :, span:].reshape(kinds * rows, span)
    cos_scr[...] = dot(cosines, both)
    sin_scr[...] = dot(sines, signed)
    pieces = []
    for s in range(facets):
        block = arrived[s][windows:, :].astype(F32)
        pieces.append(
            jnp.concatenate([block[c * held : (c + 1) * held] for c in range(span // LANES)], axis=1)
        )
    weight_scr[...] = dot(jnp.concatenate(pieces, axis=0).astype(BF), both)

    for o in range(facets * subs):
        seen[o] = 0
    lane = lax.broadcasted_iota(jnp.int32, (rows, LANES), 1)
    for j in range(count):
        who = owner_ref[j]
        slot = seen[who]
        seen[who] = slot + 1
        at = ((who // subs) ^ mine) * held + ((who % subs) ^ my_sub) * CAP + slot
        weight = weight_scr[pl.ds(at, 1), :]
        kind = pl.multiple_of(index_ref[j] * rows, rows)
        cos = cos_scr[pl.ds(kind, rows), :] * weight
        sin = sin_scr[pl.ds(kind, rows), :] * weight
        here = total[j * rows : (j + 1) * rows, :LANES]
        swapped = total[j * rows : (j + 1) * rows, LANES:]
        value = (here * cos + swapped * sin).astype(BF).astype(F32)
        shift = start_of(where_ref, sub_ref, off_ref, j, length) % M
        mask = (lane >= shift) & (lane < shift + M)
        re_scr[pl.ds(j, rows, stride=count), :] = jnp.where(mask, pltpu.roll(value, shift, 1), 0.0)
        im_scr[pl.ds(j, rows, stride=count), :] = jnp.where(mask, pltpu.roll(value, shift + M, 1), 0.0)

    chosen = choose(where_ref, sub_ref, off_ref, length)
    coarse = dot_t(back_ref[...], chosen).astype(BF)
    halves = []
    for scr in (re_scr, im_scr):
        halves.append(
            jnp.concatenate([scr[r * count : (r + 1) * count, :].astype(BF) for r in range(rows)], axis=1)
        )
    spread = jnp.concatenate(halves + halves, axis=0)
    inner = dot(coarse, spread)
    twisted = []
    for r in range(rows):
        re = inner[:M, r * LANES : (r + 1) * LANES]
        im = inner[M:, r * LANES : (r + 1) * LANES]
        for q in range(LANES // M):
            cos = turn_ref[q * M : (q + 1) * M, :]
            sin = turn_ref[LANES + q * M : LANES + (q + 1) * M, :]
            both = jnp.concatenate([re * cos - im * sin, re * sin + im * cos], axis=1)
            twisted.append(both.astype(BF))
    twisted = jnp.concatenate(twisted, axis=0)
    points = dot_t(inv_ref[...], twisted)
    points = points[: 2 * chunks] + points[2 * chunks :]
    for r in range(rows):
        out_scr[pl.ds(r, 2 * chunks, stride=rows), :] = points[:, r * LANES : (r + 1) * LANES]
    for c in range(2 * chunks):
        out_ref[0, :, c * LANES : (c + 1) * LANES] = out_scr[c * rows : (c + 1) * rows, :]


def local(strips, facet_offset, subgrid_offset, owner, screen_index, screens, grid_weight):
    facets = lax.axis_size("facet")
    subs = lax.axis_size("sub")
    rows = strips.shape[1]
    length = strips.shape[2] // 2
    chunks = length // LANES
    count = subgrid_offset.shape[0]
    span = grid_weight.shape[1]
    kinds = screens.shape[0]
    fwd, inv, turn, pick, back = [jnp.asarray(t) for t in tables(length)]
    mine = lax.axis_index("facet")
    my_sub = lax.axis_index("sub")
    where = jnp.stack([mine, my_sub]).astype(jnp.int32)
    smem = pl.BlockSpec(memory_space=pltpu.SMEM)
    vmem = pl.BlockSpec(memory_space=pltpu.VMEM)
    limit = pltpu.CompilerParams(vmem_limit_bytes=32 * 1024 * 1024)

    rows_here = grid_weight.astype(BF)
    gathered = [rows_here]
    for s in range(1, subs):
        gathered.append(lax.ppermute(rows_here, "sub", [(i, i ^ s) for i in range(subs)]))
    held = jnp.concatenate(gathered, axis=0)
    held = jnp.transpose(held.reshape(subs * CAP, span // LANES, LANES), (1, 0, 2)).reshape(-1, LANES)

    windows = pl.pallas_call(
        forward_kernel,
        out_shape=jax.ShapeDtypeStruct((count * rows, LANES), BF),
        in_specs=[smem] * 3 + [vmem] * 4,
        out_specs=vmem,
        scratch_shapes=[
            pltpu.VMEM((rows * 2 * chunks, LANES), F32),
            pltpu.VMEM((2 * count * rows, LANES), F32),
        ],
        compiler_params=limit,
    )(where, subgrid_offset, facet_offset, strips, fwd, turn, pick)
    payload = jnp.concatenate([windows, held], axis=0)

    arrived = [payload] + [None] * (facets - 1)
    for s in range(2, facets, 2):
        arrived[s] = lax.ppermute(payload, "facet", [(i, i ^ s) for i in range(facets)])
    for s in range(0, facets, 2):
        arrived[s + 1] = lax.ppermute(arrived[s], "facet", [(i, i ^ 1) for i in range(facets)])

    screens_here = lax.dynamic_slice_in_dim(screens, my_sub * rows, rows, 1)
    out = pl.pallas_call(
        functools.partial(backward_kernel, facets, subs),
        out_shape=jax.ShapeDtypeStruct((1, rows, 2 * length), F32),
        in_specs=[smem] * 5 + [vmem] * (facets + 4),
        out_specs=vmem,
        scratch_shapes=[
            pltpu.VMEM((facets * LANES, 2 * LANES), BF),
            pltpu.VMEM((kinds * rows, LANES), F32),
            pltpu.VMEM((kinds * rows, LANES), F32),
            pltpu.VMEM((facets * subs * CAP, LANES), F32),
            pltpu.VMEM((rows * count, LANES), F32),
            pltpu.VMEM((rows * count, LANES), F32),
            pltpu.VMEM((2 * chunks * rows, LANES), F32),
            pltpu.SMEM((facets * subs,), jnp.int32),
        ],
        compiler_params=limit,
    )(
        where,
        subgrid_offset,
        facet_offset,
        owner,
        screen_index,
        *arrived,
        screens_here,
        inv,
        turn,
        back,
    )
    return out


def solution(mesh):
    in_specs = (P("facet", "sub", None), P(), P(), P(), P(), P(), P(("facet", "sub"), None))
    out_specs = P("facet", "sub", None)
    return jax.shard_map(local, mesh=mesh, in_specs=in_specs, out_specs=out_specs, check_vma=False)
```

time: 1110 us -> 23.5 us (0.02)
  other arithmetic: 618 us -> 0.9 us
  matrix products: 417 us -> 0 us
  local copies, waits for them, and re-layouts: 37.4 us -> 3.35 us
  waiting for transfers between devices: 17.3 us -> 5.25 us
    another operation x18 -> x1, other arithmetic: 583 us -> 0.07 us  [local(): where = jnp.stack([mine, my_sub]).astype(jnp.int32)]
    dot_general x18 -> x0, matrix products: 417 us -> none  [the longest x8 292 us: add_block(): lax.dot_general(piece, block, (((1,), (1,)), ((), ())), preferred_element...]
    unnamed x6 -> x0, other arithmetic: 28.2 us -> none
    gather x7 -> x0, local copies, waits for them, and re-layouts: 20.2 us -> none  [the longest x2 9.22 us: local(): imag_part = spectrum[:, FL + chosen_freq]]
    all_to_all x2 -> x0, waiting for transfers between devices: 17.3 us -> none  [the longest x1 9.68 us: send_back(): lax.all_to_all(buffer, ('facet', 'sub'), split_axis=0, concat_axis=0, til...]
  transfers between devices with their start and end apart: 2 -> 10, of which waited for: 2 -> 5; matrix products, arithmetic and copies ran while one was open for 0% -> 0% of each run, Pallas kernels for 0% -> 6%
where the time goes in v1:
time: 23.5 us; the launch traced here: 23.3 us
  starting transfers between devices  9.25 us (39%)
  waiting for transfers between devices  5.25 us (22%)
  Pallas kernels  4.38 us (19%)
  local copies, waits for them, and re-layouts  3.35 us (14%)
  other arithmetic  0.9 us (4%)
    ppermute x3, starting transfers between devices, local(): lax.ppermute(rows_here, 'sub', [(i, i ^ s) for i in range(subs)])  5.62 us
    ppermute x3, waiting for transfers between devices, local(): lax.ppermute(payload, 'facet', [(i, i ^ s) for i in range(facets)])  4.01 us
    ppermute x3, starting transfers between devices, local(): lax.ppermute(payload, 'facet', [(i, i ^ s) for i in range(facets)])  3.55 us
    unnamed x24, local copies, waits for them, and re-layouts  3.33 us
    pallas_call x1, Pallas kernels, local(): pl.pallas_call(functools.partial(backward_kernel, facets, subs), out_shap...  3 us
    pallas_call x1, Pallas kernels, local(): pl.pallas_call(forward_kernel, out_shape=jax.ShapeDtypeStruct((count * ro...  1.38 us
    ppermute x4, waiting for transfers between devices, local(): lax.ppermute(arrived[s], 'facet', [(i, i ^ 1) for i in range(facets)])  1.23 us
    convert_element_type x1, other arithmetic, local(): rows_here = grid_weight.astype(BF)  0.8 us
  transfers between devices with their start and end apart: 10, of which 5 were waited for; matrix products, arithmetic and copies ran while one was open for 0% of the time, Pallas kernels for 6%

profile of v1, /device:TPU:0, one launch (start us, length us, event | category | flops | bytes accessed | tf_op | source)
XLA Modules:
  0.0 23.3 jit_solution(17457232225802583729)
XLA Ops:
  0.0 0.0 copy-start
  0.0 0.0 copy-start.7
  0.0 0.8 %convert_element_type.3 = bf16[4,512]{1,0:T(4,128)(2,1)S(1)} convert(f32[4,512]{1,0:T(4,128)} %param.18) | non-fusion elementwise | flops 2048 | bytes 12288 | tf_op jit(solution)/shard_map/convert_element_type | solution.py:262
  0.8 5.0 %collective-permute-start.2 = (bf16[4,512]{1,0:T(4,128)(2,1)S(1)}, bf16[4,512]{1,0:T(4,128)(2,1)S(1)}, u32[]{:S(2)}, u32[]{:S(2)}) collective-permute-start(bf16[4,512]{1,0:T(4,128)(2,1)S(1)} %convert_element_type.3), channel_id=1, source_target_pairs={{0,3},{1,2},{2,1},{3,0},{4,7},{5,6},{6,5},{7,4},{8,11},{9,10},{10,... | collective-permute-start | bytes 12296 | tf_op jit(solution)/shard_map/ppermute | solution.py:265
  5.9 0.0 collective-permute-start.1
  5.9 0.6 %collective-permute-start = (bf16[4,512]{1,0:T(4,128)(2,1)S(1)}, bf16[4,512]{1,0:T(4,128)(2,1)S(1)}, u32[]{:S(2)}, u32[]{:S(2)}) collective-permute-start(bf16[4,512]{1,0:T(4,128)(2,1)S(1)} %convert_element_type.3), channel_id=1, source_target_pairs={{0,1},{1,0},{2,3},{3,2},{4,5},{5,4},{6,7},{7,6},{8,9},{9,8},{10,11... | collective-permute-start | bytes 12296 | tf_op jit(solution)/shard_map/ppermute | solution.py:265
  6.4 0.0 copy-start.8
  6.4 0.0 copy-start.9
  6.4 0.1 pad_add_fusion.where_ref
  6.5 0.0 copy-done.7
  6.5 0.6 %copy-done.8 = s32[32]{0:T(128)S(1)} copy-done((s32[32]{0:T(128)S(1)}, s32[32]{0:T(128)}, u32[]{:S(2)}) %copy-start.8) | copy-done | bytes 152
  7.1 0.0 copy-done.9
  7.1 0.0 copy-start.1
  7.1 0.9 %copy-done.1 = f32[256,128]{1,0:T(8,128)S(1)} copy-done((f32[256,128]{1,0:T(8,128)S(1)}, f32[256,128]{1,0:T(8,128)}, u32[]{:S(2)}) %copy-start.1) | copy-done | bytes 131096
  8.0 0.0 copy-start.3
  8.0 0.9 %copy-done.3 = bf16[1,8,8192]{2,1,0:T(8,128)(2,1)S(1)} copy-done((bf16[1,8,8192]{2,1,0:T(8,128)(2,1)S(1)}, bf16[1,8,8192]{2,1,0:T(8,128)(2,1)}, u32[]{:S(2)}) %copy-start.3) | copy-done | bytes 131096
  8.9 0.0 copy-start.4
  8.9 0.9 %copy-done.4 = bf16[256,256]{1,0:T(8,128)(2,1)S(1)} copy-done((bf16[256,256]{1,0:T(8,128)(2,1)S(1)}, bf16[256,256]{1,0:T(8,128)(2,1)}, u32[]{:S(2)}) %copy-start.4) | copy-done | bytes 131096
  9.8 1.4 %shard_map.118 = bf16[256,128]{1,0:T(8,128)(2,1)S(1)} custom-call(s32[2]{0:T(128)S(1)} %pad_add_fusion.where_ref, s32[32]{0:T(128)S(1)} %copy-done.8, s32[8]{0:T(128)S(1)} %copy-done.9, bf16[1,8,8192]{2,1,0:T(8,128)(2,1)S(1)} %copy-done.3, bf16[64,128]{1,0:T(8,128)(2,1)S(1)} %copy-done.7, f32[256,128]{1,0:T(8,128)S(1)} %copy-done.1, ...), custom_call_target="tpu_custom_call" | custom-call | tf_op jit(solution)/shard_map/pallas_call | solution.py:269
  11.2 0.0 collective-permute-done.2
  11.2 0.0 collective-permute-done.1
  11.2 0.0 collective-permute-done
  11.3 2.7 %collective-permute-start.8 = (bf16[320,128]{1,0:T(8,128)(2,1)S(1)}, bf16[320,128]{1,0:T(8,128)(2,1)S(1)}, u32[]{:S(2)}, u32[]{:S(2)}) collective-permute-start(bf16[320,128]{1,0:T(8,128)(2,1)S(1)} %pad_maximum_fusion.refs_0_), channel_id=1, source_target_pairs={{0,24},{4,28},{8,16},{12,20},{16,8},{20,12},{24,0},{28,4},{1,25},{... | collective-permute-start | bytes 245768 | tf_op jit(solution)/shard_map/ppermute | solution.py:284
  14.0 0.5 %collective-permute-start.6 = (bf16[320,128]{1,0:T(8,128)(2,1)S(1)}, bf16[320,128]{1,0:T(8,128)(2,1)S(1)}, u32[]{:S(2)}, u32[]{:S(2)}) collective-permute-start(bf16[320,128]{1,0:T(8,128)(2,1)S(1)} %pad_maximum_fusion.refs_0_), channel_id=1, source_target_pairs={{0,16},{4,20},{8,24},{12,28},{16,0},{20,4},{24,8},{28,12},{1,17},{... | collective-permute-start | bytes 245768 | tf_op jit(solution)/shard_map/ppermute | solution.py:284
  14.5 0.3 %collective-permute-start.4 = (bf16[320,128]{1,0:T(8,128)(2,1)S(1)}, bf16[320,128]{1,0:T(8,128)(2,1)S(1)}, u32[]{:S(2)}, u32[]{:S(2)}) collective-permute-start(bf16[320,128]{1,0:T(8,128)(2,1)S(1)} %pad_maximum_fusion.refs_0_), channel_id=1, source_target_pairs={{0,8},{4,12},{8,0},{12,4},{16,24},{20,28},{24,16},{28,20},{1,9},{5... | collective-permute-start | bytes 245768 | tf_op jit(solution)/shard_map/ppermute | solution.py:284
  14.8 0.0 copy-start.2
  14.8 0.0 copy-start.5
  14.8 0.0 copy-start.6
  14.8 0.0 copy-start.10
  14.8 0.0 copy-start.11
  14.8 0.1 collective-permute-start.3
  14.9 1.9 %collective-permute-done.8.refs_6_ = bf16[320,128]{1,0:T(8,128)(2,1)S(1)} collective-permute-done((bf16[320,128]{1,0:T(8,128)(2,1)S(1)}, bf16[320,128]{1,0:T(8,128)(2,1)S(1)}, u32[]{:S(2)}, u32[]{:S(2)}) %collective-permute-start.8) | collective-permute-done | bytes 81952 | tf_op jit(solution)/shard_map/ppermute | solution.py:284
  16.8 0.0 collective-permute-start.9
  16.8 1.6 %collective-permute-done.6.refs_4_ = bf16[320,128]{1,0:T(8,128)(2,1)S(1)} collective-permute-done((bf16[320,128]{1,0:T(8,128)(2,1)S(1)}, bf16[320,128]{1,0:T(8,128)(2,1)S(1)}, u32[]{:S(2)}, u32[]{:S(2)}) %collective-permute-start.6) | collective-permute-done | bytes 81952 | tf_op jit(solution)/shard_map/ppermute | solution.py:284
  18.4 0.0 collective-permute-start.7
  18.4 0.5 %collective-permute-done.4.refs_2_ = bf16[320,128]{1,0:T(8,128)(2,1)S(1)} collective-permute-done((bf16[320,128]{1,0:T(8,128)(2,1)S(1)}, bf16[320,128]{1,0:T(8,128)(2,1)S(1)}, u32[]{:S(2)}, u32[]{:S(2)}) %collective-permute-start.4) | collective-permute-done | bytes 81952 | tf_op jit(solution)/shard_map/ppermute | solution.py:284
  18.9 0.0 collective-permute-start.5
  19.0 0.0 copy-done
  19.0 0.0 collective-permute-done.3.refs_1_
  19.0 0.0 collective-permute-done.9.refs_7_
  19.0 0.7 %collective-permute-done.7.refs_5_ = bf16[320,128]{1,0:T(8,128)(2,1)S(1)} collective-permute-done((bf16[320,128]{1,0:T(8,128)(2,1)S(1)}, bf16[320,128]{1,0:T(8,128)(2,1)S(1)}, u32[]{:S(2)}, u32[]{:S(2)}) %collective-permute-start.7) | collective-permute-done | bytes 81952 | tf_op jit(solution)/shard_map/ppermute | solution.py:286
  19.7 0.5 %collective-permute-done.5.refs_3_ = bf16[320,128]{1,0:T(8,128)(2,1)S(1)} collective-permute-done((bf16[320,128]{1,0:T(8,128)(2,1)S(1)}, bf16[320,128]{1,0:T(8,128)(2,1)S(1)}, u32[]{:S(2)}, u32[]{:S(2)}) %collective-permute-start.5) | collective-permute-done | bytes 81952 | tf_op jit(solution)/shard_map/ppermute | solution.py:286
  20.2 0.0 copy-done.2
  20.2 0.0 copy-done.5
  20.2 0.0 copy-done.6
  20.2 0.0 copy-done.10
  20.2 0.0 copy-done.11
  20.3 3.0 %shard_map.119 = f32[1,8,8192]{2,1,0:T(8,128)} custom-call(s32[2]{0:T(128)S(1)} %pad_add_fusion.where_ref, s32[32]{0:T(128)S(1)} %copy-done.8, s32[8]{0:T(128)S(1)} %copy-done.9, s32[32]{0:T(128)S(1)} %copy-done.10, s32[32]{0:T(128)S(1)} %copy-done.11, bf16[320,128]{1,0:T(8,128)(2,1)S(1)} %pad_maximum_fusion.refs_0_, ...), custom_call_target="tpu_custom_call" | custom-call | tf_op jit(solution)/shard_map/pallas_call | solution.py:289
  (3 shorter events, 0.0 us)
Async XLA Ops:
  0.0 19.0 %copy-start = (bf16[16,32,1024]{2,1,0:T(8,128)(2,1)S(1)}, bf16[16,32,1024]{2,1,0:T(8,128)(2,1)}, u32[]{:S(2)}) copy-start(bf16[16,32,1024]{2,1,0:T(8,128)(2,1)} %param.17) | copy-start | bytes 3145732
  0.0 6.5 %copy-start.7 = (bf16[64,128]{1,0:T(8,128)(2,1)S(1)}, bf16[64,128]{1,0:T(8,128)(2,1)}, u32[]{:S(2)}) copy-start(bf16[64,128]{1,0:T(8,128)(2,1)} %constant.25.clone.fwd_ref) | copy-start | bytes 49156
  0.8 10.4 %collective-permute-start.2 = (bf16[4,512]{1,0:T(4,128)(2,1)S(1)}, bf16[4,512]{1,0:T(4,128)(2,1)S(1)}, u32[]{:S(2)}, u32[]{:S(2)}) collective-permute-start(bf16[4,512]{1,0:T(4,128)(2,1)S(1)} %convert_element_type.3), channel_id=1, source_target_pairs={{0,3},{1,2},{2,1},{3,0},{4,7},{5,6},{6,5},{7,4},{8,11},{9,10},{10,... | collective-permute-start | bytes 12296 | tf_op jit(solution)/shard_map/ppermute | solution.py:265
  5.9 5.4 %collective-permute-start.1 = (bf16[4,512]{1,0:T(4,128)(2,1)S(1)}, bf16[4,512]{1,0:T(4,128)(2,1)S(1)}, u32[]{:S(2)}, u32[]{:S(2)}) collective-permute-start(bf16[4,512]{1,0:T(4,128)(2,1)S(1)} %convert_element_type.3), channel_id=1, source_target_pairs={{0,2},{1,3},{2,0},{3,1},{4,6},{5,7},{6,4},{7,5},{8,10},{9,11},{10,... | collective-permute-start | bytes 12296 | tf_op jit(solution)/shard_map/ppermute | solution.py:265
  5.9 5.4 %collective-permute-start = (bf16[4,512]{1,0:T(4,128)(2,1)S(1)}, bf16[4,512]{1,0:T(4,128)(2,1)S(1)}, u32[]{:S(2)}, u32[]{:S(2)}) collective-permute-start(bf16[4,512]{1,0:T(4,128)(2,1)S(1)} %convert_element_type.3), channel_id=1, source_target_pairs={{0,1},{1,0},{2,3},{3,2},{4,5},{5,4},{6,7},{7,6},{8,9},{9,8},{10,11... | collective-permute-start | bytes 12296 | tf_op jit(solution)/shard_map/ppermute | solution.py:265
  6.4 0.7 %copy-start.8 = (s32[32]{0:T(128)S(1)}, s32[32]{0:T(128)}, u32[]{:S(2)}) copy-start(s32[32]{0:T(128)} %sub_ref.3) | copy-start | bytes 388
  6.4 0.7 %copy-start.9 = (s32[8]{0:T(128)S(1)}, s32[8]{0:T(128)}, u32[]{:S(2)}) copy-start(s32[8]{0:T(128)} %off_ref.3) | copy-start | bytes 100
  7.1 0.9 %copy-start.1 = (f32[256,128]{1,0:T(8,128)S(1)}, f32[256,128]{1,0:T(8,128)}, u32[]{:S(2)}) copy-start(f32[256,128]{1,0:T(8,128)} %constant.27.clone.turn_ref.refs_10_) | copy-start | bytes 393220
  8.0 0.9 %copy-start.3 = (bf16[1,8,8192]{2,1,0:T(8,128)(2,1)S(1)}, bf16[1,8,8192]{2,1,0:T(8,128)(2,1)}, u32[]{:S(2)}) copy-start(bf16[1,8,8192]{2,1,0:T(8,128)(2,1)} %strips_ref.1) | copy-start | bytes 393220
  8.9 0.9 %copy-start.4 = (bf16[256,256]{1,0:T(8,128)(2,1)S(1)}, bf16[256,256]{1,0:T(8,128)(2,1)}, u32[]{:S(2)}) copy-start(bf16[256,256]{1,0:T(8,128)(2,1)} %constant.28.clone.pick_ref) | copy-start | bytes 393220
  11.3 5.6 %collective-permute-start.8 = (bf16[320,128]{1,0:T(8,128)(2,1)S(1)}, bf16[320,128]{1,0:T(8,128)(2,1)S(1)}, u32[]{:S(2)}, u32[]{:S(2)}) collective-permute-start(bf16[320,128]{1,0:T(8,128)(2,1)S(1)} %pad_maximum_fusion.refs_0_), channel_id=1, source_target_pairs={{0,24},{4,28},{8,16},{12,20},{16,8},{20,12},{24,0},{28,4},{1,25},{... | collective-permute-start | bytes 245768 | tf_op jit(solution)/shard_map/ppermute | solution.py:284
  14.0 4.4 %collective-permute-start.6 = (bf16[320,128]{1,0:T(8,128)(2,1)S(1)}, bf16[320,128]{1,0:T(8,128)(2,1)S(1)}, u32[]{:S(2)}, u32[]{:S(2)}) collective-permute-start(bf16[320,128]{1,0:T(8,128)(2,1)S(1)} %pad_maximum_fusion.refs_0_), channel_id=1, source_target_pairs={{0,16},{4,20},{8,24},{12,28},{16,0},{20,4},{24,8},{28,12},{1,17},{... | collective-permute-start | bytes 245768 | tf_op jit(solution)/shard_map/ppermute | solution.py:284
  14.5 4.4 %collective-permute-start.4 = (bf16[320,128]{1,0:T(8,128)(2,1)S(1)}, bf16[320,128]{1,0:T(8,128)(2,1)S(1)}, u32[]{:S(2)}, u32[]{:S(2)}) collective-permute-start(bf16[320,128]{1,0:T(8,128)(2,1)S(1)} %pad_maximum_fusion.refs_0_), channel_id=1, source_target_pairs={{0,8},{4,12},{8,0},{12,4},{16,24},{20,28},{24,16},{28,20},{1,9},{5... | collective-permute-start | bytes 245768 | tf_op jit(solution)/shard_map/ppermute | solution.py:284
  14.8 5.4 %copy-start.2 = (f32[256,128]{1,0:T(8,128)S(1)}, f32[256,128]{1,0:T(8,128)}, u32[]{:S(2)}) copy-start(f32[256,128]{1,0:T(8,128)} %constant.27.clone.turn_ref.refs_10_) | copy-start | bytes 393220
  14.8 5.4 %copy-start.5 = (bf16[128,256]{1,0:T(8,128)(2,1)S(1)}, bf16[128,256]{1,0:T(8,128)(2,1)}, u32[]{:S(2)}) copy-start(bf16[128,256]{1,0:T(8,128)(2,1)} %constant.29.clone.refs_11_) | copy-start | bytes 196612
  14.8 5.4 %copy-start.6 = (bf16[128,256]{1,0:T(8,128)(2,1)S(1)}, bf16[128,256]{1,0:T(8,128)(2,1)}, u32[]{:S(2)}) copy-start(bf16[128,256]{1,0:T(8,128)(2,1)} %constant.26.clone.refs_9_) | copy-start | bytes 196612
  14.8 5.4 %copy-start.10 = (s32[32]{0:T(128)S(1)}, s32[32]{0:T(128)}, u32[]{:S(2)}) copy-start(s32[32]{0:T(128)} %owner_ref.1) | copy-start | bytes 388
  14.8 5.4 %copy-start.11 = (s32[32]{0:T(128)S(1)}, s32[32]{0:T(128)}, u32[]{:S(2)}) copy-start(s32[32]{0:T(128)} %index_ref.1) | copy-start | bytes 388
  14.8 4.1 %collective-permute-start.3 = (bf16[320,128]{1,0:T(8,128)(2,1)S(1)}, bf16[320,128]{1,0:T(8,128)(2,1)S(1)}, u32[]{:S(2)}, u32[]{:S(2)}) collective-permute-start(bf16[320,128]{1,0:T(8,128)(2,1)S(1)} %pad_maximum_fusion.refs_0_), channel_id=1, source_target_pairs={{0,4},{4,0},{8,12},{12,8},{16,20},{20,16},{24,28},{28,24},{1,5},{5... | collective-permute-start | bytes 245768 | tf_op jit(solution)/shard_map/ppermute | solution.py:286
  16.8 2.2 %collective-permute-start.9 = (bf16[320,128]{1,0:T(8,128)(2,1)S(1)}, bf16[320,128]{1,0:T(8,128)(2,1)S(1)}, u32[]{:S(2)}, u32[]{:S(2)}) collective-permute-start(bf16[320,128]{1,0:T(8,128)(2,1)S(1)} %collective-permute-done.8.refs_6_), channel_id=1, source_target_pairs={{0,4},{4,0},{8,12},{12,8},{16,20},{20,16},{24,28},{28,24},{1,5},{5... | collective-permute-start | bytes 245768 | tf_op jit(solution)/shard_map/ppermute | solution.py:286
  18.4 1.3 %collective-permute-start.7 = (bf16[320,128]{1,0:T(8,128)(2,1)S(1)}, bf16[320,128]{1,0:T(8,128)(2,1)S(1)}, u32[]{:S(2)}, u32[]{:S(2)}) collective-permute-start(bf16[320,128]{1,0:T(8,128)(2,1)S(1)} %collective-permute-done.6.refs_4_), channel_id=1, source_target_pairs={{0,4},{4,0},{8,12},{12,8},{16,20},{20,16},{24,28},{28,24},{1,5},{5... | collective-permute-start | bytes 245768 | tf_op jit(solution)/shard_map/ppermute | solution.py:286
  18.9 1.3 %collective-permute-start.5 = (bf16[320,128]{1,0:T(8,128)(2,1)S(1)}, bf16[320,128]{1,0:T(8,128)(2,1)S(1)}, u32[]{:S(2)}, u32[]{:S(2)}) collective-permute-start(bf16[320,128]{1,0:T(8,128)(2,1)S(1)} %collective-permute-done.4.refs_2_), channel_id=1, source_target_pairs={{0,4},{4,0},{8,12},{12,8},{16,20},{20,16},{24,28},{28,24},{1,5},{5... | collective-permute-start | bytes 245768 | tf_op jit(solution)/shard_map/ppermute | solution.py:286

commit v2 on v1

v2 whole, which is shorter than its diff:
```python
import functools
import math

import jax
import jax.numpy as jnp
from jax import lax
from jax.experimental import pallas as pl
from jax.experimental.pallas import tpu as pltpu
from jax.sharding import PartitionSpec as P

M = 64
CAP = 4
LANES = 128

BF = jnp.bfloat16
F32 = jnp.float32


def dot(x, y):
    return jnp.dot(x, y, preferred_element_type=F32)


def dot_t(x, y):
    return lax.dot_general(x, y, (((1,), (1,)), ((), ())), preferred_element_type=F32)


def iota(shape, dim):
    return lax.broadcasted_iota(jnp.int32, shape, dim)


def sine(r):
    x = r * (2 * math.pi)
    y = x * x
    total = -1 / math.factorial(11)
    for n in (9, 7, 5, 3, 1):
        total = total * y + (-1) ** (n // 2) / math.factorial(n)
    return x * total


def circle(index, period):
    r = (index & (period - 1)).astype(F32) * (1 / period) - 0.5
    near = jnp.maximum(jnp.minimum(-r, 0.5 + r), r - 0.5)
    return sine(jnp.abs(r) - 0.25), sine(near)


def high_low(x, low):
    high = x.astype(BF).astype(F32)
    return jnp.where(low, x - high, high).astype(BF)


def column(values, width):
    groups = []
    row = iota((8, width), 0)
    for group in range(len(values) // 8):
        value = jnp.zeros((8, width), jnp.int32)
        for r in range(8):
            value = jnp.where(row == r, values[group * 8 + r], value)
        groups.append(value)
    return jnp.concatenate(groups, axis=0)


def start_of(mine, sub_ref, off_ref, j, length):
    return (sub_ref[j] + off_ref[mine]) & (length - 1)


def table_kernel(length, turn_ref, fwd_ref):
    cos, sin = circle(iota((LANES, LANES), 0) * iota((LANES, LANES), 1), length)
    turn_ref[:LANES, :] = cos
    turn_ref[LANES:, :] = sin

    chunks = length // LANES
    shape = (2 * chunks, 4 * chunks)
    row, lane = iota(shape, 0), iota(shape, 1)
    cos, sin = circle((row & (chunks - 1)) * (lane & (chunks - 1)), chunks)
    row_im, lane_im = row // chunks, lane // chunks % 2
    table = jnp.where(row_im == lane_im, cos, jnp.where(row_im == 0, sin, -sin))
    fwd_ref[...] = high_low(table, lane >= 2 * chunks)


def join_kernel(*refs):
    out_ref = refs[-1]
    row = 0
    for ref in refs[:-1]:
        out_ref[row : row + ref.shape[0], :] = ref[...]
        row += ref.shape[0]


def pack_kernel(windows_ref, *refs):
    out_ref = refs[-1]
    out_ref[: windows_ref.shape[0], :] = windows_ref[...]
    held = jnp.concatenate([ref[...] for ref in refs[:-1]], axis=0)
    row = windows_ref.shape[0]
    for c in range(0, held.shape[1], LANES):
        out_ref[row : row + held.shape[0], :] = held[:, c : c + LANES].astype(BF)
        row += held.shape[0]


def inner_kernel(strips_ref, turn_ref, fwd_ref, out_ref, in_scr):
    rows = strips_ref.shape[1]
    length = strips_ref.shape[2] // 2
    chunks = length // LANES
    for c in range(2 * chunks):
        piece = strips_ref[0, :, c * LANES : (c + 1) * LANES].astype(F32)
        in_scr[pl.ds(c, rows, stride=2 * chunks), :] = piece
    points = jnp.concatenate(
        [in_scr[r * 2 * chunks : (r + 1) * 2 * chunks, :].astype(BF) for r in range(rows)], axis=1
    )
    inner = dot(fwd_ref[...], jnp.concatenate([points, points], axis=0))
    for r in range(rows):
        re = inner[:chunks, r * LANES : (r + 1) * LANES]
        im = inner[chunks:, r * LANES : (r + 1) * LANES]
        for q in range(LANES // chunks):
            cos = turn_ref[q * chunks : (q + 1) * chunks, :]
            sin = turn_ref[LANES + q * chunks : LANES + (q + 1) * chunks, :]
            at = r * LANES + q * chunks
            out_ref[at : at + chunks, :LANES] = (re * cos + im * sin).astype(BF)
            out_ref[at : at + chunks, LANES:] = (im * cos - re * sin).astype(BF)


def window_kernel(length, sub_ref, off_ref, twisted_ref, out_ref, out_scr):
    mine = lax.axis_index("facet")
    rows = twisted_ref.shape[0] // LANES
    count = out_ref.shape[0] // rows
    starts = [start_of(mine, sub_ref, off_ref, j, length) for j in range(count)]
    block = column([s // M for s in starts], LANES)
    cos, sin = circle(block * iota((count, LANES), 1), length // M)
    scale = 1 / math.sqrt(length)
    cos, sin = cos * scale, sin * scale
    coarse = jnp.concatenate(
        [jnp.concatenate([cos, sin], axis=1), jnp.concatenate([-sin, cos], axis=1)], axis=0
    )
    coarse = jnp.concatenate([high_low(coarse, False), high_low(coarse, True)], axis=0)
    window = dot_t(coarse, twisted_ref[...])
    window = window[: 2 * count] + window[2 * count :]
    for r in range(rows):
        out_scr[pl.ds(r, 2 * count, stride=rows), :] = window[:, r * LANES : (r + 1) * LANES]
    lane = iota((rows, LANES), 1)

    def emit(j):
        shift = starts[j] & (M - 1)
        re = out_scr[j * rows : (j + 1) * rows, :]
        im = out_scr[(count + j) * rows : (count + j + 1) * rows, :]
        re = pltpu.roll(re, (LANES - shift) & (LANES - 1), 1)
        im = pltpu.roll(im, M - shift, 1)
        return jnp.where(lane < M, re, im)

    for j in range(0, count, 2):
        out_ref[j * rows : (j + 2) * rows, :] = jnp.concatenate([emit(j), emit(j + 1)], axis=0).astype(BF)


def prepare_kernel(
    facets,
    subs,
    length,
    sub_ref,
    off_ref,
    owner_ref,
    kind_ref,
    after_ref,
    screens_ref,
    place_ref,
    cos_ref,
    sin_ref,
    both_ref,
    rank_ref,
    coarse_ref,
    inv_ref,
    seen,
    cos_scr,
    sin_scr,
):
    count = sub_ref.shape[0]
    rows = cos_ref.shape[0] // count
    span = screens_ref.shape[2] // 2
    pieces = span // LANES
    chunks = length // LANES
    mine = lax.axis_index("facet")
    my_sub = lax.axis_index("sub")
    my_off = off_ref[mine]

    shape = (LANES, 2 * LANES)
    row = iota(shape, 0)
    lane = iota(shape, 1)
    lane_part = jnp.where((lane // M == 1) | (lane // M == 2), 1, 0)
    apart = (lane_part - row // M) * 8192 + (lane % M - row % M)
    for s in range(facets):
        delta = off_ref[mine ^ s] - my_off
        place_ref[s * LANES : (s + 1) * LANES, :] = jnp.where(apart == delta, 1.0, 0.0).astype(BF)

    shape = (span, LANES)
    row = iota(shape, 0)
    lane = iota(shape, 1)
    hit = row == my_off + lane % M
    both = jnp.where(hit, 1.0, 0.0).astype(BF)
    signed = jnp.where(hit, jnp.where(lane < M, -1.0, 1.0), 0.0).astype(BF)
    kinds = screens_ref.shape[0]
    tall = cos_scr.shape[0] // kinds
    first = my_sub * rows // tall * tall
    block = pl.ds(pl.multiple_of(first, tall), tall)
    cosines = screens_ref[:, block, :span].reshape(kinds * tall, span)
    sines = screens_ref[:, block, span:].reshape(kinds * tall, span)
    cos_scr[...] = dot(cosines, both)
    sin_scr[...] = dot(sines, signed)
    for j in range(count):
        kind = pl.multiple_of(kind_ref[j] * tall + my_sub * rows - first, rows)
        cos_ref[j * rows : (j + 1) * rows, :] = cos_scr[pl.ds(kind, rows), :]
        sin_ref[j * rows : (j + 1) * rows, :] = sin_scr[pl.ds(kind, rows), :]
    both_ref[...] = both

    for o in range(facets * subs):
        seen[o] = 0
    held = subs * CAP
    places = []
    for j in range(count):
        who = owner_ref[j]
        slot = seen[who]
        seen[who] = slot + 1
        facet_step = (who // subs) ^ mine
        sub_step = (who % subs) ^ my_sub
        places.append(facet_step * held * pieces + sub_step * CAP + slot)
    width = rank_ref.shape[1]
    place = column(places, width)
    lane = iota((count, width), 1)
    for c in range(pieces):
        hit = jnp.where(lane == place + c * held, 1.0, 0.0)
        rank_ref[c * count : (c + 1) * count, :] = hit.astype(BF)

    lane = iota((8, 4 * count), 1)
    block = jnp.zeros((8, 4 * count), jnp.int32)
    for j in range(count):
        start = start_of(mine, sub_ref, off_ref, j, length) // M
        block = jnp.where(lane % count == j, start, block)
    block = jnp.concatenate([block] * (M // 8), axis=0)
    shape = (M, 4 * count)
    lane = iota(shape, 1)
    cos, sin = circle(block * iota(shape, 0), length // M)
    scale = 1 / math.sqrt(length)
    cos, sin = cos * scale, sin * scale
    lane_im = lane // count % 2 == 1
    low = lane >= 2 * count
    coarse_ref[:M, :] = high_low(jnp.where(lane_im, -sin, cos), low)
    coarse_ref[M:, :] = high_low(jnp.where(lane_im, cos, sin), low)

    shape = (chunks, LANES)
    cos, sin = circle(iota(shape, 0) * iota(shape, 1), chunks)
    table = jnp.concatenate(
        [jnp.concatenate([cos, -sin], axis=1), jnp.concatenate([sin, cos], axis=1)], axis=0
    )
    inv_ref[: 2 * chunks, :] = high_low(table, False)
    inv_ref[2 * chunks :, :] = high_low(table, True)


def backward_kernel(facets, sub_ref, off_ref, *refs):
    arrived = refs[:facets]
    place_ref, cos_ref, sin_ref, both_ref, rank_ref, coarse_ref = refs[facets : facets + 6]
    inv_ref, turn_ref, out_ref, re_scr, im_scr, out_scr = refs[facets + 6 :]
    mine = lax.axis_index("facet")
    rows = out_ref.shape[1]
    length = out_ref.shape[2] // 2
    chunks = length // LANES
    count = sub_ref.shape[0]
    windows = count * rows

    total = dot(arrived[0][:windows, :], place_ref[:LANES, :])
    for s in range(1, facets):
        total = total + dot(arrived[s][:windows, :], place_ref[s * LANES : (s + 1) * LANES, :])

    held = jnp.concatenate([block[windows:, :] for block in arrived], axis=0)
    ranked = dot(rank_ref[...], held).astype(BF)
    ranked = jnp.concatenate([ranked[c : c + count] for c in range(0, ranked.shape[0], count)], axis=1)
    weights = dot(ranked, both_ref[...])

    lane = iota((rows, LANES), 1)
    for j in range(count):
        weight = weights[j : j + 1, :]
        cos = cos_ref[j * rows : (j + 1) * rows, :] * weight
        sin = sin_ref[j * rows : (j + 1) * rows, :] * weight
        here = total[j * rows : (j + 1) * rows, :LANES]
        swapped = total[j * rows : (j + 1) * rows, LANES:]
        value = (here * cos + swapped * sin).astype(BF).astype(F32)
        shift = start_of(mine, sub_ref, off_ref, j, length) & (M - 1)
        mask = (lane >= shift) & (lane < shift + M)
        re_scr[pl.ds(j, rows, stride=count), :] = jnp.where(mask, pltpu.roll(value, shift, 1), 0.0)
        im_scr[pl.ds(j, rows, stride=count), :] = jnp.where(mask, pltpu.roll(value, shift + M, 1), 0.0)

    halves = []
    for scr in (re_scr, im_scr):
        halves.append(
            jnp.concatenate([scr[r * count : (r + 1) * count, :].astype(BF) for r in range(rows)], axis=1)
        )
    spread = jnp.concatenate(halves + halves, axis=0)
    inner = dot(coarse_ref[...], spread)
    twisted = []
    for r in range(rows):
        re = inner[:M, r * LANES : (r + 1) * LANES]
        im = inner[M:, r * LANES : (r + 1) * LANES]
        for q in range(LANES // M):
            cos = turn_ref[q * M : (q + 1) * M, :]
            sin = turn_ref[LANES + q * M : LANES + (q + 1) * M, :]
            both = jnp.concatenate([re * cos - im * sin, re * sin + im * cos], axis=1)
            twisted.append(both.astype(BF))
    twisted = jnp.concatenate(twisted, axis=0)
    points = dot_t(inv_ref[...], twisted)
    points = points[: 2 * chunks] + points[2 * chunks :]
    for r in range(rows):
        out_scr[pl.ds(r, 2 * chunks, stride=rows), :] = points[:, r * LANES : (r + 1) * LANES]
    for c in range(2 * chunks):
        out_ref[0, :, c * LANES : (c + 1) * LANES] = out_scr[c * rows : (c + 1) * rows, :]


def local(strips, facet_offset, subgrid_offset, owner, screen_index, screens, grid_weight):
    facets = lax.axis_size("facet")
    subs = lax.axis_size("sub")
    rows = strips.shape[1]
    length = strips.shape[2] // 2
    chunks = length // LANES
    count = subgrid_offset.shape[0]
    span = grid_weight.shape[1]
    kinds = screens.shape[0]
    smem = pl.BlockSpec(memory_space=pltpu.SMEM)
    vmem = pl.BlockSpec(memory_space=pltpu.VMEM)
    limit = pltpu.CompilerParams(vmem_limit_bytes=32 * 1024 * 1024)
    shaped = jax.ShapeDtypeStruct

    def swap(x, step):
        return lax.ppermute(x, "facet", [(i, i ^ step) for i in range(facets)])

    def cost(flops):
        return pl.CostEstimate(flops=flops, bytes_accessed=1 << 20, transcendentals=0)

    turn, fwd = pl.pallas_call(
        functools.partial(table_kernel, length),
        out_shape=[shaped((2 * LANES, LANES), F32), shaped((2 * chunks, 4 * chunks), BF)],
        out_specs=[vmem] * 2,
        compiler_params=limit,
        cost_estimate=cost(10**11),
    )()
    held = grid_weight
    step = 1
    others = []
    while step < subs:
        beside = lax.ppermute(held, "sub", [(k, k ^ step) for k in range(subs)])
        if step == 1:
            twisted = pl.pallas_call(
                inner_kernel,
                out_shape=shaped((rows * LANES, 2 * LANES), BF),
                in_specs=[vmem] * 3,
                out_specs=vmem,
                scratch_shapes=[pltpu.VMEM((rows * 2 * chunks, LANES), F32)],
                compiler_params=limit,
            )(strips, turn, fwd)
            windows = pl.pallas_call(
                functools.partial(window_kernel, length),
                out_shape=shaped((count * rows, LANES), BF),
                in_specs=[smem] * 2 + [vmem],
                out_specs=vmem,
                scratch_shapes=[pltpu.VMEM((2 * count * rows, LANES), F32)],
                compiler_params=limit,
            )(subgrid_offset, facet_offset, twisted)
        step *= 2
        if step < subs:
            held = pl.pallas_call(
                join_kernel,
                out_shape=shaped((2 * held.shape[0], span), F32),
                in_specs=[vmem] * 2,
                out_specs=vmem,
                compiler_params=limit,
            )(held, beside)
            held, _ = lax.optimization_barrier((held, windows))
    held = [held, beside]

    tall = max(rows, 16)
    prepared = pl.pallas_call(
        functools.partial(prepare_kernel, facets, subs, length),
        out_shape=[
            shaped((facets * LANES, 2 * LANES), BF),
            shaped((count * rows, LANES), F32),
            shaped((count * rows, LANES), F32),
            shaped((span, LANES), BF),
            shaped((span // LANES * count, facets * subs * grid_weight.size // LANES), BF),
            shaped((2 * M, 4 * count), BF),
            shaped((4 * chunks, 2 * LANES), BF),
        ],
        in_specs=[smem] * 4 + [pl.BlockSpec(memory_space=pl.ANY), vmem],
        out_specs=[vmem] * 7,
        scratch_shapes=[
            pltpu.SMEM((facets * subs,), jnp.int32),
            pltpu.VMEM((kinds * tall, LANES), F32),
            pltpu.VMEM((kinds * tall, LANES), F32),
        ],
        compiler_params=limit,
        cost_estimate=cost(2*10**10),
    )(subgrid_offset, facet_offset, owner, screen_index, held[0], screens)

    windows, _ = lax.optimization_barrier((windows, prepared[3]))
    payload = pl.pallas_call(
        pack_kernel,
        out_shape=shaped((count * rows + subs * grid_weight.size // LANES, LANES), BF),
        in_specs=[vmem] * (1 + len(held)),
        out_specs=vmem,
        compiler_params=limit,
    )(windows, *held)

    arrived = [payload] + [None] * (facets - 1)
    for s in reversed(range(2, facets, 2)):
        arrived[s] = swap(payload, s)

    for s in range(0, facets, 2):
        arrived[s + 1] = swap(arrived[s], 1)

    return pl.pallas_call(
        functools.partial(backward_kernel, facets),
        out_shape=shaped((1, rows, 2 * length), F32),
        in_specs=[smem] * 2 + [vmem] * (facets + 8),
        out_specs=vmem,
        scratch_shapes=[
            pltpu.VMEM((rows * count, LANES), F32),
            pltpu.VMEM((rows * count, LANES), F32),
            pltpu.VMEM((2 * chunks * rows, LANES), F32),
        ],
        compiler_params=limit,
    )(subgrid_offset, facet_offset, *arrived, *prepared, turn)


def solution(mesh):
    in_specs = (P("facet", "sub", None), P(), P(), P(), P(), P(), P(("facet", "sub"), None))
    out_specs = P("facet", "sub", None)
    return jax.shard_map(local, mesh=mesh, in_specs=in_specs, out_specs=out_specs, check_vma=False)
```

time: 23.5 us -> 21.6 us (0.919)
  local copies, waits for them, and re-layouts: 3.35 us -> 0.3 us
  Pallas kernels: 4.38 us -> 5.74 us
  other arithmetic: 0.9 us -> 0 us
  waiting for transfers between devices: 5.25 us -> 5.8 us
    unnamed x24 -> x14, local copies, waits for them, and re-layouts: 3.33 us -> 0.3 us
    pallas_call x2 -> x7, Pallas kernels: 4.38 us -> 5.74 us  [the longest x1 2.71 us: local(): pl.pallas_call(functools.partial(backward_kernel, facets), out_shape=shap...]
    convert_element_type x1 -> x0, other arithmetic: 0.8 us -> none  [local(): rows_here = grid_weight.astype(BF)]
    ppermute x10 -> x9, waiting for transfers between devices: 5.25 us -> 5.8 us  [the longest x7 5.39 us: swap(): return lax.ppermute(x, 'facet', [(i, i ^ step) for i in range(facets)])]
    ppermute x10 -> x9, starting transfers between devices: 9.25 us -> 9.47 us  [the longest x2 5.91 us: local(): beside = lax.ppermute(held, 'sub', [(k, k ^ step) for k in range(subs)])]
  transfers between devices with their start and end apart: 10 -> 9, of which waited for: 5 -> 6; matrix products, arithmetic and copies ran while one was open for 0% -> 0% of each run, Pallas kernels for 6% -> 14%
where the time goes in v2:
time: 21.6 us; the launch traced here: 21.4 us
  starting transfers between devices  9.47 us (44%)
  waiting for transfers between devices  5.8 us (27%)
  Pallas kernels  5.74 us (27%)
  local copies, waits for them, and re-layouts  0.3 us (1%)
    ppermute x2, starting transfers between devices, local(): beside = lax.ppermute(held, 'sub', [(k, k ^ step) for k in range(subs)])  5.91 us
    ppermute x7, waiting for transfers between devices, swap(): return lax.ppermute(x, 'facet', [(i, i ^ step) for i in range(facets)])  5.39 us
    ppermute x7, starting transfers between devices, swap(): return lax.ppermute(x, 'facet', [(i, i ^ step) for i in range(facets)])  3.57 us
    pallas_call x1, Pallas kernels, local(): pl.pallas_call(functools.partial(backward_kernel, facets), out_shape=shap...  2.71 us
    pallas_call x1, Pallas kernels, local(): pl.pallas_call(functools.partial(prepare_kernel, facets, subs, length), o...  1.39 us
    pallas_call x1, Pallas kernels, local(): pl.pallas_call(functools.partial(window_kernel, length), out_shape=shaped...  1.01 us
    pallas_call x1, Pallas kernels, local(): pl.pallas_call(inner_kernel, out_shape=shaped((rows * LANES, 2 * LANES),...  0.46 us
  transfers between devices with their start and end apart: 9, of which 6 were waited for; matrix products, arithmetic and copies ran while one was open for 0% of the time, Pallas kernels for 14%

profile of v2, /device:TPU:0, one launch (start us, length us, event | category | flops | bytes accessed | tf_op | source)
XLA Modules:
  0.0 21.4 jit_solution(6989702535688613558)
XLA Ops:
  0.0 0.0 copy-start
  0.0 3.0 %collective-permute-start = (f32[4,512]{1,0:T(4,128)}, f32[4,512]{1,0:T(4,128)S(1)}, u32[]{:S(2)}, u32[]{:S(2)}) collective-permute-start(f32[4,512]{1,0:T(4,128)} %refs_0_.1), channel_id=1, source_target_pairs={{0,1},{1,0},{2,3},{3,2},{4,5},{5,4},{6,7},{7,6},{8,9},{9,8},{10,11... | collective-permute-start | bytes 24584 | tf_op jit(solution)/shard_map/ppermute | solution.py:342
  3.0 0.0 copy-start.4
  3.0 0.1 shard_map.73
  3.2 0.0 copy-done
  3.2 0.0 copy-start.2
  3.2 0.0 copy-start.3
  3.2 0.5 %shard_map.74.twisted_ref = bf16[1024,256]{1,0:T(8,128)(2,1)S(1)} custom-call(bf16[1,8,8192]{2,1,0:T(8,128)(2,1)S(1)} %copy-done, f32[256,128]{1,0:T(8,128)S(1)} %get-tuple-element.16.turn_ref.refs_15_, bf16[64,128]{1,0:T(8,128)(2,1)S(1)} %get-tuple-element.17.fwd_ref), custom_call_target="tpu_custom_call" | custom-call | tf_op jit(solution)/shard_map/pallas_call | solution.py:344
  3.7 0.2 %copy-done.2 = s32[32]{0:T(128)S(1)} copy-done((s32[32]{0:T(128)S(1)}, s32[32]{0:T(128)}, u32[]{:S(2)}) %copy-start.2) | copy-done | bytes 152
  3.9 0.0 copy-done.3
  3.9 0.0 copy-start.1
  3.9 1.0 %shard_map.75.windows_ref = bf16[256,128]{1,0:T(8,128)(2,1)S(1)} custom-call(s32[32]{0:T(128)S(1)} %copy-done.2, s32[8]{0:T(128)S(1)} %copy-done.3, bf16[1024,256]{1,0:T(8,128)(2,1)S(1)} %shard_map.74.twisted_ref), custom_call_target="tpu_custom_call" | custom-call | tf_op jit(solution)/shard_map/pallas_call | solution.py:352
  5.0 0.0 copy-start.5
  5.0 0.0 copy-start.6
  5.0 0.0 collective-permute-done.refs_1_
  5.0 0.0 copy-done.1
  5.0 2.9 %collective-permute-start.1 = (f32[8,512]{1,0:T(8,128)S(1)}, f32[8,512]{1,0:T(8,128)S(1)}, u32[]{:S(2)}, u32[]{:S(2)}) collective-permute-start(f32[8,512]{1,0:T(8,128)S(1)} %shard_map.76.after_ref.refs_0_), channel_id=1, source_target_pairs={{0,2},{1,3},{2,0},{3,1},{4,6},{5,7},{6,4},{7,5},{8,10},{9,11},{10,... | collective-permute-start | bytes 49160 | tf_op jit(solution)/shard_map/ppermute | solution.py:342
  7.9 0.0 copy-done.4
  7.9 0.0 copy-done.5
  7.9 0.0 copy-done.6
  7.9 1.4 %shard_map.77 = (bf16[1024,256]{1,0:T(8,128)(2,1)S(1)}, f32[256,128]{1,0:T(8,128)S(1)}, f32[256,128]{1,0:T(8,128)S(1)}, bf16[512,128]{1,0:T(8,128)(2,1)S(1)}, bf...) custom-call(s32[32]{0:T(128)S(1)} %copy-done.2, s32[8]{0:T(128)S(1)} %copy-done.3, ...), custom_call_target="tpu_custom_call" | custom-call | flops 20000000000 | bytes 1048576 | tf_op jit(solution)/shard_map/pallas_call | solution.py:373
  9.3 0.4 %collective-permute-done.1.refs_1_ = f32[8,512]{1,0:T(8,128)S(1)} collective-permute-done((f32[8,512]{1,0:T(8,128)S(1)}, f32[8,512]{1,0:T(8,128)S(1)}, u32[]{:S(2)}, u32[]{:S(2)}) %collective-permute-start.1) | collective-permute-done | bytes 16416 | tf_op jit(solution)/shard_map/ppermute | solution.py:342
  9.7 2.7 %collective-permute-start.7 = (bf16[320,128]{1,0:T(8,128)(2,1)S(1)}, bf16[320,128]{1,0:T(8,128)(2,1)S(1)}, u32[]{:S(2)}, u32[]{:S(2)}) collective-permute-start(bf16[320,128]{1,0:T(8,128)(2,1)S(1)} %shard_map.78.refs_0_), channel_id=1, source_target_pairs={{0,24},{4,28},{8,16},{12,20},{16,8},{20,12},{24,0},{28,4},{1,25},{... | collective-permute-start | bytes 245768 | tf_op jit(solution)/shard_map/ppermute | solution.py:326
  12.5 0.5 %collective-permute-start.5 = (bf16[320,128]{1,0:T(8,128)(2,1)S(1)}, bf16[320,128]{1,0:T(8,128)(2,1)S(1)}, u32[]{:S(2)}, u32[]{:S(2)}) collective-permute-start(bf16[320,128]{1,0:T(8,128)(2,1)S(1)} %shard_map.78.refs_0_), channel_id=1, source_target_pairs={{0,16},{4,20},{8,24},{12,28},{16,0},{20,4},{24,8},{28,12},{1,17},{... | collective-permute-start | bytes 245768 | tf_op jit(solution)/shard_map/ppermute | solution.py:326
  13.0 0.3 %collective-permute-start.3 = (bf16[320,128]{1,0:T(8,128)(2,1)S(1)}, bf16[320,128]{1,0:T(8,128)(2,1)S(1)}, u32[]{:S(2)}, u32[]{:S(2)}) collective-permute-start(bf16[320,128]{1,0:T(8,128)(2,1)S(1)} %shard_map.78.refs_0_), channel_id=1, source_target_pairs={{0,8},{4,12},{8,0},{12,4},{16,24},{20,28},{24,16},{28,20},{1,9},{5... | collective-permute-start | bytes 245768 | tf_op jit(solution)/shard_map/ppermute | solution.py:326
  13.3 0.0 collective-permute-start.2
  13.3 2.6 %collective-permute-done.7.refs_6_ = bf16[320,128]{1,0:T(8,128)(2,1)S(1)} collective-permute-done((bf16[320,128]{1,0:T(8,128)(2,1)S(1)}, bf16[320,128]{1,0:T(8,128)(2,1)S(1)}, u32[]{:S(2)}, u32[]{:S(2)}) %collective-permute-start.7) | collective-permute-done | bytes 81952 | tf_op jit(solution)/shard_map/ppermute | solution.py:326
  15.9 0.0 collective-permute-start.8
  15.9 1.0 %collective-permute-done.5.refs_4_ = bf16[320,128]{1,0:T(8,128)(2,1)S(1)} collective-permute-done((bf16[320,128]{1,0:T(8,128)(2,1)S(1)}, bf16[320,128]{1,0:T(8,128)(2,1)S(1)}, u32[]{:S(2)}, u32[]{:S(2)}) %collective-permute-start.5) | collective-permute-done | bytes 81952 | tf_op jit(solution)/shard_map/ppermute | solution.py:326
  16.9 0.0 collective-permute-start.6
  16.9 0.5 %collective-permute-done.3.refs_2_ = bf16[320,128]{1,0:T(8,128)(2,1)S(1)} collective-permute-done((bf16[320,128]{1,0:T(8,128)(2,1)S(1)}, bf16[320,128]{1,0:T(8,128)(2,1)S(1)}, u32[]{:S(2)}, u32[]{:S(2)}) %collective-permute-start.3) | collective-permute-done | bytes 81952 | tf_op jit(solution)/shard_map/ppermute | solution.py:326
  17.4 0.0 collective-permute-start.4
  17.4 0.0 collective-permute-done.2.refs_1_
  17.4 0.0 collective-permute-done.8.refs_7_
  17.4 0.8 %collective-permute-done.6.refs_5_ = bf16[320,128]{1,0:T(8,128)(2,1)S(1)} collective-permute-done((bf16[320,128]{1,0:T(8,128)(2,1)S(1)}, bf16[320,128]{1,0:T(8,128)(2,1)S(1)}, u32[]{:S(2)}, u32[]{:S(2)}) %collective-permute-start.6) | collective-permute-done | bytes 81952 | tf_op jit(solution)/shard_map/ppermute | solution.py:326
  18.2 0.5 %collective-permute-done.4.refs_3_ = bf16[320,128]{1,0:T(8,128)(2,1)S(1)} collective-permute-done((bf16[320,128]{1,0:T(8,128)(2,1)S(1)}, bf16[320,128]{1,0:T(8,128)(2,1)S(1)}, u32[]{:S(2)}, u32[]{:S(2)}) %collective-permute-start.4) | collective-permute-done | bytes 81952 | tf_op jit(solution)/shard_map/ppermute | solution.py:326
  18.7 2.7 %shard_map.79 = f32[1,8,8192]{2,1,0:T(8,128)} custom-call(s32[32]{0:T(128)S(1)} %copy-done.2, s32[8]{0:T(128)S(1)} %copy-done.3, bf16[320,128]{1,0:T(8,128)(2,1)S(1)} %shard_map.78.refs_0_, bf16[320,128]{1,0:T(8,128)(2,1)S(1)} %collective-permute-done.2.refs_1_, bf16[320,128]{1,0:T(8,128)(2,1)S(1)} %collective-permute-done.3.refs_2_, ...), custom_call_target="tpu_custom_call" | custom-call | tf_op jit(solution)/shard_map/pallas_call | solution.py:411
  (2 shorter events, 0.0 us)
Async XLA Ops:
  0.0 3.2 %copy-start = (bf16[1,8,8192]{2,1,0:T(8,128)(2,1)S(1)}, bf16[1,8,8192]{2,1,0:T(8,128)(2,1)}, u32[]{:S(2)}) copy-start(bf16[1,8,8192]{2,1,0:T(8,128)(2,1)} %strips_ref.1) | copy-start | bytes 393220
  0.0 5.0 %collective-permute-start = (f32[4,512]{1,0:T(4,128)}, f32[4,512]{1,0:T(4,128)S(1)}, u32[]{:S(2)}, u32[]{:S(2)}) collective-permute-start(f32[4,512]{1,0:T(4,128)} %refs_0_.1), channel_id=1, source_target_pairs={{0,1},{1,0},{2,3},{3,2},{4,5},{5,4},{6,7},{7,6},{8,9},{9,8},{10,11... | collective-permute-start | bytes 24584 | tf_op jit(solution)/shard_map/ppermute | solution.py:342
  3.0 4.9 %copy-start.4 = (bf16[16,32,1024]{2,1,0:T(8,128)(2,1)S(1)}, bf16[16,32,1024]{2,1,0:T(8,128)(2,1)}, u32[]{:S(2)}) copy-start(bf16[16,32,1024]{2,1,0:T(8,128)(2,1)} %screens_ref.1) | copy-start | bytes 3145732
  3.2 0.7 %copy-start.2 = (s32[32]{0:T(128)S(1)}, s32[32]{0:T(128)}, u32[]{:S(2)}) copy-start(s32[32]{0:T(128)} %sub_ref.5) | copy-start | bytes 388
  3.2 0.7 %copy-start.3 = (s32[8]{0:T(128)S(1)}, s32[8]{0:T(128)}, u32[]{:S(2)}) copy-start(s32[8]{0:T(128)} %off_ref.5) | copy-start | bytes 100
  3.9 1.1 %copy-start.1 = (f32[4,512]{1,0:T(4,128)S(1)}, f32[4,512]{1,0:T(4,128)}, u32[]{:S(2)}) copy-start(f32[4,512]{1,0:T(4,128)} %refs_0_.1) | copy-start | bytes 24580
  5.0 2.9 %copy-start.5 = (s32[32]{0:T(128)S(1)}, s32[32]{0:T(128)}, u32[]{:S(2)}) copy-start(s32[32]{0:T(128)} %owner_ref.1) | copy-start | bytes 388
  5.0 2.9 %copy-start.6 = (s32[32]{0:T(128)S(1)}, s32[32]{0:T(128)}, u32[]{:S(2)}) copy-start(s32[32]{0:T(128)} %kind_ref.1) | copy-start | bytes 388
  5.0 4.7 %collective-permute-start.1 = (f32[8,512]{1,0:T(8,128)S(1)}, f32[8,512]{1,0:T(8,128)S(1)}, u32[]{:S(2)}, u32[]{:S(2)}) collective-permute-start(f32[8,512]{1,0:T(8,128)S(1)} %shard_map.76.after_ref.refs_0_), channel_id=1, source_target_pairs={{0,2},{1,3},{2,0},{3,1},{4,6},{5,7},{6,4},{7,5},{8,10},{9,11},{10,... | collective-permute-start | bytes 49160 | tf_op jit(solution)/shard_map/ppermute | solution.py:342
  9.7 6.1 %collective-permute-start.7 = (bf16[320,128]{1,0:T(8,128)(2,1)S(1)}, bf16[320,128]{1,0:T(8,128)(2,1)S(1)}, u32[]{:S(2)}, u32[]{:S(2)}) collective-permute-start(bf16[320,128]{1,0:T(8,128)(2,1)S(1)} %shard_map.78.refs_0_), channel_id=1, source_target_pairs={{0,24},{4,28},{8,16},{12,20},{16,8},{20,12},{24,0},{28,4},{1,25},{... | collective-permute-start | bytes 245768 | tf_op jit(solution)/shard_map/ppermute | solution.py:326
  12.5 4.4 %collective-permute-start.5 = (bf16[320,128]{1,0:T(8,128)(2,1)S(1)}, bf16[320,128]{1,0:T(8,128)(2,1)S(1)}, u32[]{:S(2)}, u32[]{:S(2)}) collective-permute-start(bf16[320,128]{1,0:T(8,128)(2,1)S(1)} %shard_map.78.refs_0_), channel_id=1, source_target_pairs={{0,16},{4,20},{8,24},{12,28},{16,0},{20,4},{24,8},{28,12},{1,17},{... | collective-permute-start | bytes 245768 | tf_op jit(solution)/shard_map/ppermute | solution.py:326
  13.0 4.4 %collective-permute-start.3 = (bf16[320,128]{1,0:T(8,128)(2,1)S(1)}, bf16[320,128]{1,0:T(8,128)(2,1)S(1)}, u32[]{:S(2)}, u32[]{:S(2)}) collective-permute-start(bf16[320,128]{1,0:T(8,128)(2,1)S(1)} %shard_map.78.refs_0_), channel_id=1, source_target_pairs={{0,8},{4,12},{8,0},{12,4},{16,24},{20,28},{24,16},{28,20},{1,9},{5... | collective-permute-start | bytes 245768 | tf_op jit(solution)/shard_map/ppermute | solution.py:326
  13.3 4.1 %collective-permute-start.2 = (bf16[320,128]{1,0:T(8,128)(2,1)S(1)}, bf16[320,128]{1,0:T(8,128)(2,1)S(1)}, u32[]{:S(2)}, u32[]{:S(2)}) collective-permute-start(bf16[320,128]{1,0:T(8,128)(2,1)S(1)} %shard_map.78.refs_0_), channel_id=1, source_target_pairs={{0,4},{4,0},{8,12},{12,8},{16,20},{20,16},{24,28},{28,24},{1,5},{5... | collective-permute-start | bytes 245768 | tf_op jit(solution)/shard_map/ppermute | solution.py:326
  15.9 1.6 %collective-permute-start.8 = (bf16[320,128]{1,0:T(8,128)(2,1)S(1)}, bf16[320,128]{1,0:T(8,128)(2,1)S(1)}, u32[]{:S(2)}, u32[]{:S(2)}) collective-permute-start(bf16[320,128]{1,0:T(8,128)(2,1)S(1)} %collective-permute-done.7.refs_6_), channel_id=1, source_target_pairs={{0,4},{4,0},{8,12},{12,8},{16,20},{20,16},{24,28},{28,24},{1,5},{5... | collective-permute-start | bytes 245768 | tf_op jit(solution)/shard_map/ppermute | solution.py:326
  16.9 1.3 %collective-permute-start.6 = (bf16[320,128]{1,0:T(8,128)(2,1)S(1)}, bf16[320,128]{1,0:T(8,128)(2,1)S(1)}, u32[]{:S(2)}, u32[]{:S(2)}) collective-permute-start(bf16[320,128]{1,0:T(8,128)(2,1)S(1)} %collective-permute-done.5.refs_4_), channel_id=1, source_target_pairs={{0,4},{4,0},{8,12},{12,8},{16,20},{20,16},{24,28},{28,24},{1,5},{5... | collective-permute-start | bytes 245768 | tf_op jit(solution)/shard_map/ppermute | solution.py:326
  17.4 1.3 %collective-permute-start.4 = (bf16[320,128]{1,0:T(8,128)(2,1)S(1)}, bf16[320,128]{1,0:T(8,128)(2,1)S(1)}, u32[]{:S(2)}, u32[]{:S(2)}) collective-permute-start(bf16[320,128]{1,0:T(8,128)(2,1)S(1)} %collective-permute-done.3.refs_2_), channel_id=1, source_target_pairs={{0,4},{4,0},{8,12},{12,8},{16,20},{20,16},{24,28},{28,24},{1,5},{5... | collective-permute-start | bytes 245768 | tf_op jit(solution)/shard_map/ppermute | solution.py:326

commit v3 on v2

--- a/solution.py
+++ b/solution.py
@@ -95,10 +95,23 @@
         row += held.shape[0]
 
 
-def inner_kernel(strips_ref, turn_ref, fwd_ref, out_ref, in_scr):
+def scalars(pairs, sems):
+    copies = [pltpu.make_async_copy(a, b, sems.at[n]) for n, (a, b) in enumerate(pairs)]
+    for copy in copies:
+        copy.start()
+    return copies
+
+
+def forward_kernel(
+    sub_hbm, off_hbm, strips_ref, turn_ref, fwd_ref, out_ref, in_scr, mid_scr, out_scr, sub_ref, off_ref, sems
+):
+    copies = scalars([(sub_hbm, sub_ref), (off_hbm, off_ref)], sems)
+    mine = lax.axis_index("facet")
     rows = strips_ref.shape[1]
     length = strips_ref.shape[2] // 2
     chunks = length // LANES
+    count = sub_ref.shape[0]
+
     for c in range(2 * chunks):
         piece = strips_ref[0, :, c * LANES : (c + 1) * LANES].astype(F32)
         in_scr[pl.ds(c, rows, stride=2 * chunks), :] = piece
@@ -113,14 +126,11 @@
             cos = turn_ref[q * chunks : (q + 1) * chunks, :]
             sin = turn_ref[LANES + q * chunks : LANES + (q + 1) * chunks, :]
             at = r * LANES + q * chunks
-            out_ref[at : at + chunks, :LANES] = (re * cos + im * sin).astype(BF)
-            out_ref[at : at + chunks, LANES:] = (im * cos - re * sin).astype(BF)
-
-
-def window_kernel(length, sub_ref, off_ref, twisted_ref, out_ref, out_scr):
-    mine = lax.axis_index("facet")
-    rows = twisted_ref.shape[0] // LANES
-    count = out_ref.shape[0] // rows
+            mid_scr[at : at + chunks, :LANES] = (re * cos + im * sin).astype(BF)
+            mid_scr[at : at + chunks, LANES:] = (im * cos - re * sin).astype(BF)
+
+    for copy in copies:
+        copy.wait()
     starts = [start_of(mine, sub_ref, off_ref, j, length) for j in range(count)]
     block = column([s // M for s in starts], LANES)
     cos, sin = circle(block * iota((count, LANES), 1), length // M)
@@ -130,7 +140,7 @@
         [jnp.concatenate([cos, sin], axis=1), jnp.concatenate([-sin, cos], axis=1)], axis=0
     )
     coarse = jnp.concatenate([high_low(coarse, False), high_low(coarse, True)], axis=0)
-    window = dot_t(coarse, twisted_ref[...])
+    window = dot_t(coarse, mid_scr[...])
     window = window[: 2 * count] + window[2 * count :]
     for r in range(rows):
         out_scr[pl.ds(r, 2 * count, stride=rows), :] = window[:, r * LANES : (r + 1) * LANES]
@@ -152,10 +162,10 @@
     facets,
     subs,
     length,
-    sub_ref,
-    off_ref,
-    owner_ref,
-    kind_ref,
+    sub_hbm,
+    off_hbm,
+    owner_hbm,
+    kind_hbm,
     after_ref,
     screens_ref,
     place_ref,
@@ -168,7 +178,15 @@
     seen,
     cos_scr,
     sin_scr,
+    sub_ref,
+    off_ref,
+    owner_ref,
+    kind_ref,
+    sems,
 ):
+    copies = scalars(
+        [(sub_hbm, sub_ref), (off_hbm, off_ref), (owner_hbm, owner_ref), (kind_hbm, kind_ref)], sems
+    )
     count = sub_ref.shape[0]
     rows = cos_ref.shape[0] // count
     span = screens_ref.shape[2] // 2
@@ -176,6 +194,17 @@
     chunks = length // LANES
     mine = lax.axis_index("facet")
     my_sub = lax.axis_index("sub")
+
+    shape = (chunks, LANES)
+    cos, sin = circle(iota(shape, 0) * iota(shape, 1), chunks)
+    table = jnp.concatenate(
+        [jnp.concatenate([cos, -sin], axis=1), jnp.concatenate([sin, cos], axis=1)], axis=0
+    )
+    inv_ref[: 2 * chunks, :] = high_low(table, False)
+    inv_ref[2 * chunks :, :] = high_low(table, True)
+
+    for copy in copies:
+        copy.wait()
     my_off = off_ref[mine]
 
     shape = (LANES, 2 * LANES)
@@ -241,22 +270,15 @@
     coarse_ref[:M, :] = high_low(jnp.where(lane_im, -sin, cos), low)
     coarse_ref[M:, :] = high_low(jnp.where(lane_im, cos, sin), low)
 
-    shape = (chunks, LANES)
-    cos, sin = circle(iota(shape, 0) * iota(shape, 1), chunks)
-    table = jnp.concatenate(
-        [jnp.concatenate([cos, -sin], axis=1), jnp.concatenate([sin, cos], axis=1)], axis=0
-    )
-    inv_ref[: 2 * chunks, :] = high_low(table, False)
-    inv_ref[2 * chunks :, :] = high_low(table, True)
-
-
-def backward_kernel(facets, sub_ref, off_ref, *refs):
+
+def backward_kernel(facets, sub_hbm, off_hbm, *refs):
     arrived = refs[:facets]
     place_ref, cos_ref, sin_ref, both_ref, rank_ref, coarse_ref = refs[facets : facets + 6]
-    inv_ref, turn_ref, out_ref, re_scr, im_scr, out_scr = refs[facets + 6 :]
+    inv_ref, turn_ref, out_hbm, re_scr, im_scr, out_scr, flat_scr, sub_ref, off_ref, sems, out_sems = refs[facets + 6 :]
+    copies = scalars([(sub_hbm, sub_ref), (off_hbm, off_ref)], sems)
     mine = lax.axis_index("facet")
-    rows = out_ref.shape[1]
-    length = out_ref.shape[2] // 2
+    rows = out_hbm.shape[1]
+    length = out_hbm.shape[2] // 2
     chunks = length // LANES
     count = sub_ref.shape[0]
     windows = count * rows
@@ -270,6 +292,8 @@
     ranked = jnp.concatenate([ranked[c : c + count] for c in range(0, ranked.shape[0], count)], axis=1)
     weights = dot(ranked, both_ref[...])
 
+    for copy in copies:
+        copy.wait()
     lane = iota((rows, LANES), 1)
     for j in range(count):
         weight = weights[j : j + 1, :]
@@ -304,8 +328,17 @@
     points = points[: 2 * chunks] + points[2 * chunks :]
     for r in range(rows):
         out_scr[pl.ds(r, 2 * chunks, stride=rows), :] = points[:, r * LANES : (r + 1) * LANES]
-    for c in range(2 * chunks):
-        out_ref[0, :, c * LANES : (c + 1) * LANES] = out_scr[c * rows : (c + 1) * rows, :]
+    parts = out_sems.shape[0]
+    width = 2 * length // parts
+    copies = []
+    for p in range(parts):
+        for c in range(p * width // LANES, (p + 1) * width // LANES):
+            flat_scr[:, c * LANES : (c + 1) * LANES] = out_scr[c * rows : (c + 1) * rows, :]
+        part = pl.ds(p * width, width)
+        copies.append(pltpu.make_async_copy(flat_scr.at[:, part], out_hbm.at[0, :, part], out_sems.at[p]))
+        copies[-1].start()
+    for copy in copies:
+        copy.wait()
 
 
 def local(strips, facet_offset, subgrid_offset, owner, screen_index, screens, grid_weight):
@@ -317,10 +350,14 @@
     count = subgrid_offset.shape[0]
     span = grid_weight.shape[1]
     kinds = screens.shape[0]
-    smem = pl.BlockSpec(memory_space=pltpu.SMEM)
+    hbm = pl.BlockSpec(memory_space=pl.ANY)
     vmem = pl.BlockSpec(memory_space=pltpu.VMEM)
     limit = pltpu.CompilerParams(vmem_limit_bytes=32 * 1024 * 1024)
     shaped = jax.ShapeDtypeStruct
+
+    subgrid_offset, facet_offset, owner, screen_index = [
+        pltpu.with_memory_space_constraint(x, pltpu.HBM) for x in (subgrid_offset, facet_offset, owner, screen_index)
+    ]
 
     def swap(x, step):
         return lax.ppermute(x, "facet", [(i, i ^ step) for i in range(facets)])
@@ -341,22 +378,21 @@
     while step < subs:
         beside = lax.ppermute(held, "sub", [(k, k ^ step) for k in range(subs)])
         if step == 1:
-            twisted = pl.pallas_call(
-                inner_kernel,
-                out_shape=shaped((rows * LANES, 2 * LANES), BF),
-                in_specs=[vmem] * 3,
+            windows = pl.pallas_call(
+                forward_kernel,
+                out_shape=shaped((count * rows, LANES), BF),
+                in_specs=[hbm] * 2 + [vmem] * 3,
                 out_specs=vmem,
-                scratch_shapes=[pltpu.VMEM((rows * 2 * chunks, LANES), F32)],
+                scratch_shapes=[
+                    pltpu.VMEM((rows * 2 * chunks, LANES), F32),
+                    pltpu.VMEM((rows * LANES, 2 * LANES), BF),
+                    pltpu.VMEM((2 * count * rows, LANES), F32),
+                    pltpu.SMEM((count,), jnp.int32),
+                    pltpu.SMEM((facets,), jnp.int32),
+                    pltpu.SemaphoreType.DMA((2,)),
+                ],
                 compiler_params=limit,
-            )(strips, turn, fwd)
-            windows = pl.pallas_call(
-                functools.partial(window_kernel, length),
-                out_shape=shaped((count * rows, LANES), BF),
-                in_specs=[smem] * 2 + [vmem],
-                out_specs=vmem,
-                scratch_shapes=[pltpu.VMEM((2 * count * rows, LANES), F32)],
-                compiler_params=limit,
-            )(subgrid_offset, facet_offset, twisted)
+            )(subgrid_offset, facet_offset, strips, turn, fwd)
         step *= 2
         if step < subs:
             held = pl.pallas_call(
@@ -381,12 +417,17 @@
             shaped((2 * M, 4 * count), BF),
             shaped((4 * chunks, 2 * LANES), BF),
         ],
-        in_specs=[smem] * 4 + [pl.BlockSpec(memory_space=pl.ANY), vmem],
+        in_specs=[hbm] * 5 + [vmem],
         out_specs=[vmem] * 7,
         scratch_shapes=[
             pltpu.SMEM((facets * subs,), jnp.int32),
             pltpu.VMEM((kinds * tall, LANES), F32),
             pltpu.VMEM((kinds * tall, LANES), F32),
+            pltpu.SMEM((count,), jnp.int32),
+            pltpu.SMEM((facets,), jnp.int32),
+            pltpu.SMEM((count,), jnp.int32),
+            pltpu.SMEM((count,), jnp.int32),
+            pltpu.SemaphoreType.DMA((4,)),
         ],
         compiler_params=limit,
         cost_estimate=cost(2*10**10),
@@ -411,12 +452,17 @@
     return pl.pallas_call(
         functools.partial(backward_kernel, facets),
         out_shape=shaped((1, rows, 2 * length), F32),
-        in_specs=[smem] * 2 + [vmem] * (facets + 8),
-        out_specs=vmem,
+        in_specs=[hbm] * 2 + [vmem] * (facets + 8),
+        out_specs=hbm,
         scratch_shapes=[
             pltpu.VMEM((rows * count, LANES), F32),
             pltpu.VMEM((rows * count, LANES), F32),
             pltpu.VMEM((2 * chunks * rows, LANES), F32),
+            pltpu.VMEM((rows, 2 * length), F32),
+            pltpu.SMEM((count,), jnp.int32),
+            pltpu.SMEM((facets,), jnp.int32),
+            pltpu.SemaphoreType.DMA((2,)),
+            pltpu.SemaphoreType.DMA((4,)),
         ],
         compiler_params=limit,
     )(subgrid_offset, facet_offset, *arrived, *prepared, turn)

time: 21.6 us -> 21.2 us (0.981)
  Pallas kernels: 5.74 us -> 5.26 us
  local copies, waits for them, and re-layouts: 0.3 us -> 0.01 us
  waiting for transfers between devices: 5.8 us -> 6.03 us
    pallas_call x1, Pallas kernels: 2.71 us -> 2.26 us  [local(): pl.pallas_call(functools.partial(backward_kernel, facets), out_shape=shap...]
    unnamed x14 -> x6, local copies, waits for them, and re-layouts: 0.3 us -> 0.01 us
    pallas_call x2 -> x1, Pallas kernels: 1.47 us -> 1.3 us  [local(): pl.pallas_call(forward_kernel, out_shape=shaped((count * rows, LANES), BF...]
  transfers between devices with their start and end apart: 9 -> 9, of which waited for: 6 -> 7; matrix products, arithmetic and copies ran while one was open for 0% -> 0% of each run, Pallas kernels for 14% -> 14%
where the time goes in v3:
time: 21.2 us; the launch traced here: 21 us
  starting transfers between devices  9.63 us (45%)
  waiting for transfers between devices  6.03 us (28%)
  Pallas kernels  5.26 us (25%)
    ppermute x2, starting transfers between devices, local(): beside = lax.ppermute(held, 'sub', [(k, k ^ step) for k in range(subs)])  6.06 us
    ppermute x7, waiting for transfers between devices, swap(): return lax.ppermute(x, 'facet', [(i, i ^ step) for i in range(facets)])  5.5 us
    ppermute x7, starting transfers between devices, swap(): return lax.ppermute(x, 'facet', [(i, i ^ step) for i in range(facets)])  3.57 us
    pallas_call x1, Pallas kernels, local(): pl.pallas_call(functools.partial(backward_kernel, facets), out_shape=shap...  2.26 us
    pallas_call x1, Pallas kernels, local(): pl.pallas_call(functools.partial(prepare_kernel, facets, subs, length), o...  1.53 us
    pallas_call x1, Pallas kernels, local(): pl.pallas_call(forward_kernel, out_shape=shaped((count * rows, LANES), BF...  1.3 us
    ppermute x2, waiting for transfers between devices, local(): beside = lax.ppermute(held, 'sub', [(k, k ^ step) for k in range(subs)])  0.53 us
  transfers between devices with their start and end apart: 9, of which 7 were waited for; matrix products, arithmetic and copies ran while one was open for 0% of the time, Pallas kernels for 14%

profile of v3, /device:TPU:0, one launch (start us, length us, event | category | flops | bytes accessed | tf_op | source)
XLA Modules:
  0.0 21.0 jit_solution(54280444296207459)
XLA Ops:
  0.0 0.0 copy-start
  0.0 0.0 copy-start.2
  0.0 3.0 %collective-permute-start = (f32[4,512]{1,0:T(4,128)}, f32[4,512]{1,0:T(4,128)S(1)}, u32[]{:S(2)}, u32[]{:S(2)}) collective-permute-start(f32[4,512]{1,0:T(4,128)} %refs_0_.1), channel_id=1, source_target_pairs={{0,1},{1,0},{2,3},{3,2},{4,5},{5,4},{6,7},{7,6},{8,9},{9,8},{10,11... | collective-permute-start | bytes 24584 | tf_op jit(solution)/shard_map/ppermute | solution.py:379
  3.0 0.1 shard_map.73
  3.2 0.0 copy-done
  3.2 0.0 copy-start.1
  3.2 1.3 %shard_map.74.windows_ref = bf16[256,128]{1,0:T(8,128)(2,1)S(1)} custom-call(s32[32]{0:T(128)} %sub_hbm.5, s32[8]{0:T(128)} %off_hbm.5, bf16[1,8,8192]{2,1,0:T(8,128)(2,1)S(1)} %copy-done, f32[256,128]{1,0:T(8,128)S(1)} %get-tuple-element.16.turn_ref.refs_15_, bf16[64,128]{1,0:T(8,128)(2,1)S(1)} %get-tuple-element.17.fwd_ref), custom_call_target="tpu_custom_call" | custom-call | tf_op jit(solution)/shard_map/pallas_call | solution.py:381
  4.5 0.4 %collective-permute-done.refs_1_ = f32[4,512]{1,0:T(4,128)S(1)} collective-permute-done((f32[4,512]{1,0:T(4,128)}, f32[4,512]{1,0:T(4,128)S(1)}, u32[]{:S(2)}, u32[]{:S(2)}) %collective-permute-start) | collective-permute-done | bytes 8224 | tf_op jit(solution)/shard_map/ppermute | solution.py:379
  4.9 0.0 copy-done.1
  4.9 3.0 %collective-permute-start.1 = (f32[8,512]{1,0:T(8,128)S(1)}, f32[8,512]{1,0:T(8,128)S(1)}, u32[]{:S(2)}, u32[]{:S(2)}) collective-permute-start(f32[8,512]{1,0:T(8,128)S(1)} %shard_map.75.after_ref.refs_0_), channel_id=1, source_target_pairs={{0,2},{1,3},{2,0},{3,1},{4,6},{5,7},{6,4},{7,5},{8,10},{9,11},{10,... | collective-permute-start | bytes 49160 | tf_op jit(solution)/shard_map/ppermute | solution.py:379
  7.9 0.0 copy-done.2
  7.9 1.5 %shard_map.76 = (bf16[1024,256]{1,0:T(8,128)(2,1)S(1)}, f32[256,128]{1,0:T(8,128)S(1)}, f32[256,128]{1,0:T(8,128)S(1)}, bf16[512,128]{1,0:T(8,128)(2,1)S(1)}, bf...) custom-call(s32[32]{0:T(128)} %sub_hbm.5, s32[8]{0:T(128)} %off_hbm.5, ...), custom_call_target="tpu_custom_call" | custom-call | flops 20000000000 | bytes 1048576 | tf_op jit(solution)/shard_map/pallas_call | solution.py:409
  9.5 0.2 collective-permute-done.1.refs_1_
  9.6 2.8 %collective-permute-start.7 = (bf16[320,128]{1,0:T(8,128)(2,1)S(1)}, bf16[320,128]{1,0:T(8,128)(2,1)S(1)}, u32[]{:S(2)}, u32[]{:S(2)}) collective-permute-start(bf16[320,128]{1,0:T(8,128)(2,1)S(1)} %shard_map.77.refs_0_), channel_id=1, source_target_pairs={{0,24},{4,28},{8,16},{12,20},{16,8},{20,12},{24,0},{28,4},{1,25},{... | collective-permute-start | bytes 245768 | tf_op jit(solution)/shard_map/ppermute | solution.py:363
  12.5 0.5 %collective-permute-start.5 = (bf16[320,128]{1,0:T(8,128)(2,1)S(1)}, bf16[320,128]{1,0:T(8,128)(2,1)S(1)}, u32[]{:S(2)}, u32[]{:S(2)}) collective-permute-start(bf16[320,128]{1,0:T(8,128)(2,1)S(1)} %shard_map.77.refs_0_), channel_id=1, source_target_pairs={{0,16},{4,20},{8,24},{12,28},{16,0},{20,4},{24,8},{28,12},{1,17},{... | collective-permute-start | bytes 245768 | tf_op jit(solution)/shard_map/ppermute | solution.py:363
  13.0 0.2 collective-permute-start.3
  13.2 0.0 collective-permute-start.2
  13.2 2.6 %collective-permute-done.7.refs_6_ = bf16[320,128]{1,0:T(8,128)(2,1)S(1)} collective-permute-done((bf16[320,128]{1,0:T(8,128)(2,1)S(1)}, bf16[320,128]{1,0:T(8,128)(2,1)S(1)}, u32[]{:S(2)}, u32[]{:S(2)}) %collective-permute-start.7) | collective-permute-done | bytes 81952 | tf_op jit(solution)/shard_map/ppermute | solution.py:363
  15.8 0.0 collective-permute-start.8
  15.8 1.1 %collective-permute-done.5.refs_4_ = bf16[320,128]{1,0:T(8,128)(2,1)S(1)} collective-permute-done((bf16[320,128]{1,0:T(8,128)(2,1)S(1)}, bf16[320,128]{1,0:T(8,128)(2,1)S(1)}, u32[]{:S(2)}, u32[]{:S(2)}) %collective-permute-start.5) | collective-permute-done | bytes 81952 | tf_op jit(solution)/shard_map/ppermute | solution.py:363
  16.9 0.0 collective-permute-start.6
  16.9 0.5 %collective-permute-done.3.refs_2_ = bf16[320,128]{1,0:T(8,128)(2,1)S(1)} collective-permute-done((bf16[320,128]{1,0:T(8,128)(2,1)S(1)}, bf16[320,128]{1,0:T(8,128)(2,1)S(1)}, u32[]{:S(2)}, u32[]{:S(2)}) %collective-permute-start.3) | collective-permute-done | bytes 81952 | tf_op jit(solution)/shard_map/ppermute | solution.py:363
  17.4 0.0 collective-permute-start.4
  17.4 0.0 collective-permute-done.2.refs_1_
  17.4 0.0 collective-permute-done.8.refs_7_
  17.4 0.8 %collective-permute-done.6.refs_5_ = bf16[320,128]{1,0:T(8,128)(2,1)S(1)} collective-permute-done((bf16[320,128]{1,0:T(8,128)(2,1)S(1)}, bf16[320,128]{1,0:T(8,128)(2,1)S(1)}, u32[]{:S(2)}, u32[]{:S(2)}) %collective-permute-start.6) | collective-permute-done | bytes 81952 | tf_op jit(solution)/shard_map/ppermute | solution.py:363
  18.2 0.5 %collective-permute-done.4.refs_3_ = bf16[320,128]{1,0:T(8,128)(2,1)S(1)} collective-permute-done((bf16[320,128]{1,0:T(8,128)(2,1)S(1)}, bf16[320,128]{1,0:T(8,128)(2,1)S(1)}, u32[]{:S(2)}, u32[]{:S(2)}) %collective-permute-start.4) | collective-permute-done | bytes 81952 | tf_op jit(solution)/shard_map/ppermute | solution.py:363
  18.7 2.3 %shard_map.78 = f32[1,8,8192]{2,1,0:T(8,128)} custom-call(s32[32]{0:T(128)} %sub_hbm.5, s32[8]{0:T(128)} %off_hbm.5, bf16[320,128]{1,0:T(8,128)(2,1)S(1)} %shard_map.77.refs_0_, bf16[320,128]{1,0:T(8,128)(2,1)S(1)} %collective-permute-done.2.refs_1_, bf16[320,128]{1,0:T(8,128)(2,1)S(1)} %collective-permute-done.3.refs_2_, ...), custom_call_target="tpu_custom_call" | custom-call | tf_op jit(solution)/shard_map/pallas_call | solution.py:452
  (2 shorter events, 0.0 us)
Async XLA Ops:
  0.0 3.2 %copy-start = (bf16[1,8,8192]{2,1,0:T(8,128)(2,1)S(1)}, bf16[1,8,8192]{2,1,0:T(8,128)(2,1)}, u32[]{:S(2)}) copy-start(bf16[1,8,8192]{2,1,0:T(8,128)(2,1)} %strips_ref.1) | copy-start | bytes 393220
  0.0 7.9 %copy-start.2 = (bf16[16,32,1024]{2,1,0:T(8,128)(2,1)S(1)}, bf16[16,32,1024]{2,1,0:T(8,128)(2,1)}, u32[]{:S(2)}) copy-start(bf16[16,32,1024]{2,1,0:T(8,128)(2,1)} %screens_ref.1) | copy-start | bytes 3145732
  0.0 4.9 %collective-permute-start = (f32[4,512]{1,0:T(4,128)}, f32[4,512]{1,0:T(4,128)S(1)}, u32[]{:S(2)}, u32[]{:S(2)}) collective-permute-start(f32[4,512]{1,0:T(4,128)} %refs_0_.1), channel_id=1, source_target_pairs={{0,1},{1,0},{2,3},{3,2},{4,5},{5,4},{6,7},{7,6},{8,9},{9,8},{10,11... | collective-permute-start | bytes 24584 | tf_op jit(solution)/shard_map/ppermute | solution.py:379
  3.2 1.7 %copy-start.1 = (f32[4,512]{1,0:T(4,128)S(1)}, f32[4,512]{1,0:T(4,128)}, u32[]{:S(2)}) copy-start(f32[4,512]{1,0:T(4,128)} %refs_0_.1) | copy-start | bytes 24580
  4.9 4.8 %collective-permute-start.1 = (f32[8,512]{1,0:T(8,128)S(1)}, f32[8,512]{1,0:T(8,128)S(1)}, u32[]{:S(2)}, u32[]{:S(2)}) collective-permute-start(f32[8,512]{1,0:T(8,128)S(1)} %shard_map.75.after_ref.refs_0_), channel_id=1, source_target_pairs={{0,2},{1,3},{2,0},{3,1},{4,6},{5,7},{6,4},{7,5},{8,10},{9,11},{10,... | collective-permute-start | bytes 49160 | tf_op jit(solution)/shard_map/ppermute | solution.py:379
  9.6 6.2 %collective-permute-start.7 = (bf16[320,128]{1,0:T(8,128)(2,1)S(1)}, bf16[320,128]{1,0:T(8,128)(2,1)S(1)}, u32[]{:S(2)}, u32[]{:S(2)}) collective-permute-start(bf16[320,128]{1,0:T(8,128)(2,1)S(1)} %shard_map.77.refs_0_), channel_id=1, source_target_pairs={{0,24},{4,28},{8,16},{12,20},{16,8},{20,12},{24,0},{28,4},{1,25},{... | collective-permute-start | bytes 245768 | tf_op jit(solution)/shard_map/ppermute | solution.py:363
  12.5 4.4 %collective-permute-start.5 = (bf16[320,128]{1,0:T(8,128)(2,1)S(1)}, bf16[320,128]{1,0:T(8,128)(2,1)S(1)}, u32[]{:S(2)}, u32[]{:S(2)}) collective-permute-start(bf16[320,128]{1,0:T(8,128)(2,1)S(1)} %shard_map.77.refs_0_), channel_id=1, source_target_pairs={{0,16},{4,20},{8,24},{12,28},{16,0},{20,4},{24,8},{28,12},{1,17},{... | collective-permute-start | bytes 245768 | tf_op jit(solution)/shard_map/ppermute | solution.py:363
  13.0 4.4 %collective-permute-start.3 = (bf16[320,128]{1,0:T(8,128)(2,1)S(1)}, bf16[320,128]{1,0:T(8,128)(2,1)S(1)}, u32[]{:S(2)}, u32[]{:S(2)}) collective-permute-start(bf16[320,128]{1,0:T(8,128)(2,1)S(1)} %shard_map.77.refs_0_), channel_id=1, source_target_pairs={{0,8},{4,12},{8,0},{12,4},{16,24},{20,28},{24,16},{28,20},{1,9},{5... | collective-permute-start | bytes 245768 | tf_op jit(solution)/shard_map/ppermute | solution.py:363
  13.2 4.2 %collective-permute-start.2 = (bf16[320,128]{1,0:T(8,128)(2,1)S(1)}, bf16[320,128]{1,0:T(8,128)(2,1)S(1)}, u32[]{:S(2)}, u32[]{:S(2)}) collective-permute-start(bf16[320,128]{1,0:T(8,128)(2,1)S(1)} %shard_map.77.refs_0_), channel_id=1, source_target_pairs={{0,4},{4,0},{8,12},{12,8},{16,20},{20,16},{24,28},{28,24},{1,5},{5... | collective-permute-start | bytes 245768 | tf_op jit(solution)/shard_map/ppermute | solution.py:363
  15.8 1.6 %collective-permute-start.8 = (bf16[320,128]{1,0:T(8,128)(2,1)S(1)}, bf16[320,128]{1,0:T(8,128)(2,1)S(1)}, u32[]{:S(2)}, u32[]{:S(2)}) collective-permute-start(bf16[320,128]{1,0:T(8,128)(2,1)S(1)} %collective-permute-done.7.refs_6_), channel_id=1, source_target_pairs={{0,4},{4,0},{8,12},{12,8},{16,20},{20,16},{24,28},{28,24},{1,5},{5... | collective-permute-start | bytes 245768 | tf_op jit(solution)/shard_map/ppermute | solution.py:363
  16.9 1.3 %collective-permute-start.6 = (bf16[320,128]{1,0:T(8,128)(2,1)S(1)}, bf16[320,128]{1,0:T(8,128)(2,1)S(1)}, u32[]{:S(2)}, u32[]{:S(2)}) collective-permute-start(bf16[320,128]{1,0:T(8,128)(2,1)S(1)} %collective-permute-done.5.refs_4_), channel_id=1, source_target_pairs={{0,4},{4,0},{8,12},{12,8},{16,20},{20,16},{24,28},{28,24},{1,5},{5... | collective-permute-start | bytes 245768 | tf_op jit(solution)/shard_map/ppermute | solution.py:363
  17.4 1.3 %collective-permute-start.4 = (bf16[320,128]{1,0:T(8,128)(2,1)S(1)}, bf16[320,128]{1,0:T(8,128)(2,1)S(1)}, u32[]{:S(2)}, u32[]{:S(2)}) collective-permute-start(bf16[320,128]{1,0:T(8,128)(2,1)S(1)} %collective-permute-done.3.refs_2_), channel_id=1, source_target_pairs={{0,4},{4,0},{8,12},{12,8},{16,20},{20,16},{24,28},{28,24},{1,5},{5... | collective-permute-start | bytes 245768 | tf_op jit(solution)/shard_map/ppermute | solution.py:363

commit v4 on v3

--- a/solution.py
+++ b/solution.py
@@ -77,22 +77,27 @@
     fwd_ref[...] = high_low(table, lane >= 2 * chunks)
 
 
-def join_kernel(*refs):
-    out_ref = refs[-1]
-    row = 0
-    for ref in refs[:-1]:
-        out_ref[row : row + ref.shape[0], :] = ref[...]
-        row += ref.shape[0]
-
-
-def pack_kernel(windows_ref, *refs):
-    out_ref = refs[-1]
-    out_ref[: windows_ref.shape[0], :] = windows_ref[...]
-    held = jnp.concatenate([ref[...] for ref in refs[:-1]], axis=0)
-    row = windows_ref.shape[0]
-    for c in range(0, held.shape[1], LANES):
-        out_ref[row : row + held.shape[0], :] = held[:, c : c + LANES].astype(BF)
-        row += held.shape[0]
+def join_kernel(first_ref, second_ref, out_ref):
+    out_ref[: first_ref.shape[0], :] = first_ref[...]
+    out_ref[first_ref.shape[0] :, :] = second_ref[...]
+
+
+def merge_kernel(windows_ref, passed_ref, shift_ref, own_ref, *out_refs):
+    both = jnp.concatenate([windows_ref[...], passed_ref[...]], axis=1)
+    merged = dot(both, shift_ref[...])
+    own_ref[...] = merged[:, :LANES]
+    for n, out_ref in enumerate(out_refs):
+        out_ref[...] = merged[:, (n + 1) * LANES : (n + 2) * LANES].astype(BF)
+
+
+def pack_kernel(others, *refs):
+    merged_refs, held_refs, out_refs = refs[:others], refs[others : others + 2], refs[others + 2 :]
+    held = jnp.concatenate([ref[...] for ref in held_refs], axis=0)
+    laid = jnp.concatenate([held[:, c : c + LANES] for c in range(0, held.shape[1], LANES)], axis=0).astype(BF)
+    out_refs[0][...] = laid
+    for ref, out_ref in zip(merged_refs, out_refs[1:]):
+        out_ref[: ref.shape[0], :] = ref[...]
+        out_ref[ref.shape[0] :, :] = laid
 
 
 def scalars(pairs, sems):
@@ -103,7 +108,19 @@
 
 
 def forward_kernel(
-    sub_hbm, off_hbm, strips_ref, turn_ref, fwd_ref, out_ref, in_scr, mid_scr, out_scr, sub_ref, off_ref, sems
+    sub_hbm,
+    off_hbm,
+    strips_ref,
+    turn_ref,
+    fwd_ref,
+    out_ref,
+    shift_ref,
+    in_scr,
+    mid_scr,
+    out_scr,
+    sub_ref,
+    off_ref,
+    sems,
 ):
     copies = scalars([(sub_hbm, sub_ref), (off_hbm, off_ref)], sems)
     mine = lax.axis_index("facet")
@@ -131,6 +148,16 @@
 
     for copy in copies:
         copy.wait()
+    shape = (LANES, LANES)
+    row = iota(shape, 0)
+    lane = iota(shape, 1)
+    apart = (lane // M - row // M) * 8192 + (lane % M - row % M)
+    for n in range(shift_ref.shape[1] // LANES):
+        for core in range(2):
+            delta = off_ref[mine ^ core] - off_ref[mine ^ (2 * n)]
+            rows_here = slice(core * LANES, (core + 1) * LANES)
+            shift_ref[rows_here, n * LANES : (n + 1) * LANES] = jnp.where(apart == delta, 1.0, 0.0).astype(BF)
+
     starts = [start_of(mine, sub_ref, off_ref, j, length) for j in range(count)]
     block = column([s // M for s in starts], LANES)
     cos, sin = circle(block * iota((count, LANES), 1), length // M)
@@ -168,9 +195,9 @@
     kind_hbm,
     after_ref,
     screens_ref,
-    place_ref,
     cos_ref,
     sin_ref,
+    gather_ref,
     both_ref,
     rank_ref,
     coarse_ref,
@@ -190,7 +217,6 @@
     count = sub_ref.shape[0]
     rows = cos_ref.shape[0] // count
     span = screens_ref.shape[2] // 2
-    pieces = span // LANES
     chunks = length // LANES
     mine = lax.axis_index("facet")
     my_sub = lax.axis_index("sub")
@@ -206,15 +232,6 @@
     for copy in copies:
         copy.wait()
     my_off = off_ref[mine]
-
-    shape = (LANES, 2 * LANES)
-    row = iota(shape, 0)
-    lane = iota(shape, 1)
-    lane_part = jnp.where((lane // M == 1) | (lane // M == 2), 1, 0)
-    apart = (lane_part - row // M) * 8192 + (lane % M - row % M)
-    for s in range(facets):
-        delta = off_ref[mine ^ s] - my_off
-        place_ref[s * LANES : (s + 1) * LANES, :] = jnp.where(apart == delta, 1.0, 0.0).astype(BF)
 
     shape = (span, LANES)
     row = iota(shape, 0)
@@ -228,17 +245,18 @@
     block = pl.ds(pl.multiple_of(first, tall), tall)
     cosines = screens_ref[:, block, :span].reshape(kinds * tall, span)
     sines = screens_ref[:, block, span:].reshape(kinds * tall, span)
+    both_ref[...] = both
     cos_scr[...] = dot(cosines, both)
     sin_scr[...] = dot(sines, signed)
     for j in range(count):
         kind = pl.multiple_of(kind_ref[j] * tall + my_sub * rows - first, rows)
         cos_ref[j * rows : (j + 1) * rows, :] = cos_scr[pl.ds(kind, rows), :]
         sin_ref[j * rows : (j + 1) * rows, :] = sin_scr[pl.ds(kind, rows), :]
-    both_ref[...] = both
 
     for o in range(facets * subs):
         seen[o] = 0
     held = subs * CAP
+    pieces = span // LANES
     places = []
     for j in range(count):
         who = owner_ref[j]
@@ -246,13 +264,19 @@
         seen[who] = slot + 1
         facet_step = (who // subs) ^ mine
         sub_step = (who % subs) ^ my_sub
-        places.append(facet_step * held * pieces + sub_step * CAP + slot)
+        block = facet_step % 2 * (facets // 2) + facet_step // 2
+        places.append(block * held * pieces + sub_step * CAP + slot)
     width = rank_ref.shape[1]
     place = column(places, width)
     lane = iota((count, width), 1)
     for c in range(pieces):
         hit = jnp.where(lane == place + c * held, 1.0, 0.0)
         rank_ref[c * count : (c + 1) * count, :] = hit.astype(BF)
+
+    lane = iota((rows, LANES), 1)
+    for j in range(count):
+        shift = start_of(mine, sub_ref, off_ref, j, length) & (M - 1)
+        gather_ref[j * rows : (j + 1) * rows, :] = (lane - shift) & (LANES - 1)
 
     lane = iota((8, 4 * count), 1)
     block = jnp.zeros((8, 4 * count), jnp.int32)
@@ -271,41 +295,44 @@
     coarse_ref[M:, :] = high_low(jnp.where(lane_im, cos, sin), low)
 
 
-def backward_kernel(facets, sub_hbm, off_hbm, *refs):
-    arrived = refs[:facets]
-    place_ref, cos_ref, sin_ref, both_ref, rank_ref, coarse_ref = refs[facets : facets + 6]
-    inv_ref, turn_ref, out_hbm, re_scr, im_scr, out_scr, flat_scr, sub_ref, off_ref, sems, out_sems = refs[facets + 6 :]
-    copies = scalars([(sub_hbm, sub_ref), (off_hbm, off_ref)], sems)
-    mine = lax.axis_index("facet")
+def tail_kernel(block_ref, out_ref):
+    out_ref[...] = block_ref[block_ref.shape[0] - out_ref.shape[0] :, :]
+
+
+def screen_kernel(own_ref, *refs):
+    arrived, (cos_ref, sin_ref, out_ref) = refs[:-3], refs[-3:]
+    windows = own_ref.shape[0]
+    for at in range(0, windows, 16):
+        pair = slice(at, at + 16)
+        total = own_ref[pair, :]
+        for ref in arrived:
+            total = total + ref[pair, :].astype(F32)
+        out_ref[pair, :] = total * cos_ref[pair, :] + pltpu.roll(total, M, 1) * sin_ref[pair, :]
+
+
+def backward_kernel(others, size, product_ref, own_rows_ref, *refs):
+    arrived, across, refs = refs[:others][::-1], refs[others : 2 * others + 1][::-1], refs[2 * others + 1 :]
+    gather_ref, both_ref, rank_ref, coarse_ref, inv_ref, turn_ref, out_hbm = refs[:7]
+    re_scr, im_scr, out_scr, flat_scr, out_sems = refs[7:]
     rows = out_hbm.shape[1]
     length = out_hbm.shape[2] // 2
     chunks = length // LANES
-    count = sub_ref.shape[0]
-    windows = count * rows
-
-    total = dot(arrived[0][:windows, :], place_ref[:LANES, :])
-    for s in range(1, facets):
-        total = total + dot(arrived[s][:windows, :], place_ref[s * LANES : (s + 1) * LANES, :])
-
-    held = jnp.concatenate([block[windows:, :] for block in arrived], axis=0)
-    ranked = dot(rank_ref[...], held).astype(BF)
+    windows = product_ref.shape[0]
+    count = windows // rows
+
+    held = [own_rows_ref[...]] + [ref[windows:, :] for ref in arrived] + [ref[...] for ref in across]
+    ranked = dot(rank_ref[...], jnp.concatenate(held, axis=0)).astype(BF)
     ranked = jnp.concatenate([ranked[c : c + count] for c in range(0, ranked.shape[0], count)], axis=1)
     weights = dot(ranked, both_ref[...])
 
-    for copy in copies:
-        copy.wait()
-    lane = iota((rows, LANES), 1)
     for j in range(count):
-        weight = weights[j : j + 1, :]
-        cos = cos_ref[j * rows : (j + 1) * rows, :] * weight
-        sin = sin_ref[j * rows : (j + 1) * rows, :] * weight
-        here = total[j * rows : (j + 1) * rows, :LANES]
-        swapped = total[j * rows : (j + 1) * rows, LANES:]
-        value = (here * cos + swapped * sin).astype(BF).astype(F32)
-        shift = start_of(mine, sub_ref, off_ref, j, length) & (M - 1)
-        mask = (lane >= shift) & (lane < shift + M)
-        re_scr[pl.ds(j, rows, stride=count), :] = jnp.where(mask, pltpu.roll(value, shift, 1), 0.0)
-        im_scr[pl.ds(j, rows, stride=count), :] = jnp.where(mask, pltpu.roll(value, shift + M, 1), 0.0)
+        value = product_ref[j * rows : (j + 1) * rows, :] * weights[j : j + 1, :]
+        value = value.astype(BF).astype(F32)
+        place = gather_ref[j * rows : (j + 1) * rows, :]
+        re = jnp.take_along_axis(value, place, axis=1)
+        im = jnp.take_along_axis(value, place ^ M, axis=1)
+        re_scr[pl.ds(j, rows, stride=count), :] = jnp.where(place < M, re, 0.0)
+        im_scr[pl.ds(j, rows, stride=count), :] = jnp.where(place < M, im, 0.0)
 
     halves = []
     for scr in (re_scr, im_scr):
@@ -374,15 +401,14 @@
     )()
     held = grid_weight
     step = 1
-    others = []
     while step < subs:
-        beside = lax.ppermute(held, "sub", [(k, k ^ step) for k in range(subs)])
+        last, beside = held, lax.ppermute(held, "sub", [(k, k ^ step) for k in range(subs)])
         if step == 1:
-            windows = pl.pallas_call(
+            windows, shift = pl.pallas_call(
                 forward_kernel,
-                out_shape=shaped((count * rows, LANES), BF),
+                out_shape=[shaped((count * rows, LANES), BF), shaped((2 * LANES, facets // 2 * LANES), BF)],
                 in_specs=[hbm] * 2 + [vmem] * 3,
-                out_specs=vmem,
+                out_specs=[vmem] * 2,
                 scratch_shapes=[
                     pltpu.VMEM((rows * 2 * chunks, LANES), F32),
                     pltpu.VMEM((rows * LANES, 2 * LANES), BF),
@@ -393,25 +419,25 @@
                 ],
                 compiler_params=limit,
             )(subgrid_offset, facet_offset, strips, turn, fwd)
-        step *= 2
-        if step < subs:
-            held = pl.pallas_call(
+            passed = swap(windows, 1)
+        if step < subs // 2:
+            beside = pl.pallas_call(
                 join_kernel,
                 out_shape=shaped((2 * held.shape[0], span), F32),
                 in_specs=[vmem] * 2,
                 out_specs=vmem,
                 compiler_params=limit,
             )(held, beside)
-            held, _ = lax.optimization_barrier((held, windows))
-    held = [held, beside]
+        step *= 2
+        held, _ = lax.optimization_barrier((beside, windows))
 
     tall = max(rows, 16)
     prepared = pl.pallas_call(
         functools.partial(prepare_kernel, facets, subs, length),
         out_shape=[
-            shaped((facets * LANES, 2 * LANES), BF),
             shaped((count * rows, LANES), F32),
             shaped((count * rows, LANES), F32),
+            shaped((count * rows, LANES), jnp.int32),
             shaped((span, LANES), BF),
             shaped((span // LANES * count, facets * subs * grid_weight.size // LANES), BF),
             shaped((2 * M, 4 * count), BF),
@@ -431,41 +457,61 @@
         ],
         compiler_params=limit,
         cost_estimate=cost(2*10**10),
-    )(subgrid_offset, facet_offset, owner, screen_index, held[0], screens)
-
-    windows, _ = lax.optimization_barrier((windows, prepared[3]))
-    payload = pl.pallas_call(
-        pack_kernel,
-        out_shape=shaped((count * rows + subs * grid_weight.size // LANES, LANES), BF),
-        in_specs=[vmem] * (1 + len(held)),
+    )(subgrid_offset, facet_offset, owner, screen_index, last, screens)
+
+    others = facets // 2 - 1
+    shift, _ = lax.optimization_barrier((shift, prepared[0]))
+    own, *merged = pl.pallas_call(
+        merge_kernel,
+        out_shape=[shaped(windows.shape, F32)] + [shaped(windows.shape, BF)] * others,
+        in_specs=[vmem] * 3,
+        out_specs=[vmem] * (1 + others),
+        compiler_params=limit,
+    )(windows, passed, shift)
+    size = subs * grid_weight.size // LANES
+    own_rows, *payloads = pl.pallas_call(
+        functools.partial(pack_kernel, others),
+        out_shape=[shaped((size, LANES), BF)] + [shaped((count * rows + size, LANES), BF)] * others,
+        in_specs=[vmem] * (others + 2),
+        out_specs=[vmem] * (1 + others),
+        compiler_params=limit,
+    )(*merged, last, beside)
+
+    arrived = [swap(payload, 2 * n + 2) for n, payload in enumerate(payloads)]
+    across = [swap(own_rows, 1), swap(own_rows, 3)]
+    for block in arrived[1:]:
+        tail = pl.pallas_call(
+            tail_kernel,
+            out_shape=shaped((size, LANES), BF),
+            in_specs=[vmem],
+            out_specs=vmem,
+            compiler_params=limit,
+        )(block)
+        across.append(swap(tail, 1))
+
+    cos, sin, *prepared = prepared
+    product = pl.pallas_call(
+        screen_kernel,
+        out_shape=shaped(windows.shape, F32),
+        in_specs=[vmem] * (others + 3),
         out_specs=vmem,
         compiler_params=limit,
-    )(windows, *held)
-
-    arrived = [payload] + [None] * (facets - 1)
-    for s in reversed(range(2, facets, 2)):
-        arrived[s] = swap(payload, s)
-
-    for s in range(0, facets, 2):
-        arrived[s + 1] = swap(arrived[s], 1)
+    )(own, *arrived, cos, sin)
 
     return pl.pallas_call(
-        functools.partial(backward_kernel, facets),
+        functools.partial(backward_kernel, others, size),
         out_shape=shaped((1, rows, 2 * length), F32),
-        in_specs=[hbm] * 2 + [vmem] * (facets + 8),
+        in_specs=[vmem] * (2 * others + 9),
         out_specs=hbm,
         scratch_shapes=[
             pltpu.VMEM((rows * count, LANES), F32),
             pltpu.VMEM((rows * count, LANES), F32),
             pltpu.VMEM((2 * chunks * rows, LANES), F32),
             pltpu.VMEM((rows, 2 * length), F32),
-            pltpu.SMEM((count,), jnp.int32),
-            pltpu.SMEM((facets,), jnp.int32),
-            pltpu.SemaphoreType.DMA((2,)),
             pltpu.SemaphoreType.DMA((4,)),
         ],
         compiler_params=limit,
-    )(subgrid_offset, facet_offset, *arrived, *prepared, turn)
+    )(product, own_rows, *arrived[::-1], *across[::-1], *prepared, turn)
 
 
 def solution(mesh):

time: 21.2 us -> 20.1 us (0.948)
  waiting for transfers between devices: 6.03 us -> 3.08 us
  starting transfers between devices: 9.63 us -> 11.4 us
    ppermute x7 -> x8, waiting for transfers between devices: 5.5 us -> 2.83 us  [swap(): return lax.ppermute(x, 'facet', [(i, i ^ step) for i in range(facets)])]
    ppermute x7 -> x8, starting transfers between devices: 3.57 us -> 5.38 us  [swap(): return lax.ppermute(x, 'facet', [(i, i ^ step) for i in range(facets)])]
    ppermute x2, waiting for transfers between devices: 0.53 us -> 0.25 us  [local(): lax.ppermute(held, 'sub', [(k, k ^ step) for k in range(subs)])]
    pallas_call x3 -> x7, Pallas kernels: 3.57 us -> 3.54 us  [the longest x1 1.85 us: local(): pl.pallas_call(functools.partial(backward_kernel, others, size), out_shap...]
  transfers between devices with their start and end apart: 9 -> 10, of which waited for: 7 -> 5; matrix products, arithmetic and copies ran while one was open for 0% -> 0% of each run, Pallas kernels for 14% -> 17%
where the time goes in v4:
time: 20.1 us; the launch traced here: 20 us
  starting transfers between devices  11.4 us (57%)
  Pallas kernels  5.32 us (26%)
  waiting for transfers between devices  3.08 us (15%)
    ppermute x2, starting transfers between devices, local(): lax.ppermute(held, 'sub', [(k, k ^ step) for k in range(subs)])  6.06 us
    ppermute x8, starting transfers between devices, swap(): return lax.ppermute(x, 'facet', [(i, i ^ step) for i in range(facets)])  5.38 us
    ppermute x8, waiting for transfers between devices, swap(): return lax.ppermute(x, 'facet', [(i, i ^ step) for i in range(facets)])  2.83 us
    pallas_call x1, Pallas kernels, local(): pl.pallas_call(functools.partial(backward_kernel, others, size), out_shap...  1.85 us
    pallas_call x1, Pallas kernels, local(): pl.pallas_call(functools.partial(prepare_kernel, facets, subs, length), o...  1.63 us
    pallas_call x1, Pallas kernels, local(): pl.pallas_call(forward_kernel, out_shape=[shaped((count * rows, LANES), B...  1.34 us
  transfers between devices with their start and end apart: 10, of which 5 were waited for; matrix products, arithmetic and copies ran while one was open for 0% of the time, Pallas kernels for 17%

profile of v4, /device:TPU:0, one launch (start us, length us, event | category | flops | bytes accessed | tf_op | source)
XLA Modules:
  0.0 20.0 jit_solution(7296599232504184163)
XLA Ops:
  0.0 0.0 copy-start
  0.0 0.0 copy-start.2
  0.0 3.0 %collective-permute-start.1 = (f32[4,512]{1,0:T(4,128)}, f32[4,512]{1,0:T(4,128)S(1)}, u32[]{:S(2)}, u32[]{:S(2)}) collective-permute-start(f32[4,512]{1,0:T(4,128)} %first_ref.1), channel_id=1, source_target_pairs={{0,1},{1,0},{2,3},{3,2},{4,5},{5,4},{6,7},{7,6},{8,9},{9,8},{10,11... | collective-permute-start | bytes 24584 | tf_op jit(solution)/shard_map/ppermute | solution.py:405
  3.0 0.1 shard_map.73
  3.2 0.0 copy-done
  3.2 0.0 copy-start.1
  3.2 1.3 %shard_map.74 = (bf16[256,128]{1,0:T(8,128)(2,1)S(1)}, bf16[256,512]{1,0:T(8,128)(2,1)S(1)}) custom-call(s32[32]{0:T(128)} %sub_hbm.3, s32[8]{0:T(128)} %off_hbm.3, bf16[1,8,8192]{2,1,0:T(8,128)(2,1)S(1)} %copy-done, f32[256,128]{1,0:T(8,128)S(1)} %get-tuple-element.26.turn_ref.refs_12_, bf16[64,128]{1,0:T(8,128)(2,1)S(1)} %get-tuple-element.27.fwd_ref), custom_call_target="tpu_custom_call" | custom-call | tf_op jit(solution)/shard_map/pallas_call | solution.py:407
  4.5 0.1 collective-permute-start
  4.6 0.2 %collective-permute-done.1.second_ref = f32[4,512]{1,0:T(4,128)S(1)} collective-permute-done((f32[4,512]{1,0:T(4,128)}, f32[4,512]{1,0:T(4,128)S(1)}, u32[]{:S(2)}, u32[]{:S(2)}) %collective-permute-start.1) | collective-permute-done | bytes 8224 | tf_op jit(solution)/shard_map/ppermute | solution.py:405
  4.9 0.0 copy-done.1
  4.9 3.0 %collective-permute-start.2 = (f32[8,512]{1,0:T(8,128)S(1)}, f32[8,512]{1,0:T(8,128)S(1)}, u32[]{:S(2)}, u32[]{:S(2)}) collective-permute-start(f32[8,512]{1,0:T(8,128)S(1)} %shard_map.75.after_ref.refs_3_), channel_id=1, source_target_pairs={{0,2},{1,3},{2,0},{3,1},{4,6},{5,7},{6,4},{7,5},{8,10},{9,11},{10,... | collective-permute-start | bytes 49160 | tf_op jit(solution)/shard_map/ppermute | solution.py:405
  7.9 0.0 copy-done.2
  7.9 1.6 %shard_map.76 = (f32[256,128]{1,0:T(8,128)S(1)}, f32[256,128]{1,0:T(8,128)S(1)}, s32[256,128]{1,0:T(8,128)S(1)}, bf16[512,128]{1,0:T(8,128)(2,1)S(1)}, bf16[128,...) custom-call(s32[32]{0:T(128)} %sub_hbm.3, s32[8]{0:T(128)} %off_hbm.3, ...), custom_call_target="tpu_custom_call" | custom-call | flops 20000000000 | bytes 1048576 | tf_op jit(solution)/shard_map/pallas_call | solution.py:435
  9.5 0.0 collective-permute-done.passed_ref
  9.6 0.2 %shard_map.77 = (f32[256,128]{1,0:T(8,128)S(1)}, bf16[256,128]{1,0:T(8,128)(2,1)S(1)}, bf16[256,128]{1,0:T(8,128)(2,1)S(1)}, bf16[256,128]{1,0:T(8,128)(2,1)S(1)}) custom-call(bf16[256,128]{1,0:T(8,128)(2,1)S(1)} %get-tuple-element.28.windows_ref, bf16[256,128]{1,0:T(8,128)(2,1)S(1)} %collective-permute-done.passed_ref, ...), custom_call_target="tpu_custom_call" | custom-call | tf_op jit(solution)/shard_map/pallas_call | solution.py:464
  9.8 0.0 collective-permute-done.2.refs_4_
  9.8 2.7 %collective-permute-start.5 = (bf16[320,128]{1,0:T(8,128)(2,1)S(1)}, bf16[320,128]{1,0:T(8,128)(2,1)S(1)}, u32[]{:S(2)}, u32[]{:S(2)}) collective-permute-start(bf16[320,128]{1,0:T(8,128)(2,1)S(1)} %get-tuple-element.39), channel_id=1, source_target_pairs={{0,24},{4,28},{8,16},{12,20},{16,8},{20,12},{24,0},{28,4},{1,25},{... | collective-permute-start | bytes 245768 | tf_op jit(solution)/shard_map/ppermute | solution.py:390
  12.5 0.5 %collective-permute-start.4 = (bf16[320,128]{1,0:T(8,128)(2,1)S(1)}, bf16[320,128]{1,0:T(8,128)(2,1)S(1)}, u32[]{:S(2)}, u32[]{:S(2)}) collective-permute-start(bf16[320,128]{1,0:T(8,128)(2,1)S(1)} %get-tuple-element.38), channel_id=1, source_target_pairs={{0,16},{4,20},{8,24},{12,28},{16,0},{20,4},{24,8},{28,12},{1,17},{... | collective-permute-start | bytes 245768 | tf_op jit(solution)/shard_map/ppermute | solution.py:390
  13.0 0.4 %collective-permute-start.3 = (bf16[320,128]{1,0:T(8,128)(2,1)S(1)}, bf16[320,128]{1,0:T(8,128)(2,1)S(1)}, u32[]{:S(2)}, u32[]{:S(2)}) collective-permute-start(bf16[320,128]{1,0:T(8,128)(2,1)S(1)} %get-tuple-element.37), channel_id=1, source_target_pairs={{0,8},{4,12},{8,0},{12,4},{16,24},{20,28},{24,16},{28,20},{1,9},{5... | collective-permute-start | bytes 245768 | tf_op jit(solution)/shard_map/ppermute | solution.py:390
  13.4 0.0 collective-permute-start.8
  13.4 1.7 %collective-permute-start.9 = (bf16[64,128]{1,0:T(8,128)(2,1)S(1)}, bf16[64,128]{1,0:T(8,128)(2,1)S(1)}, u32[]{:S(2)}, u32[]{:S(2)}) collective-permute-start(bf16[64,128]{1,0:T(8,128)(2,1)S(1)} %get-tuple-element.41.own_rows_ref), channel_id=1, source_target_pairs={{0,4},{4,0},{8,12},{12,8},{16,20},{20,16},{24,28},{28,24},{1,5},{5... | collective-permute-start | bytes 49160 | tf_op jit(solution)/shard_map/ppermute | solution.py:390
  15.1 0.2 %collective-permute-done.5.refs_2_.block_ref.refs_0_ = bf16[320,128]{1,0:T(8,128)(2,1)S(1)} collective-permute-done((bf16[320,128]{1,0:T(8,128)(2,1)S(1)}, bf16[320,128]{1,0:T(8,128)(2,1)S(1)}, u32[]{:S(2)}, u32[]{:S(2)}) %collective-permute-start.5) | collective-permute-done | bytes 81952 | tf_op jit(solution)/shard_map/ppermute | solution.py:390
  15.4 0.0 collective-permute-start.6
  15.4 1.6 %collective-permute-done.4.refs_1_.block_ref = bf16[320,128]{1,0:T(8,128)(2,1)S(1)} collective-permute-done((bf16[320,128]{1,0:T(8,128)(2,1)S(1)}, bf16[320,128]{1,0:T(8,128)(2,1)S(1)}, u32[]{:S(2)}, u32[]{:S(2)}) %collective-permute-start.4) | collective-permute-done | bytes 81952 | tf_op jit(solution)/shard_map/ppermute | solution.py:390
  16.9 0.0 collective-permute-start.7
  16.9 0.5 %collective-permute-done.3.refs_0_.refs_2_ = bf16[320,128]{1,0:T(8,128)(2,1)S(1)} collective-permute-done((bf16[320,128]{1,0:T(8,128)(2,1)S(1)}, bf16[320,128]{1,0:T(8,128)(2,1)S(1)}, u32[]{:S(2)}, u32[]{:S(2)}) %collective-permute-start.3) | collective-permute-done | bytes 81952 | tf_op jit(solution)/shard_map/ppermute | solution.py:390
  17.4 0.1 shard_map.79.product_ref
  17.6 0.0 collective-permute-done.8.refs_5_
  17.6 0.0 collective-permute-done.9.refs_6_
  17.6 0.0 collective-permute-done.6.refs_3_
  17.6 0.5 %collective-permute-done.7.refs_4_ = bf16[64,128]{1,0:T(8,128)(2,1)S(1)} collective-permute-done((bf16[64,128]{1,0:T(8,128)(2,1)S(1)}, bf16[64,128]{1,0:T(8,128)(2,1)S(1)}, u32[]{:S(2)}, u32[]{:S(2)}) %collective-permute-start.7) | collective-permute-done | bytes 16416 | tf_op jit(solution)/shard_map/ppermute | solution.py:390
  18.1 1.8 %shard_map.82 = f32[1,8,8192]{2,1,0:T(8,128)} custom-call(f32[256,128]{1,0:T(8,128)S(1)} %shard_map.79.product_ref, bf16[64,128]{1,0:T(8,128)(2,1)S(1)} %get-tuple-element.41.own_rows_ref, bf16[320,128]{1,0:T(8,128)(2,1)S(1)} %collective-permute-done.5.refs_2_.block_ref.refs_0_, bf16[320,128]{1,0:T(8,128)(2,1)S(1)} %collective-permute-done.4.refs_1_.block_ref, ...), custom_call_target="tpu_custom_call" | custom-call | tf_op jit(solution)/shard_map/pallas_call | solution.py:501
  (4 shorter events, 0.0 us)
Async XLA Ops:
  0.0 3.2 %copy-start = (bf16[1,8,8192]{2,1,0:T(8,128)(2,1)S(1)}, bf16[1,8,8192]{2,1,0:T(8,128)(2,1)}, u32[]{:S(2)}) copy-start(bf16[1,8,8192]{2,1,0:T(8,128)(2,1)} %strips_ref.1) | copy-start | bytes 393220
  0.0 7.9 %copy-start.2 = (bf16[16,32,1024]{2,1,0:T(8,128)(2,1)S(1)}, bf16[16,32,1024]{2,1,0:T(8,128)(2,1)}, u32[]{:S(2)}) copy-start(bf16[16,32,1024]{2,1,0:T(8,128)(2,1)} %screens_ref.1) | copy-start | bytes 3145732
  0.0 4.9 %collective-permute-start.1 = (f32[4,512]{1,0:T(4,128)}, f32[4,512]{1,0:T(4,128)S(1)}, u32[]{:S(2)}, u32[]{:S(2)}) collective-permute-start(f32[4,512]{1,0:T(4,128)} %first_ref.1), channel_id=1, source_target_pairs={{0,1},{1,0},{2,3},{3,2},{4,5},{5,4},{6,7},{7,6},{8,9},{9,8},{10,11... | collective-permute-start | bytes 24584 | tf_op jit(solution)/shard_map/ppermute | solution.py:405
  3.2 1.7 %copy-start.1 = (f32[4,512]{1,0:T(4,128)S(1)}, f32[4,512]{1,0:T(4,128)}, u32[]{:S(2)}) copy-start(f32[4,512]{1,0:T(4,128)} %first_ref.1) | copy-start | bytes 24580
  4.5 5.0 %collective-permute-start = (bf16[256,128]{1,0:T(8,128)(2,1)S(1)}, bf16[256,128]{1,0:T(8,128)(2,1)S(1)}, u32[]{:S(2)}, u32[]{:S(2)}) collective-permute-start(bf16[256,128]{1,0:T(8,128)(2,1)S(1)} %get-tuple-element.28.windows_ref), channel_id=1, source_target_pairs={{0,4},{4,0},{8,12},{12,8},{16,20},{20,16},{24,28},{28,24},{1,5},{5... | collective-permute-start | bytes 196616 | tf_op jit(solution)/shard_map/ppermute | solution.py:390
  4.9 4.9 %collective-permute-start.2 = (f32[8,512]{1,0:T(8,128)S(1)}, f32[8,512]{1,0:T(8,128)S(1)}, u32[]{:S(2)}, u32[]{:S(2)}) collective-permute-start(f32[8,512]{1,0:T(8,128)S(1)} %shard_map.75.after_ref.refs_3_), channel_id=1, source_target_pairs={{0,2},{1,3},{2,0},{3,1},{4,6},{5,7},{6,4},{7,5},{8,10},{9,11},{10,... | collective-permute-start | bytes 49160 | tf_op jit(solution)/shard_map/ppermute | solution.py:405
  9.8 5.5 %collective-permute-start.5 = (bf16[320,128]{1,0:T(8,128)(2,1)S(1)}, bf16[320,128]{1,0:T(8,128)(2,1)S(1)}, u32[]{:S(2)}, u32[]{:S(2)}) collective-permute-start(bf16[320,128]{1,0:T(8,128)(2,1)S(1)} %get-tuple-element.39), channel_id=1, source_target_pairs={{0,24},{4,28},{8,16},{12,20},{16,8},{20,12},{24,0},{28,4},{1,25},{... | collective-permute-start | bytes 245768 | tf_op jit(solution)/shard_map/ppermute | solution.py:390
  12.5 4.4 %collective-permute-start.4 = (bf16[320,128]{1,0:T(8,128)(2,1)S(1)}, bf16[320,128]{1,0:T(8,128)(2,1)S(1)}, u32[]{:S(2)}, u32[]{:S(2)}) collective-permute-start(bf16[320,128]{1,0:T(8,128)(2,1)S(1)} %get-tuple-element.38), channel_id=1, source_target_pairs={{0,16},{4,20},{8,24},{12,28},{16,0},{20,4},{24,8},{28,12},{1,17},{... | collective-permute-start | bytes 245768 | tf_op jit(solution)/shard_map/ppermute | solution.py:390
  13.0 4.4 %collective-permute-start.3 = (bf16[320,128]{1,0:T(8,128)(2,1)S(1)}, bf16[320,128]{1,0:T(8,128)(2,1)S(1)}, u32[]{:S(2)}, u32[]{:S(2)}) collective-permute-start(bf16[320,128]{1,0:T(8,128)(2,1)S(1)} %get-tuple-element.37), channel_id=1, source_target_pairs={{0,8},{4,12},{8,0},{12,4},{16,24},{20,28},{24,16},{28,20},{1,9},{5... | collective-permute-start | bytes 245768 | tf_op jit(solution)/shard_map/ppermute | solution.py:390
  13.4 4.2 %collective-permute-start.8 = (bf16[64,128]{1,0:T(8,128)(2,1)S(1)}, bf16[64,128]{1,0:T(8,128)(2,1)S(1)}, u32[]{:S(2)}, u32[]{:S(2)}) collective-permute-start(bf16[64,128]{1,0:T(8,128)(2,1)S(1)} %get-tuple-element.41.own_rows_ref), channel_id=1, source_target_pairs={{0,12},{4,8},{8,4},{12,0},{16,28},{20,24},{24,20},{28,16},{1,13},{... | collective-permute-start | bytes 49160 | tf_op jit(solution)/shard_map/ppermute | solution.py:390
  13.4 4.2 %collective-permute-start.9 = (bf16[64,128]{1,0:T(8,128)(2,1)S(1)}, bf16[64,128]{1,0:T(8,128)(2,1)S(1)}, u32[]{:S(2)}, u32[]{:S(2)}) collective-permute-start(bf16[64,128]{1,0:T(8,128)(2,1)S(1)} %get-tuple-element.41.own_rows_ref), channel_id=1, source_target_pairs={{0,4},{4,0},{8,12},{12,8},{16,20},{20,16},{24,28},{28,24},{1,5},{5... | collective-permute-start | bytes 49160 | tf_op jit(solution)/shard_map/ppermute | solution.py:390
  15.4 2.2 %collective-permute-start.6 = (bf16[64,128]{1,0:T(8,128)(2,1)S(1)}, bf16[64,128]{1,0:T(8,128)(2,1)S(1)}, u32[]{:S(2)}, u32[]{:S(2)}) collective-permute-start(bf16[64,128]{1,0:T(8,128)(2,1)S(1)} %shard_map.80), channel_id=1, source_target_pairs={{0,4},{4,0},{8,12},{12,8},{16,20},{20,16},{24,28},{28,24},{1,5},{5... | collective-permute-start | bytes 49160 | tf_op jit(solution)/shard_map/ppermute | solution.py:390
  16.9 1.2 %collective-permute-start.7 = (bf16[64,128]{1,0:T(8,128)(2,1)S(1)}, bf16[64,128]{1,0:T(8,128)(2,1)S(1)}, u32[]{:S(2)}, u32[]{:S(2)}) collective-permute-start(bf16[64,128]{1,0:T(8,128)(2,1)S(1)} %shard_map.81), channel_id=1, source_target_pairs={{0,4},{4,0},{8,12},{12,8},{16,20},{20,16},{24,28},{28,24},{1,5},{5... | collective-permute-start | bytes 49160 | tf_op jit(solution)/shard_map/ppermute | solution.py:390

commit v5 on v4

--- a/solution.py
+++ b/solution.py
@@ -117,7 +117,7 @@
     shift_ref,
     in_scr,
     mid_scr,
-    out_scr,
+    low_scr,
     sub_ref,
     off_ref,
     sems,
@@ -143,8 +143,10 @@
             cos = turn_ref[q * chunks : (q + 1) * chunks, :]
             sin = turn_ref[LANES + q * chunks : LANES + (q + 1) * chunks, :]
             at = r * LANES + q * chunks
-            mid_scr[at : at + chunks, :LANES] = (re * cos + im * sin).astype(BF)
-            mid_scr[at : at + chunks, LANES:] = (im * cos - re * sin).astype(BF)
+            for lanes, value in ((slice(0, LANES), re * cos + im * sin), (slice(LANES, 2 * LANES), im * cos - re * sin)):
+                high = value.astype(BF)
+                mid_scr[at : at + chunks, lanes] = high
+                low_scr[at : at + chunks, lanes] = (value - high.astype(F32)).astype(BF)
 
     for copy in copies:
         copy.wait()
@@ -158,8 +160,8 @@
             rows_here = slice(core * LANES, (core + 1) * LANES)
             shift_ref[rows_here, n * LANES : (n + 1) * LANES] = jnp.where(apart == delta, 1.0, 0.0).astype(BF)
 
-    starts = [start_of(mine, sub_ref, off_ref, j, length) for j in range(count)]
-    block = column([s // M for s in starts], LANES)
+    starts = column([start_of(mine, sub_ref, off_ref, j, length) for j in range(count)], LANES)
+    block = starts >> (M.bit_length() - 1)
     cos, sin = circle(block * iota((count, LANES), 1), length // M)
     scale = 1 / math.sqrt(length)
     cos, sin = cos * scale, sin * scale
@@ -168,58 +170,54 @@
     )
     coarse = jnp.concatenate([high_low(coarse, False), high_low(coarse, True)], axis=0)
     window = dot_t(coarse, mid_scr[...])
-    window = window[: 2 * count] + window[2 * count :]
+    window = window[: 2 * count] + window[2 * count :] + dot_t(coarse[: 2 * count], low_scr[...])
+    lane = iota((count, LANES), 1)
+    taken = (lane + (starts & (M - 1))) & (LANES - 1)
     for r in range(rows):
-        out_scr[pl.ds(r, 2 * count, stride=rows), :] = window[:, r * LANES : (r + 1) * LANES]
-    lane = iota((rows, LANES), 1)
-
-    def emit(j):
-        shift = starts[j] & (M - 1)
-        re = out_scr[j * rows : (j + 1) * rows, :]
-        im = out_scr[(count + j) * rows : (count + j + 1) * rows, :]
-        re = pltpu.roll(re, (LANES - shift) & (LANES - 1), 1)
-        im = pltpu.roll(im, M - shift, 1)
-        return jnp.where(lane < M, re, im)
-
-    for j in range(0, count, 2):
-        out_ref[j * rows : (j + 2) * rows, :] = jnp.concatenate([emit(j), emit(j + 1)], axis=0).astype(BF)
+        re = window[:count, r * LANES : (r + 1) * LANES]
+        im = window[count:, r * LANES : (r + 1) * LANES]
+        re = jnp.take_along_axis(re, taken, axis=1)
+        im = jnp.take_along_axis(im, taken ^ M, axis=1)
+        out_ref[r * count : (r + 1) * count, :] = jnp.where(lane < M, re, im).astype(BF)
 
 
 def prepare_kernel(
-    facets,
     subs,
     length,
     sub_hbm,
     off_hbm,
+    kind_hbm,
     owner_hbm,
-    kind_hbm,
     after_ref,
     screens_ref,
     cos_ref,
     sin_ref,
+    both_ref,
+    other_ref,
+    rank_ref,
     gather_ref,
-    both_ref,
-    rank_ref,
     coarse_ref,
     inv_ref,
-    seen,
     cos_scr,
     sin_scr,
     sub_ref,
     off_ref,
+    kind_ref,
     owner_ref,
-    kind_ref,
     sems,
 ):
-    copies = scalars(
-        [(sub_hbm, sub_ref), (off_hbm, off_ref), (owner_hbm, owner_ref), (kind_hbm, kind_ref)], sems
-    )
-    count = sub_ref.shape[0]
+    pairs = [(sub_hbm, sub_ref), (off_hbm, off_ref), (kind_hbm, kind_ref), (owner_hbm, owner_ref)]
+    copies = scalars(pairs, sems)
+    chunks = length // LANES
+    mine = lax.axis_index("facet")
+    count = kind_ref.shape[0]
     rows = cos_ref.shape[0] // count
     span = screens_ref.shape[2] // 2
-    chunks = length // LANES
-    mine = lax.axis_index("facet")
     my_sub = lax.axis_index("sub")
+    shape = (span, LANES)
+    lane = iota(shape, 1)
+    apart = iota(shape, 0) - lane % M
+    sign = jnp.where(lane < M, -1.0, 1.0)
 
     shape = (chunks, LANES)
     cos, sin = circle(iota(shape, 0) * iota(shape, 1), chunks)
@@ -231,14 +229,9 @@
 
     for copy in copies:
         copy.wait()
-    my_off = off_ref[mine]
-
-    shape = (span, LANES)
-    row = iota(shape, 0)
-    lane = iota(shape, 1)
-    hit = row == my_off + lane % M
+    hit = apart == off_ref[mine]
     both = jnp.where(hit, 1.0, 0.0).astype(BF)
-    signed = jnp.where(hit, jnp.where(lane < M, -1.0, 1.0), 0.0).astype(BF)
+    signed = jnp.where(hit, sign, 0.0).astype(BF)
     kinds = screens_ref.shape[0]
     tall = cos_scr.shape[0] // kinds
     first = my_sub * rows // tall * tall
@@ -246,43 +239,45 @@
     cosines = screens_ref[:, block, :span].reshape(kinds * tall, span)
     sines = screens_ref[:, block, span:].reshape(kinds * tall, span)
     both_ref[...] = both
+    other_ref[...] = jnp.where(apart == off_ref[mine ^ 1], 1.0, 0.0).astype(BF)
     cos_scr[...] = dot(cosines, both)
     sin_scr[...] = dot(sines, signed)
     for j in range(count):
         kind = pl.multiple_of(kind_ref[j] * tall + my_sub * rows - first, rows)
-        cos_ref[j * rows : (j + 1) * rows, :] = cos_scr[pl.ds(kind, rows), :]
-        sin_ref[j * rows : (j + 1) * rows, :] = sin_scr[pl.ds(kind, rows), :]
-
-    for o in range(facets * subs):
-        seen[o] = 0
-    held = subs * CAP
-    pieces = span // LANES
-    places = []
-    for j in range(count):
-        who = owner_ref[j]
-        slot = seen[who]
-        seen[who] = slot + 1
-        facet_step = (who // subs) ^ mine
-        sub_step = (who % subs) ^ my_sub
-        block = facet_step % 2 * (facets // 2) + facet_step // 2
-        places.append(block * held * pieces + sub_step * CAP + slot)
-    width = rank_ref.shape[1]
-    place = column(places, width)
-    lane = iota((count, width), 1)
-    for c in range(pieces):
-        hit = jnp.where(lane == place + c * held, 1.0, 0.0)
-        rank_ref[c * count : (c + 1) * count, :] = hit.astype(BF)
-
-    lane = iota((rows, LANES), 1)
-    for j in range(count):
-        shift = start_of(mine, sub_ref, off_ref, j, length) & (M - 1)
-        gather_ref[j * rows : (j + 1) * rows, :] = (lane - shift) & (LANES - 1)
+        cos_ref[pl.ds(j, rows, stride=count), :] = cos_scr[pl.ds(kind, rows), :]
+        sin_ref[pl.ds(j, rows, stride=count), :] = sin_scr[pl.ds(kind, rows), :]
+
+    owners = [owner_ref[j] for j in range(count)]
+    lane = iota((8, LANES), 1)
+    wide = []
+    for first in range(0, count, LANES):
+        value = jnp.full((8, LANES), -1, jnp.int32)
+        for j in range(first, min(first + LANES, count)):
+            value = jnp.where(lane == j - first, owners[j], value)
+        wide.append(value)
+    tall_owner = column(owners, LANES)
+    slot = jnp.zeros((count, 1), F32)
+    for n, value in enumerate(wide):
+        same = jnp.concatenate([value] * (count // 8), axis=0) == tall_owner
+        earlier = iota((count, LANES), 1) + n * LANES < iota((count, LANES), 0)
+        slot = slot + jnp.sum(jnp.where(same & earlier, 1.0, 0.0), axis=1, keepdims=True)
+    bits = subs.bit_length() - 1
+    facet_step = (tall_owner >> bits) ^ mine
+    sub_step = (tall_owner & (subs - 1)) ^ my_sub
+    facets = off_ref.shape[0]
+    block = (facet_step & 1) * (facets // 2) + (facet_step >> 1)
+    place = (block * subs + sub_step) * CAP + slot.astype(jnp.int32)
+    for at in range(0, rank_ref.shape[1], LANES):
+        hit = iota((count, LANES), 1) + at == place
+        rank_ref[:, at : at + LANES] = jnp.where(hit, 1.0, 0.0).astype(BF)
+
+    starts = [start_of(mine, sub_ref, off_ref, j, length) for j in range(count)]
+    gather_ref[...] = (iota((count, LANES), 1) - (column(starts, LANES) & (M - 1))) & (LANES - 1)
 
     lane = iota((8, 4 * count), 1)
     block = jnp.zeros((8, 4 * count), jnp.int32)
     for j in range(count):
-        start = start_of(mine, sub_ref, off_ref, j, length) // M
-        block = jnp.where(lane % count == j, start, block)
+        block = jnp.where(lane % count == j, starts[j] // M, block)
     block = jnp.concatenate([block] * (M // 8), axis=0)
     shape = (M, 4 * count)
     lane = iota(shape, 1)
@@ -295,12 +290,22 @@
     coarse_ref[M:, :] = high_low(jnp.where(lane_im, cos, sin), low)
 
 
-def tail_kernel(block_ref, out_ref):
-    out_ref[...] = block_ref[block_ref.shape[0] - out_ref.shape[0] :, :]
-
-
-def screen_kernel(own_ref, *refs):
-    arrived, (cos_ref, sin_ref, out_ref) = refs[:-3], refs[-3:]
+def cut(blocks, chunks, hits):
+    rows = []
+    for block in blocks:
+        size = block.shape[0] // chunks
+        rows.append(jnp.concatenate([block[c * size : (c + 1) * size] for c in range(chunks)], axis=1))
+    return dot(jnp.concatenate(rows, axis=0), hits).astype(BF)
+
+
+def tail_kernel(size, block_ref, hits_ref, out_ref):
+    chunks = hits_ref.shape[0] // LANES
+    out_ref[...] = cut([block_ref[block_ref.shape[0] - size :, :]], chunks, hits_ref[...])
+
+
+def screen_kernel(size, own_ref, *refs):
+    cos_ref, sin_ref, hits_ref, out_ref, cut_ref = refs[-5:]
+    arrived, others = refs[:-8], refs[-8:-5]
     windows = own_ref.shape[0]
     for at in range(0, windows, 16):
         pair = slice(at, at + 16)
@@ -308,39 +313,32 @@
         for ref in arrived:
             total = total + ref[pair, :].astype(F32)
         out_ref[pair, :] = total * cos_ref[pair, :] + pltpu.roll(total, M, 1) * sin_ref[pair, :]
-
-
-def backward_kernel(others, size, product_ref, own_rows_ref, *refs):
-    arrived, across, refs = refs[:others][::-1], refs[others : 2 * others + 1][::-1], refs[2 * others + 1 :]
-    gather_ref, both_ref, rank_ref, coarse_ref, inv_ref, turn_ref, out_hbm = refs[:7]
-    re_scr, im_scr, out_scr, flat_scr, out_sems = refs[7:]
+    held = [others[0][...]] + [ref[windows:, :] for ref in arrived] + [ref[...] for ref in others[1:]]
+    cut_ref[...] = cut(held, hits_ref.shape[0] // LANES, hits_ref[...])
+
+
+def backward_kernel(product_ref, *refs):
+    cuts, refs = refs[:-9][::-1], refs[-9:]
+    rank_ref, gather_ref, coarse_ref, inv_ref, turn_ref, out_hbm, out_scr, flat_scr, out_sems = refs
     rows = out_hbm.shape[1]
     length = out_hbm.shape[2] // 2
     chunks = length // LANES
     windows = product_ref.shape[0]
     count = windows // rows
 
-    held = [own_rows_ref[...]] + [ref[windows:, :] for ref in arrived] + [ref[...] for ref in across]
-    ranked = dot(rank_ref[...], jnp.concatenate(held, axis=0)).astype(BF)
-    ranked = jnp.concatenate([ranked[c : c + count] for c in range(0, ranked.shape[0], count)], axis=1)
-    weights = dot(ranked, both_ref[...])
-
-    for j in range(count):
-        value = product_ref[j * rows : (j + 1) * rows, :] * weights[j : j + 1, :]
+    weights = dot(rank_ref[...], jnp.concatenate([ref[...] for ref in cuts], axis=0))
+
+    place = gather_ref[...]
+    inside = place < M
+    blocks = []
+    for r in range(rows):
+        value = product_ref[r * count : (r + 1) * count, :] * weights
         value = value.astype(BF).astype(F32)
-        place = gather_ref[j * rows : (j + 1) * rows, :]
-        re = jnp.take_along_axis(value, place, axis=1)
-        im = jnp.take_along_axis(value, place ^ M, axis=1)
-        re_scr[pl.ds(j, rows, stride=count), :] = jnp.where(place < M, re, 0.0)
-        im_scr[pl.ds(j, rows, stride=count), :] = jnp.where(place < M, im, 0.0)
-
-    halves = []
-    for scr in (re_scr, im_scr):
-        halves.append(
-            jnp.concatenate([scr[r * count : (r + 1) * count, :].astype(BF) for r in range(rows)], axis=1)
-        )
-    spread = jnp.concatenate(halves + halves, axis=0)
-    inner = dot(coarse_ref[...], spread)
+        re = jnp.where(inside, jnp.take_along_axis(value, place, axis=1), 0.0)
+        im = jnp.where(inside, jnp.take_along_axis(value, place ^ M, axis=1), 0.0)
+        blocks.append(jnp.concatenate([re, im], axis=0).astype(BF))
+    spread = jnp.concatenate(blocks, axis=1)
+    inner = dot(coarse_ref[...], jnp.concatenate([spread, spread], axis=0))
     twisted = []
     for r in range(rows):
         re = inner[:M, r * LANES : (r + 1) * LANES]
@@ -400,10 +398,10 @@
         cost_estimate=cost(10**11),
     )()
     held = grid_weight
-    step = 1
-    while step < subs:
+    steps = [1 << n for n in range(subs.bit_length() - 1)]
+    for step in steps:
         last, beside = held, lax.ppermute(held, "sub", [(k, k ^ step) for k in range(subs)])
-        if step == 1:
+        if step == steps[0]:
             windows, shift = pl.pallas_call(
                 forward_kernel,
                 out_shape=[shaped((count * rows, LANES), BF), shaped((2 * LANES, facets // 2 * LANES), BF)],
@@ -412,7 +410,7 @@
                 scratch_shapes=[
                     pltpu.VMEM((rows * 2 * chunks, LANES), F32),
                     pltpu.VMEM((rows * LANES, 2 * LANES), BF),
-                    pltpu.VMEM((2 * count * rows, LANES), F32),
+                    pltpu.VMEM((rows * LANES, 2 * LANES), BF),
                     pltpu.SMEM((count,), jnp.int32),
                     pltpu.SMEM((facets,), jnp.int32),
                     pltpu.SemaphoreType.DMA((2,)),
@@ -420,7 +418,7 @@
                 compiler_params=limit,
             )(subgrid_offset, facet_offset, strips, turn, fwd)
             passed = swap(windows, 1)
-        if step < subs // 2:
+        if step != steps[-1]:
             beside = pl.pallas_call(
                 join_kernel,
                 out_shape=shaped((2 * held.shape[0], span), F32),
@@ -428,25 +426,24 @@
                 out_specs=vmem,
                 compiler_params=limit,
             )(held, beside)
-        step *= 2
         held, _ = lax.optimization_barrier((beside, windows))
 
     tall = max(rows, 16)
-    prepared = pl.pallas_call(
-        functools.partial(prepare_kernel, facets, subs, length),
+    cos, sin, both, other, *ready = pl.pallas_call(
+        functools.partial(prepare_kernel, subs, length),
         out_shape=[
             shaped((count * rows, LANES), F32),
             shaped((count * rows, LANES), F32),
-            shaped((count * rows, LANES), jnp.int32),
             shaped((span, LANES), BF),
-            shaped((span // LANES * count, facets * subs * grid_weight.size // LANES), BF),
+            shaped((span, LANES), BF),
+            shaped((count, facets * subs * CAP), BF),
+            shaped((count, LANES), jnp.int32),
             shaped((2 * M, 4 * count), BF),
             shaped((4 * chunks, 2 * LANES), BF),
         ],
         in_specs=[hbm] * 5 + [vmem],
-        out_specs=[vmem] * 7,
+        out_specs=[vmem] * 8,
         scratch_shapes=[
-            pltpu.SMEM((facets * subs,), jnp.int32),
             pltpu.VMEM((kinds * tall, LANES), F32),
             pltpu.VMEM((kinds * tall, LANES), F32),
             pltpu.SMEM((count,), jnp.int32),
@@ -456,11 +453,11 @@
             pltpu.SemaphoreType.DMA((4,)),
         ],
         compiler_params=limit,
-        cost_estimate=cost(2*10**10),
-    )(subgrid_offset, facet_offset, owner, screen_index, last, screens)
+        cost_estimate=cost(2 * 10**10),
+    )(subgrid_offset, facet_offset, screen_index, owner, last, screens)
 
     others = facets // 2 - 1
-    shift, _ = lax.optimization_barrier((shift, prepared[0]))
+    shift, _ = lax.optimization_barrier((shift, both))
     own, *merged = pl.pallas_call(
         merge_kernel,
         out_shape=[shaped(windows.shape, F32)] + [shaped(windows.shape, BF)] * others,
@@ -479,39 +476,37 @@
 
     arrived = [swap(payload, 2 * n + 2) for n, payload in enumerate(payloads)]
     across = [swap(own_rows, 1), swap(own_rows, 3)]
+    late = []
     for block in arrived[1:]:
         tail = pl.pallas_call(
-            tail_kernel,
-            out_shape=shaped((size, LANES), BF),
-            in_specs=[vmem],
+            functools.partial(tail_kernel, size),
+            out_shape=shaped((subs * CAP, LANES), BF),
+            in_specs=[vmem] * 2,
             out_specs=vmem,
             compiler_params=limit,
-        )(block)
-        across.append(swap(tail, 1))
-
-    cos, sin, *prepared = prepared
-    product = pl.pallas_call(
-        screen_kernel,
-        out_shape=shaped(windows.shape, F32),
-        in_specs=[vmem] * (others + 3),
-        out_specs=vmem,
+        )(block, other)
+        late.append(swap(tail, 1))
+
+    product, early = pl.pallas_call(
+        functools.partial(screen_kernel, size),
+        out_shape=[shaped(windows.shape, F32), shaped(((others + 3) * subs * CAP, LANES), BF)],
+        in_specs=[vmem] * (others + 7),
+        out_specs=[vmem] * 2,
         compiler_params=limit,
-    )(own, *arrived, cos, sin)
+    )(own, *arrived, own_rows, *across, cos, sin, both)
 
     return pl.pallas_call(
-        functools.partial(backward_kernel, others, size),
+        backward_kernel,
         out_shape=shaped((1, rows, 2 * length), F32),
-        in_specs=[vmem] * (2 * others + 9),
+        in_specs=[vmem] * (len(late) + 7),
         out_specs=hbm,
         scratch_shapes=[
-            pltpu.VMEM((rows * count, LANES), F32),
-            pltpu.VMEM((rows * count, LANES), F32),
             pltpu.VMEM((2 * chunks * rows, LANES), F32),
             pltpu.VMEM((rows, 2 * length), F32),
             pltpu.SemaphoreType.DMA((4,)),
         ],
         compiler_params=limit,
-    )(product, own_rows, *arrived[::-1], *across[::-1], *prepared, turn)
+    )(product, *late[::-1], early, *ready, turn)
 
 
 def solution(mesh):

time: 20.1 us -> 19.9 us (0.990)
  Pallas kernels: 5.32 us -> 4.99 us
    pallas_call x5, Pallas kernels: 3.58 us -> 3.18 us  [the longest x1 1.51 us: local(): pl.pallas_call(backward_kernel, out_shape=shaped((1, rows, 2 * length), F...]
    ppermute x8, waiting for transfers between devices: 2.83 us -> 2.6 us  [swap(): return lax.ppermute(x, 'facet', [(i, i ^ step) for i in range(facets)])]
  transfers between devices with their start and end apart: 10 -> 10, of which waited for: 5 -> 5; matrix products, arithmetic and copies ran while one was open for 0% -> 0% of each run, Pallas kernels for 17% -> 18%
where the time goes in v5:
time: 19.9 us; the launch traced here: 19.7 us
  starting transfers between devices  11.6 us (58%)
  Pallas kernels  4.99 us (25%)
  waiting for transfers between devices  2.99 us (15%)
    ppermute x2, starting transfers between devices, local(): lax.ppermute(held, 'sub', [(k, k ^ step) for k in range(subs)])  6.06 us
    ppermute x8, starting transfers between devices, swap(): return lax.ppermute(x, 'facet', [(i, i ^ step) for i in range(facets)])  5.57 us
    ppermute x8, waiting for transfers between devices, swap(): return lax.ppermute(x, 'facet', [(i, i ^ step) for i in range(facets)])  2.6 us
    pallas_call x1, Pallas kernels, local(): pl.pallas_call(backward_kernel, out_shape=shaped((1, rows, 2 * length), F...  1.51 us
    pallas_call x1, Pallas kernels, local(): pl.pallas_call(forward_kernel, out_shape=[shaped((count * rows, LANES), B...  1.41 us
    pallas_call x1, Pallas kernels, local(): pl.pallas_call(functools.partial(prepare_kernel, subs, length), out_shape...  1.24 us
  transfers between devices with their start and end apart: 10, of which 5 were waited for; matrix products, arithmetic and copies ran while one was open for 0% of the time, Pallas kernels for 18%

profile of v5, /device:TPU:0, one launch (start us, length us, event | category | flops | bytes accessed | tf_op | source)
XLA Modules:
  0.0 19.7 jit_solution(1498785503249115620)
XLA Ops:
  0.0 0.0 copy-start
  0.0 0.0 copy-start.2
  0.0 3.0 %collective-permute-start.1 = (f32[4,512]{1,0:T(4,128)}, f32[4,512]{1,0:T(4,128)S(1)}, u32[]{:S(2)}, u32[]{:S(2)}) collective-permute-start(f32[4,512]{1,0:T(4,128)} %first_ref.1), channel_id=1, source_target_pairs={{0,1},{1,0},{2,3},{3,2},{4,5},{5,4},{6,7},{7,6},{8,9},{9,8},{10,11... | collective-permute-start | bytes 24584 | tf_op jit(solution)/shard_map/ppermute | solution.py:403
  3.0 0.1 shard_map.73
  3.2 0.0 copy-done
  3.2 0.0 copy-start.1
  3.2 1.4 %shard_map.74 = (bf16[256,128]{1,0:T(8,128)(2,1)S(1)}, bf16[256,512]{1,0:T(8,128)(2,1)S(1)}) custom-call(s32[32]{0:T(128)} %sub_hbm.3, s32[8]{0:T(128)} %off_hbm.3, bf16[1,8,8192]{2,1,0:T(8,128)(2,1)S(1)} %copy-done, f32[256,128]{1,0:T(8,128)S(1)} %get-tuple-element.29.turn_ref.refs_7_, bf16[64,128]{1,0:T(8,128)(2,1)S(1)} %get-tuple-element.30.fwd_ref), custom_call_target="tpu_custom_call" | custom-call | tf_op jit(solution)/shard_map/pallas_call | solution.py:405
  4.6 0.1 collective-permute-start
  4.7 0.2 collective-permute-done.1.second_ref
  4.9 0.0 copy-done.1
  4.9 3.0 %collective-permute-start.2 = (f32[8,512]{1,0:T(8,128)S(1)}, f32[8,512]{1,0:T(8,128)S(1)}, u32[]{:S(2)}, u32[]{:S(2)}) collective-permute-start(f32[8,512]{1,0:T(8,128)S(1)} %shard_map.75.after_ref.refs_3_), channel_id=1, source_target_pairs={{0,2},{1,3},{2,0},{3,1},{4,6},{5,7},{6,4},{7,5},{8,10},{9,11},{10,... | collective-permute-start | bytes 49160 | tf_op jit(solution)/shard_map/ppermute | solution.py:403
  7.9 0.0 copy-done.2
  7.9 1.2 %shard_map.76 = (f32[256,128]{1,0:T(8,128)S(1)}, f32[256,128]{1,0:T(8,128)S(1)}, bf16[512,128]{1,0:T(8,128)(2,1)S(1)}, bf16[512,128]{1,0:T(8,128)(2,1)S(1)}, bf1...) custom-call(s32[32]{0:T(128)} %sub_hbm.3, ...), custom_call_target="tpu_custom_call" | custom-call | flops 20000000000 | bytes 1048576 | tf_op jit(solution)/shard_map/pallas_call | solution.py:432
  9.2 0.0 collective-permute-done.passed_ref
  9.2 0.2 %shard_map.77 = (f32[256,128]{1,0:T(8,128)S(1)}, bf16[256,128]{1,0:T(8,128)(2,1)S(1)}, bf16[256,128]{1,0:T(8,128)(2,1)S(1)}, bf16[256,128]{1,0:T(8,128)(2,1)S(1)}) custom-call(bf16[256,128]{1,0:T(8,128)(2,1)S(1)} %get-tuple-element.31.windows_ref, bf16[256,128]{1,0:T(8,128)(2,1)S(1)} %collective-permute-done.passed_ref, ...), custom_call_target="tpu_custom_call" | custom-call | tf_op jit(solution)/shard_map/pallas_call | solution.py:461
  9.4 0.2 %collective-permute-done.2.refs_4_ = f32[8,512]{1,0:T(8,128)S(1)} collective-permute-done((f32[8,512]{1,0:T(8,128)S(1)}, f32[8,512]{1,0:T(8,128)S(1)}, u32[]{:S(2)}, u32[]{:S(2)}) %collective-permute-start.2) | collective-permute-done | bytes 16416 | tf_op jit(solution)/shard_map/ppermute | solution.py:403
  9.7 1.9 %collective-permute-start.4 = (bf16[320,128]{1,0:T(8,128)(2,1)S(1)}, bf16[320,128]{1,0:T(8,128)(2,1)S(1)}, u32[]{:S(2)}, u32[]{:S(2)}) collective-permute-start(bf16[320,128]{1,0:T(8,128)(2,1)S(1)} %get-tuple-element.41), channel_id=1, source_target_pairs={{0,16},{4,20},{8,24},{12,28},{16,0},{20,4},{24,8},{28,12},{1,17},{... | collective-permute-start | bytes 245768 | tf_op jit(solution)/shard_map/ppermute | solution.py:388
  11.6 1.4 %collective-permute-start.5 = (bf16[320,128]{1,0:T(8,128)(2,1)S(1)}, bf16[320,128]{1,0:T(8,128)(2,1)S(1)}, u32[]{:S(2)}, u32[]{:S(2)}) collective-permute-start(bf16[320,128]{1,0:T(8,128)(2,1)S(1)} %get-tuple-element.42), channel_id=1, source_target_pairs={{0,24},{4,28},{8,16},{12,20},{16,8},{20,12},{24,0},{28,4},{1,25},{... | collective-permute-start | bytes 245768 | tf_op jit(solution)/shard_map/ppermute | solution.py:388
  13.0 0.2 %collective-permute-start.3 = (bf16[320,128]{1,0:T(8,128)(2,1)S(1)}, bf16[320,128]{1,0:T(8,128)(2,1)S(1)}, u32[]{:S(2)}, u32[]{:S(2)}) collective-permute-start(bf16[320,128]{1,0:T(8,128)(2,1)S(1)} %get-tuple-element.40), channel_id=1, source_target_pairs={{0,8},{4,12},{8,0},{12,4},{16,24},{20,28},{24,16},{28,20},{1,9},{5... | collective-permute-start | bytes 245768 | tf_op jit(solution)/shard_map/ppermute | solution.py:388
  13.2 0.0 collective-permute-start.6
  13.2 1.9 %collective-permute-start.7 = (bf16[64,128]{1,0:T(8,128)(2,1)S(1)}, bf16[64,128]{1,0:T(8,128)(2,1)S(1)}, u32[]{:S(2)}, u32[]{:S(2)}) collective-permute-start(bf16[64,128]{1,0:T(8,128)(2,1)S(1)} %get-tuple-element.43.refs_3_), channel_id=1, source_target_pairs={{0,12},{4,8},{8,4},{12,0},{16,28},{20,24},{24,20},{28,16},{1,13},{... | collective-permute-start | bytes 49160 | tf_op jit(solution)/shard_map/ppermute | solution.py:388
  15.1 0.0 collective-permute-done.4.refs_1_.block_ref
  15.1 0.1 shard_map.81
  15.3 0.0 collective-permute-start.9
  15.3 1.6 %collective-permute-done.5.refs_2_.block_ref = bf16[320,128]{1,0:T(8,128)(2,1)S(1)} collective-permute-done((bf16[320,128]{1,0:T(8,128)(2,1)S(1)}, bf16[320,128]{1,0:T(8,128)(2,1)S(1)}, u32[]{:S(2)}, u32[]{:S(2)}) %collective-permute-start.5) | collective-permute-done | bytes 81952 | tf_op jit(solution)/shard_map/ppermute | solution.py:388
  16.9 0.1 shard_map.80
  17.0 0.0 collective-permute-start.8
  17.0 0.0 collective-permute-done.6.refs_4_
  17.1 0.0 collective-permute-done.7.refs_5_
  17.1 0.4 %collective-permute-done.3.refs_0_ = bf16[320,128]{1,0:T(8,128)(2,1)S(1)} collective-permute-done((bf16[320,128]{1,0:T(8,128)(2,1)S(1)}, bf16[320,128]{1,0:T(8,128)(2,1)S(1)}, u32[]{:S(2)}, u32[]{:S(2)}) %collective-permute-start.3) | collective-permute-done | bytes 81952 | tf_op jit(solution)/shard_map/ppermute | solution.py:388
  17.4 0.2 shard_map.79
  17.6 0.0 collective-permute-done.9.refs_1_
  17.6 0.6 %collective-permute-done.8.refs_0_ = bf16[16,128]{1,0:T(8,128)(2,1)S(1)} collective-permute-done((bf16[16,128]{1,0:T(8,128)(2,1)S(1)}, bf16[16,128]{1,0:T(8,128)(2,1)S(1)}, u32[]{:S(2)}, u32[]{:S(2)}) %collective-permute-start.8) | collective-permute-done | bytes 4128 | tf_op jit(solution)/shard_map/ppermute | solution.py:388
  18.2 1.5 %shard_map.82 = f32[1,8,8192]{2,1,0:T(8,128)} custom-call(f32[256,128]{1,0:T(8,128)S(1)} %get-tuple-element.46.product_ref, bf16[16,128]{1,0:T(8,128)(2,1)S(1)} %collective-permute-done.8.refs_0_, bf16[16,128]{1,0:T(8,128)(2,1)S(1)} %collective-permute-done.9.refs_1_, bf16[96,128]{1,0:T(8,128)(2,1)S(1)} %get-tuple-element.48.refs_2_, ...), custom_call_target="tpu_custom_call" | custom-call | tf_op jit(solution)/shard_map/pallas_call | solution.py:498
  (2 shorter events, 0.0 us)
Async XLA Ops:
  0.0 3.2 %copy-start = (bf16[1,8,8192]{2,1,0:T(8,128)(2,1)S(1)}, bf16[1,8,8192]{2,1,0:T(8,128)(2,1)}, u32[]{:S(2)}) copy-start(bf16[1,8,8192]{2,1,0:T(8,128)(2,1)} %strips_ref.1) | copy-start | bytes 393220
  0.0 7.9 %copy-start.2 = (bf16[16,32,1024]{2,1,0:T(8,128)(2,1)S(1)}, bf16[16,32,1024]{2,1,0:T(8,128)(2,1)}, u32[]{:S(2)}) copy-start(bf16[16,32,1024]{2,1,0:T(8,128)(2,1)} %screens_ref.1) | copy-start | bytes 3145732
  0.0 4.9 %collective-permute-start.1 = (f32[4,512]{1,0:T(4,128)}, f32[4,512]{1,0:T(4,128)S(1)}, u32[]{:S(2)}, u32[]{:S(2)}) collective-permute-start(f32[4,512]{1,0:T(4,128)} %first_ref.1), channel_id=1, source_target_pairs={{0,1},{1,0},{2,3},{3,2},{4,5},{5,4},{6,7},{7,6},{8,9},{9,8},{10,11... | collective-permute-start | bytes 24584 | tf_op jit(solution)/shard_map/ppermute | solution.py:403
  3.2 1.7 %copy-start.1 = (f32[4,512]{1,0:T(4,128)S(1)}, f32[4,512]{1,0:T(4,128)}, u32[]{:S(2)}) copy-start(f32[4,512]{1,0:T(4,128)} %first_ref.1) | copy-start | bytes 24580
  4.6 4.5 %collective-permute-start = (bf16[256,128]{1,0:T(8,128)(2,1)S(1)}, bf16[256,128]{1,0:T(8,128)(2,1)S(1)}, u32[]{:S(2)}, u32[]{:S(2)}) collective-permute-start(bf16[256,128]{1,0:T(8,128)(2,1)S(1)} %get-tuple-element.31.windows_ref), channel_id=1, source_target_pairs={{0,4},{4,0},{8,12},{12,8},{16,20},{20,16},{24,28},{28,24},{1,5},{5... | collective-permute-start | bytes 196616 | tf_op jit(solution)/shard_map/ppermute | solution.py:388
  4.9 4.8 %collective-permute-start.2 = (f32[8,512]{1,0:T(8,128)S(1)}, f32[8,512]{1,0:T(8,128)S(1)}, u32[]{:S(2)}, u32[]{:S(2)}) collective-permute-start(f32[8,512]{1,0:T(8,128)S(1)} %shard_map.75.after_ref.refs_3_), channel_id=1, source_target_pairs={{0,2},{1,3},{2,0},{3,1},{4,6},{5,7},{6,4},{7,5},{8,10},{9,11},{10,... | collective-permute-start | bytes 49160 | tf_op jit(solution)/shard_map/ppermute | solution.py:403
  9.7 5.5 %collective-permute-start.4 = (bf16[320,128]{1,0:T(8,128)(2,1)S(1)}, bf16[320,128]{1,0:T(8,128)(2,1)S(1)}, u32[]{:S(2)}, u32[]{:S(2)}) collective-permute-start(bf16[320,128]{1,0:T(8,128)(2,1)S(1)} %get-tuple-element.41), channel_id=1, source_target_pairs={{0,16},{4,20},{8,24},{12,28},{16,0},{20,4},{24,8},{28,12},{1,17},{... | collective-permute-start | bytes 245768 | tf_op jit(solution)/shard_map/ppermute | solution.py:388
  11.6 5.3 %collective-permute-start.5 = (bf16[320,128]{1,0:T(8,128)(2,1)S(1)}, bf16[320,128]{1,0:T(8,128)(2,1)S(1)}, u32[]{:S(2)}, u32[]{:S(2)}) collective-permute-start(bf16[320,128]{1,0:T(8,128)(2,1)S(1)} %get-tuple-element.42), channel_id=1, source_target_pairs={{0,24},{4,28},{8,16},{12,20},{16,8},{20,12},{24,0},{28,4},{1,25},{... | collective-permute-start | bytes 245768 | tf_op jit(solution)/shard_map/ppermute | solution.py:388
  13.0 4.4 %collective-permute-start.3 = (bf16[320,128]{1,0:T(8,128)(2,1)S(1)}, bf16[320,128]{1,0:T(8,128)(2,1)S(1)}, u32[]{:S(2)}, u32[]{:S(2)}) collective-permute-start(bf16[320,128]{1,0:T(8,128)(2,1)S(1)} %get-tuple-element.40), channel_id=1, source_target_pairs={{0,8},{4,12},{8,0},{12,4},{16,24},{20,28},{24,16},{28,20},{1,9},{5... | collective-permute-start | bytes 245768 | tf_op jit(solution)/shard_map/ppermute | solution.py:388
  13.2 3.8 %collective-permute-start.6 = (bf16[64,128]{1,0:T(8,128)(2,1)S(1)}, bf16[64,128]{1,0:T(8,128)(2,1)S(1)}, u32[]{:S(2)}, u32[]{:S(2)}) collective-permute-start(bf16[64,128]{1,0:T(8,128)(2,1)S(1)} %get-tuple-element.43.refs_3_), channel_id=1, source_target_pairs={{0,4},{4,0},{8,12},{12,8},{16,20},{20,16},{24,28},{28,24},{1,5},{5... | collective-permute-start | bytes 49160 | tf_op jit(solution)/shard_map/ppermute | solution.py:388
  13.2 3.8 %collective-permute-start.7 = (bf16[64,128]{1,0:T(8,128)(2,1)S(1)}, bf16[64,128]{1,0:T(8,128)(2,1)S(1)}, u32[]{:S(2)}, u32[]{:S(2)}) collective-permute-start(bf16[64,128]{1,0:T(8,128)(2,1)S(1)} %get-tuple-element.43.refs_3_), channel_id=1, source_target_pairs={{0,12},{4,8},{8,4},{12,0},{16,28},{20,24},{24,20},{28,16},{1,13},{... | collective-permute-start | bytes 49160 | tf_op jit(solution)/shard_map/ppermute | solution.py:388
  15.3 2.3 %collective-permute-start.9 = (bf16[16,128]{1,0:T(8,128)(2,1)S(1)}, bf16[16,128]{1,0:T(8,128)(2,1)S(1)}, u32[]{:S(2)}, u32[]{:S(2)}) collective-permute-start(bf16[16,128]{1,0:T(8,128)(2,1)S(1)} %shard_map.81), channel_id=1, source_target_pairs={{0,4},{4,0},{8,12},{12,8},{16,20},{20,16},{24,28},{28,24},{1,5},{5... | collective-permute-start | bytes 12296 | tf_op jit(solution)/shard_map/ppermute | solution.py:388
  17.0 1.2 %collective-permute-start.8 = (bf16[16,128]{1,0:T(8,128)(2,1)S(1)}, bf16[16,128]{1,0:T(8,128)(2,1)S(1)}, u32[]{:S(2)}, u32[]{:S(2)}) collective-permute-start(bf16[16,128]{1,0:T(8,128)(2,1)S(1)} %shard_map.80), channel_id=1, source_target_pairs={{0,4},{4,0},{8,12},{12,8},{16,20},{20,16},{24,28},{28,24},{1,5},{5... | collective-permute-start | bytes 12296 | tf_op jit(solution)/shard_map/ppermute | solution.py:388

commit v6 on v5

--- a/solution.py
+++ b/solution.py
@@ -90,14 +90,30 @@
         out_ref[...] = merged[:, (n + 1) * LANES : (n + 2) * LANES].astype(BF)
 
 
-def pack_kernel(others, *refs):
-    merged_refs, held_refs, out_refs = refs[:others], refs[others : others + 2], refs[others + 2 :]
-    held = jnp.concatenate([ref[...] for ref in held_refs], axis=0)
+def pack_kernel(merged_ref, first_ref, second_ref, laid_ref, out_ref):
+    held = jnp.concatenate([first_ref[...], second_ref[...]], axis=0)
     laid = jnp.concatenate([held[:, c : c + LANES] for c in range(0, held.shape[1], LANES)], axis=0).astype(BF)
-    out_refs[0][...] = laid
-    for ref, out_ref in zip(merged_refs, out_refs[1:]):
-        out_ref[: ref.shape[0], :] = ref[...]
-        out_ref[ref.shape[0] :, :] = laid
+    laid_ref[...] = laid
+    out_ref[: merged_ref.shape[0], :] = merged_ref[...]
+    out_ref[merged_ref.shape[0] :, :] = laid
+
+
+def cut(blocks, hits):
+    chunks = hits.shape[0] // LANES
+    rows = []
+    for block in blocks:
+        size = block.shape[0] // chunks
+        rows.append(jnp.concatenate([block[c * size : (c + 1) * size] for c in range(chunks)], axis=1))
+    return dot(jnp.concatenate(rows, axis=0), hits).astype(BF)
+
+
+def attach_kernel(parts, *refs):
+    merged_refs, (laid_ref, passed_ref, shown_ref), out_refs = refs[:parts], refs[parts : parts + 3], refs[parts + 3 :]
+    for n in range(parts):
+        hits = shown_ref[:, n * LANES : (n + 1) * LANES]
+        windows = merged_refs[n].shape[0]
+        out_refs[n][:windows, :] = merged_refs[n][...]
+        out_refs[n][windows:, :] = cut([laid_ref[...], passed_ref[...]], hits)
 
 
 def scalars(pairs, sems):
@@ -194,6 +210,7 @@
     sin_ref,
     both_ref,
     other_ref,
+    shown_ref,
     rank_ref,
     gather_ref,
     coarse_ref,
@@ -240,6 +257,9 @@
     sines = screens_ref[:, block, span:].reshape(kinds * tall, span)
     both_ref[...] = both
     other_ref[...] = jnp.where(apart == off_ref[mine ^ 1], 1.0, 0.0).astype(BF)
+    for n in range(shown_ref.shape[1] // LANES):
+        hit = apart == off_ref[mine ^ (2 * n + 2)]
+        shown_ref[:, n * LANES : (n + 1) * LANES] = jnp.where(hit, 1.0, 0.0).astype(BF)
     cos_scr[...] = dot(cosines, both)
     sin_scr[...] = dot(sines, signed)
     for j in range(count):
@@ -265,7 +285,9 @@
     facet_step = (tall_owner >> bits) ^ mine
     sub_step = (tall_owner & (subs - 1)) ^ my_sub
     facets = off_ref.shape[0]
-    block = (facet_step & 1) * (facets // 2) + (facet_step >> 1)
+    block = jnp.where(facet_step < 2, facet_step, facet_step + 1)
+    block = jnp.where(facet_step == facets - 2, 2, block)
+    block = jnp.where(facet_step == facets - 1, facets - 1, block)
     place = (block * subs + sub_step) * CAP + slot.astype(jnp.int32)
     for at in range(0, rank_ref.shape[1], LANES):
         hit = iota((count, LANES), 1) + at == place
@@ -290,22 +312,13 @@
     coarse_ref[M:, :] = high_low(jnp.where(lane_im, cos, sin), low)
 
 
-def cut(blocks, chunks, hits):
-    rows = []
-    for block in blocks:
-        size = block.shape[0] // chunks
-        rows.append(jnp.concatenate([block[c * size : (c + 1) * size] for c in range(chunks)], axis=1))
-    return dot(jnp.concatenate(rows, axis=0), hits).astype(BF)
-
-
 def tail_kernel(size, block_ref, hits_ref, out_ref):
-    chunks = hits_ref.shape[0] // LANES
-    out_ref[...] = cut([block_ref[block_ref.shape[0] - size :, :]], chunks, hits_ref[...])
-
-
-def screen_kernel(size, own_ref, *refs):
-    cos_ref, sin_ref, hits_ref, out_ref, cut_ref = refs[-5:]
-    arrived, others = refs[:-8], refs[-8:-5]
+    out_ref[...] = cut([block_ref[block_ref.shape[0] - size :, :]], hits_ref[...])
+
+
+def screen_kernel(own_ref, *refs):
+    laid_ref, passed_ref, cos_ref, sin_ref, hits_ref, out_ref, cut_ref = refs[-7:]
+    arrived = refs[:-7]
     windows = own_ref.shape[0]
     for at in range(0, windows, 16):
         pair = slice(at, at + 16)
@@ -313,12 +326,17 @@
         for ref in arrived:
             total = total + ref[pair, :].astype(F32)
         out_ref[pair, :] = total * cos_ref[pair, :] + pltpu.roll(total, M, 1) * sin_ref[pair, :]
-    held = [others[0][...]] + [ref[windows:, :] for ref in arrived] + [ref[...] for ref in others[1:]]
-    cut_ref[...] = cut(held, hits_ref.shape[0] // LANES, hits_ref[...])
+    here = cut([laid_ref[...], passed_ref[...], arrived[-1][windows:, :]], hits_ref[...])
+    cut_ref[: here.shape[0], :] = here
+    at = here.shape[0]
+    for ref in arrived[:-1]:
+        rows = ref.shape[0] - windows
+        cut_ref[at : at + rows, :] = ref[windows:, :]
+        at += rows
 
 
 def backward_kernel(product_ref, *refs):
-    cuts, refs = refs[:-9][::-1], refs[-9:]
+    cuts, refs = refs[:-9], refs[-9:]
     rank_ref, gather_ref, coarse_ref, inv_ref, turn_ref, out_hbm, out_scr, flat_scr, out_sems = refs
     rows = out_hbm.shape[1]
     length = out_hbm.shape[2] // 2
@@ -429,20 +447,21 @@
         held, _ = lax.optimization_barrier((beside, windows))
 
     tall = max(rows, 16)
-    cos, sin, both, other, *ready = pl.pallas_call(
+    cos, sin, both, other, shown, *ready = pl.pallas_call(
         functools.partial(prepare_kernel, subs, length),
         out_shape=[
             shaped((count * rows, LANES), F32),
             shaped((count * rows, LANES), F32),
             shaped((span, LANES), BF),
             shaped((span, LANES), BF),
+            shaped((span, (facets // 2 - 2) * LANES), BF),
             shaped((count, facets * subs * CAP), BF),
             shaped((count, LANES), jnp.int32),
             shaped((2 * M, 4 * count), BF),
             shaped((4 * chunks, 2 * LANES), BF),
         ],
         in_specs=[hbm] * 5 + [vmem],
-        out_specs=[vmem] * 8,
+        out_specs=[vmem] * 9,
         scratch_shapes=[
             pltpu.VMEM((kinds * tall, LANES), F32),
             pltpu.VMEM((kinds * tall, LANES), F32),
@@ -466,39 +485,46 @@
         compiler_params=limit,
     )(windows, passed, shift)
     size = subs * grid_weight.size // LANES
-    own_rows, *payloads = pl.pallas_call(
-        functools.partial(pack_kernel, others),
-        out_shape=[shaped((size, LANES), BF)] + [shaped((count * rows + size, LANES), BF)] * others,
-        in_specs=[vmem] * (others + 2),
-        out_specs=[vmem] * (1 + others),
-        compiler_params=limit,
-    )(*merged, last, beside)
-
-    arrived = [swap(payload, 2 * n + 2) for n, payload in enumerate(payloads)]
-    across = [swap(own_rows, 1), swap(own_rows, 3)]
-    late = []
-    for block in arrived[1:]:
-        tail = pl.pallas_call(
-            functools.partial(tail_kernel, size),
-            out_shape=shaped((subs * CAP, LANES), BF),
-            in_specs=[vmem] * 2,
-            out_specs=vmem,
-            compiler_params=limit,
-        )(block, other)
-        late.append(swap(tail, 1))
+    laid, payload = pl.pallas_call(
+        pack_kernel,
+        out_shape=[shaped((size, LANES), BF), shaped((count * rows + size, LANES), BF)],
+        in_specs=[vmem] * 3,
+        out_specs=[vmem] * 2,
+        compiler_params=limit,
+    )(merged[-1], last, beside)
+
+    far = swap(payload, facets - 2)
+    laid_other = swap(laid, 1)
+    parts = others - 1
+    payloads = pl.pallas_call(
+        functools.partial(attach_kernel, parts),
+        out_shape=[shaped((count * rows + 2 * subs * CAP, LANES), BF)] * parts,
+        in_specs=[vmem] * (parts + 3),
+        out_specs=[vmem] * parts,
+        compiler_params=limit,
+    )(*merged[:-1], laid, laid_other, shown)
+    arrived = [swap(block, 2 * n + 2) for n, block in enumerate(payloads)] + [far]
+    tail = pl.pallas_call(
+        functools.partial(tail_kernel, size),
+        out_shape=shaped((subs * CAP, LANES), BF),
+        in_specs=[vmem] * 2,
+        out_specs=vmem,
+        compiler_params=limit,
+    )(far, other)
+    late = swap(tail, 1)
 
     product, early = pl.pallas_call(
-        functools.partial(screen_kernel, size),
-        out_shape=[shaped(windows.shape, F32), shaped(((others + 3) * subs * CAP, LANES), BF)],
-        in_specs=[vmem] * (others + 7),
+        screen_kernel,
+        out_shape=[shaped(windows.shape, F32), shaped(((facets - 1) * subs * CAP, LANES), BF)],
+        in_specs=[vmem] * (others + 6),
         out_specs=[vmem] * 2,
         compiler_params=limit,
-    )(own, *arrived, own_rows, *across, cos, sin, both)
+    )(own, *arrived, laid, laid_other, cos, sin, both)
 
     return pl.pallas_call(
         backward_kernel,
         out_shape=shaped((1, rows, 2 * length), F32),
-        in_specs=[vmem] * (len(late) + 7),
+        in_specs=[vmem] * 8,
         out_specs=hbm,
         scratch_shapes=[
             pltpu.VMEM((2 * chunks * rows, LANES), F32),
@@ -506,7 +532,7 @@
             pltpu.SemaphoreType.DMA((4,)),
         ],
         compiler_params=limit,
-    )(product, *late[::-1], early, *ready, turn)
+    )(product, early, late, *ready, turn)
 
 
 def solution(mesh):

time: 19.9 us -> 19.5 us (0.980)
  starting transfers between devices: 11.6 us -> 10.8 us
  waiting for transfers between devices: 2.99 us -> 3.43 us
    ppermute x8 -> x6, starting transfers between devices: 5.57 us -> 4.72 us  [swap(): return lax.ppermute(x, 'facet', [(i, i ^ step) for i in range(facets)])]
    ppermute x8 -> x6, waiting for transfers between devices: 2.6 us -> 3.09 us  [swap(): return lax.ppermute(x, 'facet', [(i, i ^ step) for i in range(facets)])]
  transfers between devices with their start and end apart: 10 -> 8, of which waited for: 5 -> 5; matrix products, arithmetic and copies ran while one was open for 0% -> 0% of each run, Pallas kernels for 18% -> 18%
where the time goes in v6:
time: 19.5 us; the launch traced here: 19.4 us
  starting transfers between devices  10.8 us (55%)
  Pallas kernels  5.05 us (26%)
  waiting for transfers between devices  3.43 us (18%)
    ppermute x2, starting transfers between devices, local(): lax.ppermute(held, 'sub', [(k, k ^ step) for k in range(subs)])  6.06 us
    ppermute x6, starting transfers between devices, swap(): return lax.ppermute(x, 'facet', [(i, i ^ step) for i in range(facets)])  4.72 us
    ppermute x6, waiting for transfers between devices, swap(): return lax.ppermute(x, 'facet', [(i, i ^ step) for i in range(facets)])  3.09 us
    pallas_call x1, Pallas kernels, local(): pl.pallas_call(backward_kernel, out_shape=shaped((1, rows, 2 * length), F...  1.52 us
    pallas_call x1, Pallas kernels, local(): pl.pallas_call(forward_kernel, out_shape=[shaped((count * rows, LANES), B...  1.41 us
    pallas_call x1, Pallas kernels, local(): pl.pallas_call(functools.partial(prepare_kernel, subs, length), out_shape...  1.3 us
  transfers between devices with their start and end apart: 8, of which 5 were waited for; matrix products, arithmetic and copies ran while one was open for 0% of the time, Pallas kernels for 18%

profile of v6, /device:TPU:0, one launch (start us, length us, event | category | flops | bytes accessed | tf_op | source)
XLA Modules:
  0.0 19.4 jit_solution(2431844945892384265)
XLA Ops:
  0.0 0.0 copy-start
  0.0 0.0 copy-start.2
  0.0 3.0 %collective-permute-start.1 = (f32[4,512]{1,0:T(4,128)}, f32[4,512]{1,0:T(4,128)S(1)}, u32[]{:S(2)}, u32[]{:S(2)}) collective-permute-start(f32[4,512]{1,0:T(4,128)} %first_ref.1), channel_id=1, source_target_pairs={{0,1},{1,0},{2,3},{3,2},{4,5},{5,4},{6,7},{7,6},{8,9},{9,8},{10,11... | collective-permute-start | bytes 24584 | tf_op jit(solution)/shard_map/ppermute | solution.py:421
  3.0 0.1 shard_map.73
  3.2 0.0 copy-done
  3.2 0.0 copy-start.1
  3.2 1.4 %shard_map.74 = (bf16[256,128]{1,0:T(8,128)(2,1)S(1)}, bf16[256,512]{1,0:T(8,128)(2,1)S(1)}) custom-call(s32[32]{0:T(128)} %sub_hbm.3, s32[8]{0:T(128)} %off_hbm.3, bf16[1,8,8192]{2,1,0:T(8,128)(2,1)S(1)} %copy-done, f32[256,128]{1,0:T(8,128)S(1)} %get-tuple-element.30.turn_ref.refs_6_, bf16[64,128]{1,0:T(8,128)(2,1)S(1)} %get-tuple-element.31.fwd_ref), custom_call_target="tpu_custom_call" | custom-call | tf_op jit(solution)/shard_map/pallas_call | solution.py:423
  4.6 0.1 collective-permute-start
  4.7 0.2 collective-permute-done.1.second_ref
  4.9 0.0 copy-done.1
  4.9 3.0 %collective-permute-start.2 = (f32[8,512]{1,0:T(8,128)S(1)}, f32[8,512]{1,0:T(8,128)S(1)}, u32[]{:S(2)}, u32[]{:S(2)}) collective-permute-start(f32[8,512]{1,0:T(8,128)S(1)} %shard_map.75.after_ref.first_ref), channel_id=1, source_target_pairs={{0,2},{1,3},{2,0},{3,1},{4,6},{5,7},{6,4},{7,5},{8,10},{9,11},{10,... | collective-permute-start | bytes 49160 | tf_op jit(solution)/shard_map/ppermute | solution.py:421
  7.9 0.0 copy-done.2
  7.9 1.3 %shard_map.76 = (f32[256,128]{1,0:T(8,128)S(1)}, f32[256,128]{1,0:T(8,128)S(1)}, bf16[512,128]{1,0:T(8,128)(2,1)S(1)}, bf16[512,128]{1,0:T(8,128)(2,1)S(1)}, bf1...) custom-call(s32[32]{0:T(128)} %sub_hbm.3, ...), custom_call_target="tpu_custom_call" | custom-call | flops 20000000000 | bytes 1048576 | tf_op jit(solution)/shard_map/pallas_call | solution.py:450
  9.2 0.0 collective-permute-done.passed_ref
  9.2 0.2 %shard_map.77 = (f32[256,128]{1,0:T(8,128)S(1)}, bf16[256,128]{1,0:T(8,128)(2,1)S(1)}, bf16[256,128]{1,0:T(8,128)(2,1)S(1)}, bf16[256,128]{1,0:T(8,128)(2,1)S(1)}) custom-call(bf16[256,128]{1,0:T(8,128)(2,1)S(1)} %get-tuple-element.32.windows_ref, bf16[256,128]{1,0:T(8,128)(2,1)S(1)} %collective-permute-done.passed_ref, ...), custom_call_target="tpu_custom_call" | custom-call | tf_op jit(solution)/shard_map/pallas_call | solution.py:480
  9.5 0.2 collective-permute-done.2.second_ref
  9.6 0.1 collective-permute-start.3
  9.7 2.8 %collective-permute-start.6 = (bf16[320,128]{1,0:T(8,128)(2,1)S(1)}, bf16[320,128]{1,0:T(8,128)(2,1)S(1)}, u32[]{:S(2)}, u32[]{:S(2)}) collective-permute-start(bf16[320,128]{1,0:T(8,128)(2,1)S(1)} %get-tuple-element.45), channel_id=1, source_target_pairs={{0,24},{4,28},{8,16},{12,20},{16,8},{20,12},{24,0},{28,4},{1,25},{... | collective-permute-start | bytes 245768 | tf_op jit(solution)/shard_map/ppermute | solution.py:406
  12.6 0.0 collective-permute-done.3.refs_3_.refs_4_
  12.6 0.2 shard_map.79
  12.7 0.6 %collective-permute-start.4 = (bf16[288,128]{1,0:T(8,128)(2,1)S(1)}, bf16[288,128]{1,0:T(8,128)(2,1)S(1)}, u32[]{:S(2)}, u32[]{:S(2)}) collective-permute-start(bf16[288,128]{1,0:T(8,128)(2,1)S(1)} %get-tuple-element.43), channel_id=1, source_target_pairs={{0,8},{4,12},{8,0},{12,4},{16,24},{20,28},{24,16},{28,20},{1,9},{5... | collective-permute-start | bytes 221192 | tf_op jit(solution)/shard_map/ppermute | solution.py:406
  13.3 1.1 %collective-permute-start.5 = (bf16[288,128]{1,0:T(8,128)(2,1)S(1)}, bf16[288,128]{1,0:T(8,128)(2,1)S(1)}, u32[]{:S(2)}, u32[]{:S(2)}) collective-permute-start(bf16[288,128]{1,0:T(8,128)(2,1)S(1)} %get-tuple-element.44), channel_id=1, source_target_pairs={{0,16},{4,20},{8,24},{12,28},{16,0},{20,4},{24,8},{28,12},{1,17},{... | collective-permute-start | bytes 221192 | tf_op jit(solution)/shard_map/ppermute | solution.py:406
  14.5 1.2 %collective-permute-done.6.refs_2_.block_ref = bf16[320,128]{1,0:T(8,128)(2,1)S(1)} collective-permute-done((bf16[320,128]{1,0:T(8,128)(2,1)S(1)}, bf16[320,128]{1,0:T(8,128)(2,1)S(1)}, u32[]{:S(2)}, u32[]{:S(2)}) %collective-permute-start.6) | collective-permute-done | bytes 81952 | tf_op jit(solution)/shard_map/ppermute | solution.py:406
  15.7 0.1 shard_map.81
  15.8 0.0 collective-permute-start.7
  15.8 1.6 %collective-permute-done.4.refs_0_ = bf16[288,128]{1,0:T(8,128)(2,1)S(1)} collective-permute-done((bf16[288,128]{1,0:T(8,128)(2,1)S(1)}, bf16[288,128]{1,0:T(8,128)(2,1)S(1)}, u32[]{:S(2)}, u32[]{:S(2)}) %collective-permute-start.4) | collective-permute-done | bytes 73760 | tf_op jit(solution)/shard_map/ppermute | solution.py:406
  17.4 0.2 %collective-permute-done.5.refs_1_ = bf16[288,128]{1,0:T(8,128)(2,1)S(1)} collective-permute-done((bf16[288,128]{1,0:T(8,128)(2,1)S(1)}, bf16[288,128]{1,0:T(8,128)(2,1)S(1)}, u32[]{:S(2)}, u32[]{:S(2)}) %collective-permute-start.5) | collective-permute-done | bytes 73760 | tf_op jit(solution)/shard_map/ppermute | solution.py:406
  17.7 0.2 shard_map.80
  17.8 0.0 collective-permute-done.7.refs_1_
  17.8 1.5 %shard_map.82 = f32[1,8,8192]{2,1,0:T(8,128)} custom-call(f32[256,128]{1,0:T(8,128)S(1)} %get-tuple-element.48.product_ref, bf16[112,128]{1,0:T(8,128)(2,1)S(1)} %get-tuple-element.49.refs_0_, bf16[16,128]{1,0:T(8,128)(2,1)S(1)} %collective-permute-done.7.refs_1_, bf16[32,128]{1,0:T(8,128)(2,1)S(1)} %get-tuple-element.51.refs_2_, ...), custom_call_target="tpu_custom_call" | custom-call | tf_op jit(solution)/shard_map/pallas_call | solution.py:524
  (2 shorter events, 0.0 us)
Async XLA Ops:
  0.0 3.2 %copy-start = (bf16[1,8,8192]{2,1,0:T(8,128)(2,1)S(1)}, bf16[1,8,8192]{2,1,0:T(8,128)(2,1)}, u32[]{:S(2)}) copy-start(bf16[1,8,8192]{2,1,0:T(8,128)(2,1)} %strips_ref.1) | copy-start | bytes 393220
  0.0 7.9 %copy-start.2 = (bf16[16,32,1024]{2,1,0:T(8,128)(2,1)S(1)}, bf16[16,32,1024]{2,1,0:T(8,128)(2,1)}, u32[]{:S(2)}) copy-start(bf16[16,32,1024]{2,1,0:T(8,128)(2,1)} %screens_ref.1) | copy-start | bytes 3145732
  0.0 4.9 %collective-permute-start.1 = (f32[4,512]{1,0:T(4,128)}, f32[4,512]{1,0:T(4,128)S(1)}, u32[]{:S(2)}, u32[]{:S(2)}) collective-permute-start(f32[4,512]{1,0:T(4,128)} %first_ref.1), channel_id=1, source_target_pairs={{0,1},{1,0},{2,3},{3,2},{4,5},{5,4},{6,7},{7,6},{8,9},{9,8},{10,11... | collective-permute-start | bytes 24584 | tf_op jit(solution)/shard_map/ppermute | solution.py:421
  3.2 1.7 %copy-start.1 = (f32[4,512]{1,0:T(4,128)S(1)}, f32[4,512]{1,0:T(4,128)}, u32[]{:S(2)}) copy-start(f32[4,512]{1,0:T(4,128)} %first_ref.1) | copy-start | bytes 24580
  4.6 4.6 %collective-permute-start = (bf16[256,128]{1,0:T(8,128)(2,1)S(1)}, bf16[256,128]{1,0:T(8,128)(2,1)S(1)}, u32[]{:S(2)}, u32[]{:S(2)}) collective-permute-start(bf16[256,128]{1,0:T(8,128)(2,1)S(1)} %get-tuple-element.32.windows_ref), channel_id=1, source_target_pairs={{0,4},{4,0},{8,12},{12,8},{16,20},{20,16},{24,28},{28,24},{1,5},{5... | collective-permute-start | bytes 196616 | tf_op jit(solution)/shard_map/ppermute | solution.py:406
  4.9 4.8 %collective-permute-start.2 = (f32[8,512]{1,0:T(8,128)S(1)}, f32[8,512]{1,0:T(8,128)S(1)}, u32[]{:S(2)}, u32[]{:S(2)}) collective-permute-start(f32[8,512]{1,0:T(8,128)S(1)} %shard_map.75.after_ref.first_ref), channel_id=1, source_target_pairs={{0,2},{1,3},{2,0},{3,1},{4,6},{5,7},{6,4},{7,5},{8,10},{9,11},{10,... | collective-permute-start | bytes 49160 | tf_op jit(solution)/shard_map/ppermute | solution.py:421
  9.6 2.9 %collective-permute-start.3 = (bf16[64,128]{1,0:T(8,128)(2,1)S(1)}, bf16[64,128]{1,0:T(8,128)(2,1)S(1)}, u32[]{:S(2)}, u32[]{:S(2)}) collective-permute-start(bf16[64,128]{1,0:T(8,128)(2,1)S(1)} %get-tuple-element.41.refs_2_.refs_3_), channel_id=1, source_target_pairs={{0,4},{4,0},{8,12},{12,8},{16,20},{20,16},{24,28},{28,24},{1,5},{5... | collective-permute-start | bytes 49160 | tf_op jit(solution)/shard_map/ppermute | solution.py:406
  9.7 6.0 %collective-permute-start.6 = (bf16[320,128]{1,0:T(8,128)(2,1)S(1)}, bf16[320,128]{1,0:T(8,128)(2,1)S(1)}, u32[]{:S(2)}, u32[]{:S(2)}) collective-permute-start(bf16[320,128]{1,0:T(8,128)(2,1)S(1)} %get-tuple-element.45), channel_id=1, source_target_pairs={{0,24},{4,28},{8,16},{12,20},{16,8},{20,12},{24,0},{28,4},{1,25},{... | collective-permute-start | bytes 245768 | tf_op jit(solution)/shard_map/ppermute | solution.py:406
  12.7 4.7 %collective-permute-start.4 = (bf16[288,128]{1,0:T(8,128)(2,1)S(1)}, bf16[288,128]{1,0:T(8,128)(2,1)S(1)}, u32[]{:S(2)}, u32[]{:S(2)}) collective-permute-start(bf16[288,128]{1,0:T(8,128)(2,1)S(1)} %get-tuple-element.43), channel_id=1, source_target_pairs={{0,8},{4,12},{8,0},{12,4},{16,24},{20,28},{24,16},{28,20},{1,9},{5... | collective-permute-start | bytes 221192 | tf_op jit(solution)/shard_map/ppermute | solution.py:406
  13.3 4.4 %collective-permute-start.5 = (bf16[288,128]{1,0:T(8,128)(2,1)S(1)}, bf16[288,128]{1,0:T(8,128)(2,1)S(1)}, u32[]{:S(2)}, u32[]{:S(2)}) collective-permute-start(bf16[288,128]{1,0:T(8,128)(2,1)S(1)} %get-tuple-element.44), channel_id=1, source_target_pairs={{0,16},{4,20},{8,24},{12,28},{16,0},{20,4},{24,8},{28,12},{1,17},{... | collective-permute-start | bytes 221192 | tf_op jit(solution)/shard_map/ppermute | solution.py:406
  15.8 2.0 %collective-permute-start.7 = (bf16[16,128]{1,0:T(8,128)(2,1)S(1)}, bf16[16,128]{1,0:T(8,128)(2,1)S(1)}, u32[]{:S(2)}, u32[]{:S(2)}) collective-permute-start(bf16[16,128]{1,0:T(8,128)(2,1)S(1)} %shard_map.81), channel_id=1, source_target_pairs={{0,4},{4,0},{8,12},{12,8},{16,20},{20,16},{24,28},{28,24},{1,5},{5... | collective-permute-start | bytes 12296 | tf_op jit(solution)/shard_map/ppermute | solution.py:406

commit v7 on v6

--- a/solution.py
+++ b/solution.py
@@ -312,45 +312,36 @@
     coarse_ref[M:, :] = high_low(jnp.where(lane_im, cos, sin), low)
 
 
-def tail_kernel(size, block_ref, hits_ref, out_ref):
-    out_ref[...] = cut([block_ref[block_ref.shape[0] - size :, :]], hits_ref[...])
-
-
-def screen_kernel(own_ref, *refs):
-    laid_ref, passed_ref, cos_ref, sin_ref, hits_ref, out_ref, cut_ref = refs[-7:]
-    arrived = refs[:-7]
+def first_kernel(own_ref, block_ref, laid_ref, passed_ref, hits_ref, other_ref, tail_ref, cut_ref, total_ref):
     windows = own_ref.shape[0]
-    for at in range(0, windows, 16):
-        pair = slice(at, at + 16)
-        total = own_ref[pair, :]
-        for ref in arrived:
-            total = total + ref[pair, :].astype(F32)
-        out_ref[pair, :] = total * cos_ref[pair, :] + pltpu.roll(total, M, 1) * sin_ref[pair, :]
-    here = cut([laid_ref[...], passed_ref[...], arrived[-1][windows:, :]], hits_ref[...])
-    cut_ref[: here.shape[0], :] = here
-    at = here.shape[0]
-    for ref in arrived[:-1]:
-        rows = ref.shape[0] - windows
-        cut_ref[at : at + rows, :] = ref[windows:, :]
-        at += rows
-
-
-def backward_kernel(product_ref, *refs):
-    cuts, refs = refs[:-9], refs[-9:]
-    rank_ref, gather_ref, coarse_ref, inv_ref, turn_ref, out_hbm, out_scr, flat_scr, out_sems = refs
+    rows = block_ref[windows:, :]
+    tail_ref[...] = cut([rows], other_ref[...])
+    cut_ref[...] = cut([laid_ref[...], passed_ref[...], rows], hits_ref[...])
+    total_ref[...] = own_ref[...] + block_ref[:windows, :].astype(F32)
+
+
+def backward_kernel(total_ref, *refs):
+    arrived, refs = refs[:-13], refs[-13:]
+    cut_ref, late_ref, cos_ref, sin_ref = refs[:4]
+    rank_ref, gather_ref, coarse_ref, inv_ref, turn_ref, out_hbm, out_scr, flat_scr, out_sems = refs[4:]
     rows = out_hbm.shape[1]
     length = out_hbm.shape[2] // 2
     chunks = length // LANES
-    windows = product_ref.shape[0]
+    windows = total_ref.shape[0]
     count = windows // rows
 
-    weights = dot(rank_ref[...], jnp.concatenate([ref[...] for ref in cuts], axis=0))
+    cuts = [cut_ref[...]] + [ref[windows:, :] for ref in arrived] + [late_ref[...]]
+    weights = dot(rank_ref[...], jnp.concatenate(cuts, axis=0))
 
     place = gather_ref[...]
     inside = place < M
     blocks = []
     for r in range(rows):
-        value = product_ref[r * count : (r + 1) * count, :] * weights
+        here = slice(r * count, (r + 1) * count)
+        total = total_ref[here, :]
+        for ref in arrived:
+            total = total + ref[here, :].astype(F32)
+        value = (total * cos_ref[here, :] + pltpu.roll(total, M, 1) * sin_ref[here, :]) * weights
         value = value.astype(BF).astype(F32)
         re = jnp.where(inside, jnp.take_along_axis(value, place, axis=1), 0.0)
         im = jnp.where(inside, jnp.take_along_axis(value, place ^ M, axis=1), 0.0)
@@ -503,28 +494,24 @@
         out_specs=[vmem] * parts,
         compiler_params=limit,
     )(*merged[:-1], laid, laid_other, shown)
-    arrived = [swap(block, 2 * n + 2) for n, block in enumerate(payloads)] + [far]
-    tail = pl.pallas_call(
-        functools.partial(tail_kernel, size),
-        out_shape=shaped((subs * CAP, LANES), BF),
-        in_specs=[vmem] * 2,
-        out_specs=vmem,
-        compiler_params=limit,
-    )(far, other)
+    arrived = [swap(block, 2 * n + 2) for n, block in enumerate(payloads)]
+    tail, here, total = pl.pallas_call(
+        first_kernel,
+        out_shape=[
+            shaped((subs * CAP, LANES), BF),
+            shaped((3 * subs * CAP, LANES), BF),
+            shaped(windows.shape, F32),
+        ],
+        in_specs=[vmem] * 6,
+        out_specs=[vmem] * 3,
+        compiler_params=limit,
+    )(own, far, laid, laid_other, both, other)
     late = swap(tail, 1)
-
-    product, early = pl.pallas_call(
-        screen_kernel,
-        out_shape=[shaped(windows.shape, F32), shaped(((facets - 1) * subs * CAP, LANES), BF)],
-        in_specs=[vmem] * (others + 6),
-        out_specs=[vmem] * 2,
-        compiler_params=limit,
-    )(own, *arrived, laid, laid_other, cos, sin, both)
 
     return pl.pallas_call(
         backward_kernel,
         out_shape=shaped((1, rows, 2 * length), F32),
-        in_specs=[vmem] * 8,
+        in_specs=[vmem] * (parts + 10),
         out_specs=hbm,
         scratch_shapes=[
             pltpu.VMEM((2 * chunks * rows, LANES), F32),
@@ -532,7 +519,7 @@
             pltpu.SemaphoreType.DMA((4,)),
         ],
         compiler_params=limit,
-    )(product, early, late, *ready, turn)
+    )(total, *arrived, here, late, cos, sin, *ready, turn)
 
 
 def solution(mesh):

time: 19.5 us -> 19.4 us (level)
  transfers between devices with their start and end apart: 8 -> 8, of which waited for: 5 -> 6; matrix products, arithmetic and copies ran while one was open for 0% -> 0% of each run, Pallas kernels for 18% -> 18%
where the time goes in v7:
time: 19.4 us; the launch traced here: 19.3 us
  starting transfers between devices  10.9 us (56%)
  Pallas kernels  4.97 us (26%)
  waiting for transfers between devices  3.32 us (17%)
    ppermute x2, starting transfers between devices, local(): lax.ppermute(held, 'sub', [(k, k ^ step) for k in range(subs)])  6.06 us
    ppermute x6, starting transfers between devices, swap(): return lax.ppermute(x, 'facet', [(i, i ^ step) for i in range(facets)])  4.79 us
    ppermute x6, waiting for transfers between devices, swap(): return lax.ppermute(x, 'facet', [(i, i ^ step) for i in range(facets)])  2.98 us
    pallas_call x1, Pallas kernels, local(): pl.pallas_call(backward_kernel, out_shape=shaped((1, rows, 2 * length), F...  1.57 us
    pallas_call x1, Pallas kernels, local(): pl.pallas_call(forward_kernel, out_shape=[shaped((count * rows, LANES), B...  1.41 us
    pallas_call x1, Pallas kernels, local(): pl.pallas_call(functools.partial(prepare_kernel, subs, length), out_shape...  1.3 us
  transfers between devices with their start and end apart: 8, of which 6 were waited for; matrix products, arithmetic and copies ran while one was open for 0% of the time, Pallas kernels for 18%

profile of v7, /device:TPU:0, one launch (start us, length us, event | category | flops | bytes accessed | tf_op | source)
XLA Modules:
  0.0 19.3 jit_solution(12364013755766060233)
XLA Ops:
  0.0 0.0 copy-start
  0.0 0.0 copy-start.2
  0.0 3.0 %collective-permute-start.1 = (f32[4,512]{1,0:T(4,128)}, f32[4,512]{1,0:T(4,128)S(1)}, u32[]{:S(2)}, u32[]{:S(2)}) collective-permute-start(f32[4,512]{1,0:T(4,128)} %first_ref.1), channel_id=1, source_target_pairs={{0,1},{1,0},{2,3},{3,2},{4,5},{5,4},{6,7},{7,6},{8,9},{9,8},{10,11... | collective-permute-start | bytes 24584 | tf_op jit(solution)/shard_map/ppermute | solution.py:412
  3.0 0.1 shard_map.73
  3.2 0.0 copy-done
  3.2 0.0 copy-start.1
  3.2 1.4 %shard_map.74 = (bf16[256,128]{1,0:T(8,128)(2,1)S(1)}, bf16[256,512]{1,0:T(8,128)(2,1)S(1)}) custom-call(s32[32]{0:T(128)} %sub_hbm.3, s32[8]{0:T(128)} %off_hbm.3, bf16[1,8,8192]{2,1,0:T(8,128)(2,1)S(1)} %copy-done, f32[256,128]{1,0:T(8,128)S(1)} %get-tuple-element.31.turn_ref.refs_10_, bf16[64,128]{1,0:T(8,128)(2,1)S(1)} %get-tuple-element.32.fwd_ref), custom_call_target="tpu_custom_call" | custom-call | tf_op jit(solution)/shard_map/pallas_call | solution.py:414
  4.6 0.1 collective-permute-start
  4.7 0.2 collective-permute-done.1.second_ref
  4.9 0.0 copy-done.1
  4.9 3.0 %collective-permute-start.2 = (f32[8,512]{1,0:T(8,128)S(1)}, f32[8,512]{1,0:T(8,128)S(1)}, u32[]{:S(2)}, u32[]{:S(2)}) collective-permute-start(f32[8,512]{1,0:T(8,128)S(1)} %shard_map.75.after_ref.first_ref), channel_id=1, source_target_pairs={{0,2},{1,3},{2,0},{3,1},{4,6},{5,7},{6,4},{7,5},{8,10},{9,11},{10,... | collective-permute-start | bytes 49160 | tf_op jit(solution)/shard_map/ppermute | solution.py:412
  7.9 0.0 copy-done.2
  7.9 1.3 %shard_map.76 = (f32[256,128]{1,0:T(8,128)S(1)}, f32[256,128]{1,0:T(8,128)S(1)}, bf16[512,128]{1,0:T(8,128)(2,1)S(1)}, bf16[512,128]{1,0:T(8,128)(2,1)S(1)}, bf1...) custom-call(s32[32]{0:T(128)} %sub_hbm.3, ...), custom_call_target="tpu_custom_call" | custom-call | flops 20000000000 | bytes 1048576 | tf_op jit(solution)/shard_map/pallas_call | solution.py:441
  9.2 0.0 collective-permute-done.passed_ref
  9.2 0.2 %shard_map.77 = (f32[256,128]{1,0:T(8,128)S(1)}, bf16[256,128]{1,0:T(8,128)(2,1)S(1)}, bf16[256,128]{1,0:T(8,128)(2,1)S(1)}, bf16[256,128]{1,0:T(8,128)(2,1)S(1)}) custom-call(bf16[256,128]{1,0:T(8,128)(2,1)S(1)} %get-tuple-element.33.windows_ref, bf16[256,128]{1,0:T(8,128)(2,1)S(1)} %collective-permute-done.passed_ref, ...), custom_call_target="tpu_custom_call" | custom-call | tf_op jit(solution)/shard_map/pallas_call | solution.py:471
  9.5 0.2 collective-permute-done.2.second_ref
  9.6 0.1 collective-permute-start.4
  9.7 2.8 %collective-permute-start.3 = (bf16[320,128]{1,0:T(8,128)(2,1)S(1)}, bf16[320,128]{1,0:T(8,128)(2,1)S(1)}, u32[]{:S(2)}, u32[]{:S(2)}) collective-permute-start(bf16[320,128]{1,0:T(8,128)(2,1)S(1)} %get-tuple-element.40), channel_id=1, source_target_pairs={{0,24},{4,28},{8,16},{12,20},{16,8},{20,12},{24,0},{28,4},{1,25},{... | collective-permute-start | bytes 245768 | tf_op jit(solution)/shard_map/ppermute | solution.py:397
  12.6 0.0 collective-permute-done.4.passed_ref.refs_3_
  12.6 0.2 shard_map.80
  12.7 0.6 %collective-permute-start.5 = (bf16[288,128]{1,0:T(8,128)(2,1)S(1)}, bf16[288,128]{1,0:T(8,128)(2,1)S(1)}, u32[]{:S(2)}, u32[]{:S(2)}) collective-permute-start(bf16[288,128]{1,0:T(8,128)(2,1)S(1)} %get-tuple-element.47), channel_id=1, source_target_pairs={{0,8},{4,12},{8,0},{12,4},{16,24},{20,28},{24,16},{28,20},{1,9},{5... | collective-permute-start | bytes 221192 | tf_op jit(solution)/shard_map/ppermute | solution.py:397
  13.3 1.1 %collective-permute-start.6 = (bf16[288,128]{1,0:T(8,128)(2,1)S(1)}, bf16[288,128]{1,0:T(8,128)(2,1)S(1)}, u32[]{:S(2)}, u32[]{:S(2)}) collective-permute-start(bf16[288,128]{1,0:T(8,128)(2,1)S(1)} %get-tuple-element.48), channel_id=1, source_target_pairs={{0,16},{4,20},{8,24},{12,28},{16,0},{20,4},{24,8},{28,12},{1,17},{... | collective-permute-start | bytes 221192 | tf_op jit(solution)/shard_map/ppermute | solution.py:397
  14.5 1.2 %collective-permute-done.3.block_ref = bf16[320,128]{1,0:T(8,128)(2,1)S(1)} collective-permute-done((bf16[320,128]{1,0:T(8,128)(2,1)S(1)}, bf16[320,128]{1,0:T(8,128)(2,1)S(1)}, u32[]{:S(2)}, u32[]{:S(2)}) %collective-permute-start.3) | collective-permute-done | bytes 81952 | tf_op jit(solution)/shard_map/ppermute | solution.py:397
  15.7 0.2 shard_map.79
  15.8 0.1 collective-permute-start.7
  15.9 1.2 %collective-permute-done.7.refs_3_ = bf16[16,128]{1,0:T(8,128)(2,1)S(1)} collective-permute-done((bf16[16,128]{1,0:T(8,128)(2,1)S(1)}, bf16[16,128]{1,0:T(8,128)(2,1)S(1)}, u32[]{:S(2)}, u32[]{:S(2)}) %collective-permute-start.7) | collective-permute-done | bytes 4128 | tf_op jit(solution)/shard_map/ppermute | solution.py:397
  17.1 0.4 %collective-permute-done.5.refs_0_ = bf16[288,128]{1,0:T(8,128)(2,1)S(1)} collective-permute-done((bf16[288,128]{1,0:T(8,128)(2,1)S(1)}, bf16[288,128]{1,0:T(8,128)(2,1)S(1)}, u32[]{:S(2)}, u32[]{:S(2)}) %collective-permute-start.5) | collective-permute-done | bytes 73760 | tf_op jit(solution)/shard_map/ppermute | solution.py:397
  17.4 0.2 %collective-permute-done.6.refs_1_ = bf16[288,128]{1,0:T(8,128)(2,1)S(1)} collective-permute-done((bf16[288,128]{1,0:T(8,128)(2,1)S(1)}, bf16[288,128]{1,0:T(8,128)(2,1)S(1)}, u32[]{:S(2)}, u32[]{:S(2)}) %collective-permute-start.6) | collective-permute-done | bytes 73760 | tf_op jit(solution)/shard_map/ppermute | solution.py:397
  17.7 1.6 %shard_map.81 = f32[1,8,8192]{2,1,0:T(8,128)} custom-call(f32[256,128]{1,0:T(8,128)S(1)} %get-tuple-element.43.total_ref, bf16[288,128]{1,0:T(8,128)(2,1)S(1)} %collective-permute-done.5.refs_0_, bf16[288,128]{1,0:T(8,128)(2,1)S(1)} %collective-permute-done.6.refs_1_, bf16[48,128]{1,0:T(8,128)(2,1)S(1)} %get-tuple-element.49.refs_2_, ...), custom_call_target="tpu_custom_call" | custom-call | tf_op jit(solution)/shard_map/pallas_call | solution.py:511
  (2 shorter events, 0.0 us)
Async XLA Ops:
  0.0 3.2 %copy-start = (bf16[1,8,8192]{2,1,0:T(8,128)(2,1)S(1)}, bf16[1,8,8192]{2,1,0:T(8,128)(2,1)}, u32[]{:S(2)}) copy-start(bf16[1,8,8192]{2,1,0:T(8,128)(2,1)} %strips_ref.1) | copy-start | bytes 393220
  0.0 7.9 %copy-start.2 = (bf16[16,32,1024]{2,1,0:T(8,128)(2,1)S(1)}, bf16[16,32,1024]{2,1,0:T(8,128)(2,1)}, u32[]{:S(2)}) copy-start(bf16[16,32,1024]{2,1,0:T(8,128)(2,1)} %screens_ref.1) | copy-start | bytes 3145732
  0.0 4.9 %collective-permute-start.1 = (f32[4,512]{1,0:T(4,128)}, f32[4,512]{1,0:T(4,128)S(1)}, u32[]{:S(2)}, u32[]{:S(2)}) collective-permute-start(f32[4,512]{1,0:T(4,128)} %first_ref.1), channel_id=1, source_target_pairs={{0,1},{1,0},{2,3},{3,2},{4,5},{5,4},{6,7},{7,6},{8,9},{9,8},{10,11... | collective-permute-start | bytes 24584 | tf_op jit(solution)/shard_map/ppermute | solution.py:412
  3.2 1.7 %copy-start.1 = (f32[4,512]{1,0:T(4,128)S(1)}, f32[4,512]{1,0:T(4,128)}, u32[]{:S(2)}) copy-start(f32[4,512]{1,0:T(4,128)} %first_ref.1) | copy-start | bytes 24580
  4.6 4.6 %collective-permute-start = (bf16[256,128]{1,0:T(8,128)(2,1)S(1)}, bf16[256,128]{1,0:T(8,128)(2,1)S(1)}, u32[]{:S(2)}, u32[]{:S(2)}) collective-permute-start(bf16[256,128]{1,0:T(8,128)(2,1)S(1)} %get-tuple-element.33.windows_ref), channel_id=1, source_target_pairs={{0,4},{4,0},{8,12},{12,8},{16,20},{20,16},{24,28},{28,24},{1,5},{5... | collective-permute-start | bytes 196616 | tf_op jit(solution)/shard_map/ppermute | solution.py:397
  4.9 4.8 %collective-permute-start.2 = (f32[8,512]{1,0:T(8,128)S(1)}, f32[8,512]{1,0:T(8,128)S(1)}, u32[]{:S(2)}, u32[]{:S(2)}) collective-permute-start(f32[8,512]{1,0:T(8,128)S(1)} %shard_map.75.after_ref.first_ref), channel_id=1, source_target_pairs={{0,2},{1,3},{2,0},{3,1},{4,6},{5,7},{6,4},{7,5},{8,10},{9,11},{10,... | collective-permute-start | bytes 49160 | tf_op jit(solution)/shard_map/ppermute | solution.py:412
  9.6 2.9 %collective-permute-start.4 = (bf16[64,128]{1,0:T(8,128)(2,1)S(1)}, bf16[64,128]{1,0:T(8,128)(2,1)S(1)}, u32[]{:S(2)}, u32[]{:S(2)}) collective-permute-start(bf16[64,128]{1,0:T(8,128)(2,1)S(1)} %get-tuple-element.41.laid_ref.refs_2_), channel_id=1, source_target_pairs={{0,4},{4,0},{8,12},{12,8},{16,20},{20,16},{24,28},{28,24},{1,5},{5... | collective-permute-start | bytes 49160 | tf_op jit(solution)/shard_map/ppermute | solution.py:397
  9.7 6.0 %collective-permute-start.3 = (bf16[320,128]{1,0:T(8,128)(2,1)S(1)}, bf16[320,128]{1,0:T(8,128)(2,1)S(1)}, u32[]{:S(2)}, u32[]{:S(2)}) collective-permute-start(bf16[320,128]{1,0:T(8,128)(2,1)S(1)} %get-tuple-element.40), channel_id=1, source_target_pairs={{0,24},{4,28},{8,16},{12,20},{16,8},{20,12},{24,0},{28,4},{1,25},{... | collective-permute-start | bytes 245768 | tf_op jit(solution)/shard_map/ppermute | solution.py:397
  12.7 4.7 %collective-permute-start.5 = (bf16[288,128]{1,0:T(8,128)(2,1)S(1)}, bf16[288,128]{1,0:T(8,128)(2,1)S(1)}, u32[]{:S(2)}, u32[]{:S(2)}) collective-permute-start(bf16[288,128]{1,0:T(8,128)(2,1)S(1)} %get-tuple-element.47), channel_id=1, source_target_pairs={{0,8},{4,12},{8,0},{12,4},{16,24},{20,28},{24,16},{28,20},{1,9},{5... | collective-permute-start | bytes 221192 | tf_op jit(solution)/shard_map/ppermute | solution.py:397
  13.3 4.4 %collective-permute-start.6 = (bf16[288,128]{1,0:T(8,128)(2,1)S(1)}, bf16[288,128]{1,0:T(8,128)(2,1)S(1)}, u32[]{:S(2)}, u32[]{:S(2)}) collective-permute-start(bf16[288,128]{1,0:T(8,128)(2,1)S(1)} %get-tuple-element.48), channel_id=1, source_target_pairs={{0,16},{4,20},{8,24},{12,28},{16,0},{20,4},{24,8},{28,12},{1,17},{... | collective-permute-start | bytes 221192 | tf_op jit(solution)/shard_map/ppermute | solution.py:397
  15.8 1.2 %collective-permute-start.7 = (bf16[16,128]{1,0:T(8,128)(2,1)S(1)}, bf16[16,128]{1,0:T(8,128)(2,1)S(1)}, u32[]{:S(2)}, u32[]{:S(2)}) collective-permute-start(bf16[16,128]{1,0:T(8,128)(2,1)S(1)} %get-tuple-element.50), channel_id=1, source_target_pairs={{0,4},{4,0},{8,12},{12,8},{16,20},{20,16},{24,28},{28,24},{1,5},{5... | collective-permute-start | bytes 12296 | tf_op jit(solution)/shard_map/ppermute | solution.py:397

commit v8 on v7

--- a/solution.py
+++ b/solution.py
@@ -109,11 +109,11 @@
 
 def attach_kernel(parts, *refs):
     merged_refs, (laid_ref, passed_ref, shown_ref), out_refs = refs[:parts], refs[parts : parts + 3], refs[parts + 3 :]
+    rows = cut([laid_ref[...], passed_ref[...]], shown_ref[...])
     for n in range(parts):
-        hits = shown_ref[:, n * LANES : (n + 1) * LANES]
         windows = merged_refs[n].shape[0]
         out_refs[n][:windows, :] = merged_refs[n][...]
-        out_refs[n][windows:, :] = cut([laid_ref[...], passed_ref[...]], hits)
+        out_refs[n][windows:, :] = rows[:, n * LANES : (n + 1) * LANES]
 
 
 def scalars(pairs, sems):
@@ -321,7 +321,7 @@
 
 
 def backward_kernel(total_ref, *refs):
-    arrived, refs = refs[:-13], refs[-13:]
+    arrived, refs = refs[:-13][::-1], refs[-13:]
     cut_ref, late_ref, cos_ref, sin_ref = refs[:4]
     rank_ref, gather_ref, coarse_ref, inv_ref, turn_ref, out_hbm, out_scr, flat_scr, out_sems = refs[4:]
     rows = out_hbm.shape[1]
@@ -519,7 +519,7 @@
             pltpu.SemaphoreType.DMA((4,)),
         ],
         compiler_params=limit,
-    )(total, *arrived, here, late, cos, sin, *ready, turn)
+    )(total, *arrived[::-1], here, late, cos, sin, *ready, turn)
 
 
 def solution(mesh):

time: 19.4 us -> 19.4 us (level)
  no operation moved by 1% of the time
where the time goes in v8:
time: 19.4 us; the launch traced here: 19.2 us
  starting transfers between devices  10.8 us (56%)
  Pallas kernels  4.97 us (26%)
  waiting for transfers between devices  3.29 us (17%)
    ppermute x2, starting transfers between devices, local(): lax.ppermute(held, 'sub', [(k, k ^ step) for k in range(subs)])  6.06 us
    ppermute x6, starting transfers between devices, swap(): return lax.ppermute(x, 'facet', [(i, i ^ step) for i in range(facets)])  4.79 us
    ppermute x6, waiting for transfers between devices, swap(): return lax.ppermute(x, 'facet', [(i, i ^ step) for i in range(facets)])  2.95 us
    pallas_call x1, Pallas kernels, local(): pl.pallas_call(backward_kernel, out_shape=shaped((1, rows, 2 * length), F...  1.57 us
    pallas_call x1, Pallas kernels, local(): pl.pallas_call(forward_kernel, out_shape=[shaped((count * rows, LANES), B...  1.41 us
    pallas_call x1, Pallas kernels, local(): pl.pallas_call(functools.partial(prepare_kernel, subs, length), out_shape...  1.3 us
  transfers between devices with their start and end apart: 8, of which 6 were waited for; matrix products, arithmetic and copies ran while one was open for 0% of the time, Pallas kernels for 18%

profile of v8, /device:TPU:0, one launch (start us, length us, event | category | flops | bytes accessed | tf_op | source)
XLA Modules:
  0.0 19.2 jit_solution(9231310597548806494)
XLA Ops:
  0.0 0.0 copy-start
  0.0 0.0 copy-start.2
  0.0 3.0 %collective-permute-start.1 = (f32[4,512]{1,0:T(4,128)}, f32[4,512]{1,0:T(4,128)S(1)}, u32[]{:S(2)}, u32[]{:S(2)}) collective-permute-start(f32[4,512]{1,0:T(4,128)} %first_ref.1), channel_id=1, source_target_pairs={{0,1},{1,0},{2,3},{3,2},{4,5},{5,4},{6,7},{7,6},{8,9},{9,8},{10,11... | collective-permute-start | bytes 24584 | tf_op jit(solution)/shard_map/ppermute | solution.py:412
  3.0 0.1 shard_map.73
  3.2 0.0 copy-done
  3.2 0.0 copy-start.1
  3.2 1.4 %shard_map.74 = (bf16[256,128]{1,0:T(8,128)(2,1)S(1)}, bf16[256,512]{1,0:T(8,128)(2,1)S(1)}) custom-call(s32[32]{0:T(128)} %sub_hbm.3, s32[8]{0:T(128)} %off_hbm.3, bf16[1,8,8192]{2,1,0:T(8,128)(2,1)S(1)} %copy-done, f32[256,128]{1,0:T(8,128)S(1)} %get-tuple-element.31.turn_ref.refs_10_, bf16[64,128]{1,0:T(8,128)(2,1)S(1)} %get-tuple-element.32.fwd_ref), custom_call_target="tpu_custom_call" | custom-call | tf_op jit(solution)/shard_map/pallas_call | solution.py:414
  4.6 0.1 collective-permute-start
  4.7 0.2 collective-permute-done.1.second_ref
  4.9 0.0 copy-done.1
  4.9 3.0 %collective-permute-start.2 = (f32[8,512]{1,0:T(8,128)S(1)}, f32[8,512]{1,0:T(8,128)S(1)}, u32[]{:S(2)}, u32[]{:S(2)}) collective-permute-start(f32[8,512]{1,0:T(8,128)S(1)} %shard_map.75.after_ref.first_ref), channel_id=1, source_target_pairs={{0,2},{1,3},{2,0},{3,1},{4,6},{5,7},{6,4},{7,5},{8,10},{9,11},{10,... | collective-permute-start | bytes 49160 | tf_op jit(solution)/shard_map/ppermute | solution.py:412
  7.9 0.0 copy-done.2
  7.9 1.3 %shard_map.76 = (f32[256,128]{1,0:T(8,128)S(1)}, f32[256,128]{1,0:T(8,128)S(1)}, bf16[512,128]{1,0:T(8,128)(2,1)S(1)}, bf16[512,128]{1,0:T(8,128)(2,1)S(1)}, bf1...) custom-call(s32[32]{0:T(128)} %sub_hbm.3, ...), custom_call_target="tpu_custom_call" | custom-call | flops 20000000000 | bytes 1048576 | tf_op jit(solution)/shard_map/pallas_call | solution.py:441
  9.2 0.0 collective-permute-done.passed_ref
  9.2 0.2 %shard_map.77 = (f32[256,128]{1,0:T(8,128)S(1)}, bf16[256,128]{1,0:T(8,128)(2,1)S(1)}, bf16[256,128]{1,0:T(8,128)(2,1)S(1)}, bf16[256,128]{1,0:T(8,128)(2,1)S(1)}) custom-call(bf16[256,128]{1,0:T(8,128)(2,1)S(1)} %get-tuple-element.33.windows_ref, bf16[256,128]{1,0:T(8,128)(2,1)S(1)} %collective-permute-done.passed_ref, ...), custom_call_target="tpu_custom_call" | custom-call | tf_op jit(solution)/shard_map/pallas_call | solution.py:471
  9.5 0.2 collective-permute-done.2.second_ref
  9.6 0.1 collective-permute-start.4
  9.7 2.8 %collective-permute-start.3 = (bf16[320,128]{1,0:T(8,128)(2,1)S(1)}, bf16[320,128]{1,0:T(8,128)(2,1)S(1)}, u32[]{:S(2)}, u32[]{:S(2)}) collective-permute-start(bf16[320,128]{1,0:T(8,128)(2,1)S(1)} %get-tuple-element.40), channel_id=1, source_target_pairs={{0,24},{4,28},{8,16},{12,20},{16,8},{20,12},{24,0},{28,4},{1,25},{... | collective-permute-start | bytes 245768 | tf_op jit(solution)/shard_map/ppermute | solution.py:397
  12.6 0.0 collective-permute-done.4.passed_ref.refs_3_
  12.6 0.1 shard_map.80
  12.7 0.6 %collective-permute-start.5 = (bf16[288,128]{1,0:T(8,128)(2,1)S(1)}, bf16[288,128]{1,0:T(8,128)(2,1)S(1)}, u32[]{:S(2)}, u32[]{:S(2)}) collective-permute-start(bf16[288,128]{1,0:T(8,128)(2,1)S(1)} %get-tuple-element.47), channel_id=1, source_target_pairs={{0,16},{4,20},{8,24},{12,28},{16,0},{20,4},{24,8},{28,12},{1,17},{... | collective-permute-start | bytes 221192 | tf_op jit(solution)/shard_map/ppermute | solution.py:397
  13.3 1.2 %collective-permute-start.6 = (bf16[288,128]{1,0:T(8,128)(2,1)S(1)}, bf16[288,128]{1,0:T(8,128)(2,1)S(1)}, u32[]{:S(2)}, u32[]{:S(2)}) collective-permute-start(bf16[288,128]{1,0:T(8,128)(2,1)S(1)} %get-tuple-element.48), channel_id=1, source_target_pairs={{0,8},{4,12},{8,0},{12,4},{16,24},{20,28},{24,16},{28,20},{1,9},{5... | collective-permute-start | bytes 221192 | tf_op jit(solution)/shard_map/ppermute | solution.py:397
  14.4 1.1 %collective-permute-done.3.block_ref = bf16[320,128]{1,0:T(8,128)(2,1)S(1)} collective-permute-done((bf16[320,128]{1,0:T(8,128)(2,1)S(1)}, bf16[320,128]{1,0:T(8,128)(2,1)S(1)}, u32[]{:S(2)}, u32[]{:S(2)}) %collective-permute-start.3) | collective-permute-done | bytes 81952 | tf_op jit(solution)/shard_map/ppermute | solution.py:397
  15.6 0.2 shard_map.79
  15.8 0.1 collective-permute-start.7
  15.8 1.2 %collective-permute-done.7.refs_3_ = bf16[16,128]{1,0:T(8,128)(2,1)S(1)} collective-permute-done((bf16[16,128]{1,0:T(8,128)(2,1)S(1)}, bf16[16,128]{1,0:T(8,128)(2,1)S(1)}, u32[]{:S(2)}, u32[]{:S(2)}) %collective-permute-start.7) | collective-permute-done | bytes 4128 | tf_op jit(solution)/shard_map/ppermute | solution.py:397
  17.0 0.2 collective-permute-done.5.refs_0_
  17.2 0.5 %collective-permute-done.6.refs_1_ = bf16[288,128]{1,0:T(8,128)(2,1)S(1)} collective-permute-done((bf16[288,128]{1,0:T(8,128)(2,1)S(1)}, bf16[288,128]{1,0:T(8,128)(2,1)S(1)}, u32[]{:S(2)}, u32[]{:S(2)}) %collective-permute-start.6) | collective-permute-done | bytes 73760 | tf_op jit(solution)/shard_map/ppermute | solution.py:397
  17.6 1.6 %shard_map.81 = f32[1,8,8192]{2,1,0:T(8,128)} custom-call(f32[256,128]{1,0:T(8,128)S(1)} %get-tuple-element.43.total_ref, bf16[288,128]{1,0:T(8,128)(2,1)S(1)} %collective-permute-done.5.refs_0_, bf16[288,128]{1,0:T(8,128)(2,1)S(1)} %collective-permute-done.6.refs_1_, bf16[48,128]{1,0:T(8,128)(2,1)S(1)} %get-tuple-element.49.refs_2_, ...), custom_call_target="tpu_custom_call" | custom-call | tf_op jit(solution)/shard_map/pallas_call | solution.py:511
  (2 shorter events, 0.0 us)
Async XLA Ops:
  0.0 3.2 %copy-start = (bf16[1,8,8192]{2,1,0:T(8,128)(2,1)S(1)}, bf16[1,8,8192]{2,1,0:T(8,128)(2,1)}, u32[]{:S(2)}) copy-start(bf16[1,8,8192]{2,1,0:T(8,128)(2,1)} %strips_ref.1) | copy-start | bytes 393220
  0.0 7.9 %copy-start.2 = (bf16[16,32,1024]{2,1,0:T(8,128)(2,1)S(1)}, bf16[16,32,1024]{2,1,0:T(8,128)(2,1)}, u32[]{:S(2)}) copy-start(bf16[16,32,1024]{2,1,0:T(8,128)(2,1)} %screens_ref.1) | copy-start | bytes 3145732
  0.0 4.9 %collective-permute-start.1 = (f32[4,512]{1,0:T(4,128)}, f32[4,512]{1,0:T(4,128)S(1)}, u32[]{:S(2)}, u32[]{:S(2)}) collective-permute-start(f32[4,512]{1,0:T(4,128)} %first_ref.1), channel_id=1, source_target_pairs={{0,1},{1,0},{2,3},{3,2},{4,5},{5,4},{6,7},{7,6},{8,9},{9,8},{10,11... | collective-permute-start | bytes 24584 | tf_op jit(solution)/shard_map/ppermute | solution.py:412
  3.2 1.7 %copy-start.1 = (f32[4,512]{1,0:T(4,128)S(1)}, f32[4,512]{1,0:T(4,128)}, u32[]{:S(2)}) copy-start(f32[4,512]{1,0:T(4,128)} %first_ref.1) | copy-start | bytes 24580
  4.6 4.6 %collective-permute-start = (bf16[256,128]{1,0:T(8,128)(2,1)S(1)}, bf16[256,128]{1,0:T(8,128)(2,1)S(1)}, u32[]{:S(2)}, u32[]{:S(2)}) collective-permute-start(bf16[256,128]{1,0:T(8,128)(2,1)S(1)} %get-tuple-element.33.windows_ref), channel_id=1, source_target_pairs={{0,4},{4,0},{8,12},{12,8},{16,20},{20,16},{24,28},{28,24},{1,5},{5... | collective-permute-start | bytes 196616 | tf_op jit(solution)/shard_map/ppermute | solution.py:397
  4.9 4.8 %collective-permute-start.2 = (f32[8,512]{1,0:T(8,128)S(1)}, f32[8,512]{1,0:T(8,128)S(1)}, u32[]{:S(2)}, u32[]{:S(2)}) collective-permute-start(f32[8,512]{1,0:T(8,128)S(1)} %shard_map.75.after_ref.first_ref), channel_id=1, source_target_pairs={{0,2},{1,3},{2,0},{3,1},{4,6},{5,7},{6,4},{7,5},{8,10},{9,11},{10,... | collective-permute-start | bytes 49160 | tf_op jit(solution)/shard_map/ppermute | solution.py:412
  9.6 2.9 %collective-permute-start.4 = (bf16[64,128]{1,0:T(8,128)(2,1)S(1)}, bf16[64,128]{1,0:T(8,128)(2,1)S(1)}, u32[]{:S(2)}, u32[]{:S(2)}) collective-permute-start(bf16[64,128]{1,0:T(8,128)(2,1)S(1)} %get-tuple-element.41.laid_ref.refs_2_), channel_id=1, source_target_pairs={{0,4},{4,0},{8,12},{12,8},{16,20},{20,16},{24,28},{28,24},{1,5},{5... | collective-permute-start | bytes 49160 | tf_op jit(solution)/shard_map/ppermute | solution.py:397
  9.7 5.9 %collective-permute-start.3 = (bf16[320,128]{1,0:T(8,128)(2,1)S(1)}, bf16[320,128]{1,0:T(8,128)(2,1)S(1)}, u32[]{:S(2)}, u32[]{:S(2)}) collective-permute-start(bf16[320,128]{1,0:T(8,128)(2,1)S(1)} %get-tuple-element.40), channel_id=1, source_target_pairs={{0,24},{4,28},{8,16},{12,20},{16,8},{20,12},{24,0},{28,4},{1,25},{... | collective-permute-start | bytes 245768 | tf_op jit(solution)/shard_map/ppermute | solution.py:397
  12.7 4.5 %collective-permute-start.5 = (bf16[288,128]{1,0:T(8,128)(2,1)S(1)}, bf16[288,128]{1,0:T(8,128)(2,1)S(1)}, u32[]{:S(2)}, u32[]{:S(2)}) collective-permute-start(bf16[288,128]{1,0:T(8,128)(2,1)S(1)} %get-tuple-element.47), channel_id=1, source_target_pairs={{0,16},{4,20},{8,24},{12,28},{16,0},{20,4},{24,8},{28,12},{1,17},{... | collective-permute-start | bytes 221192 | tf_op jit(solution)/shard_map/ppermute | solution.py:397
  13.3 4.4 %collective-permute-start.6 = (bf16[288,128]{1,0:T(8,128)(2,1)S(1)}, bf16[288,128]{1,0:T(8,128)(2,1)S(1)}, u32[]{:S(2)}, u32[]{:S(2)}) collective-permute-start(bf16[288,128]{1,0:T(8,128)(2,1)S(1)} %get-tuple-element.48), channel_id=1, source_target_pairs={{0,8},{4,12},{8,0},{12,4},{16,24},{20,28},{24,16},{28,20},{1,9},{5... | collective-permute-start | bytes 221192 | tf_op jit(solution)/shard_map/ppermute | solution.py:397
  15.8 1.2 %collective-permute-start.7 = (bf16[16,128]{1,0:T(8,128)(2,1)S(1)}, bf16[16,128]{1,0:T(8,128)(2,1)S(1)}, u32[]{:S(2)}, u32[]{:S(2)}) collective-permute-start(bf16[16,128]{1,0:T(8,128)(2,1)S(1)} %get-tuple-element.50), channel_id=1, source_target_pairs={{0,4},{4,0},{8,12},{12,8},{16,20},{20,16},{24,28},{28,24},{1,5},{5... | collective-permute-start | bytes 12296 | tf_op jit(solution)/shard_map/ppermute | solution.py:397

commit v9 on v8

--- a/solution.py
+++ b/solution.py
@@ -516,7 +516,7 @@
         scratch_shapes=[
             pltpu.VMEM((2 * chunks * rows, LANES), F32),
             pltpu.VMEM((rows, 2 * length), F32),
-            pltpu.SemaphoreType.DMA((4,)),
+            pltpu.SemaphoreType.DMA((2,)),
         ],
         compiler_params=limit,
     )(total, *arrived[::-1], here, late, cos, sin, *ready, turn)

time: 19.4 us -> 19.4 us (level)
  no operation moved by 1% of the time
where the time goes in v9:
time: 19.4 us; the launch traced here: 19.2 us
  starting transfers between devices  10.8 us (56%)
  Pallas kernels  4.97 us (26%)
  waiting for transfers between devices  3.29 us (17%)
    ppermute x2, starting transfers between devices, local(): lax.ppermute(held, 'sub', [(k, k ^ step) for k in range(subs)])  6.06 us
    ppermute x6, starting transfers between devices, swap(): return lax.ppermute(x, 'facet', [(i, i ^ step) for i in range(facets)])  4.79 us
    ppermute x6, waiting for transfers between devices, swap(): return lax.ppermute(x, 'facet', [(i, i ^ step) for i in range(facets)])  2.95 us
    pallas_call x1, Pallas kernels, local(): pl.pallas_call(backward_kernel, out_shape=shaped((1, rows, 2 * length), F...  1.57 us
    pallas_call x1, Pallas kernels, local(): pl.pallas_call(forward_kernel, out_shape=[shaped((count * rows, LANES), B...  1.41 us
    pallas_call x1, Pallas kernels, local(): pl.pallas_call(functools.partial(prepare_kernel, subs, length), out_shape...  1.3 us
  transfers between devices with their start and end apart: 8, of which 6 were waited for; matrix products, arithmetic and copies ran while one was open for 0% of the time, Pallas kernels for 18%

profile of v9, /device:TPU:0, one launch (start us, length us, event | category | flops | bytes accessed | tf_op | source)
XLA Modules:
  0.0 19.2 jit_solution(5012445106189765911)
XLA Ops:
  0.0 0.0 copy-start
  0.0 0.0 copy-start.2
  0.0 3.0 %collective-permute-start.1 = (f32[4,512]{1,0:T(4,128)}, f32[4,512]{1,0:T(4,128)S(1)}, u32[]{:S(2)}, u32[]{:S(2)}) collective-permute-start(f32[4,512]{1,0:T(4,128)} %first_ref.1), channel_id=1, source_target_pairs={{0,1},{1,0},{2,3},{3,2},{4,5},{5,4},{6,7},{7,6},{8,9},{9,8},{10,11... | collective-permute-start | bytes 24584 | tf_op jit(solution)/shard_map/ppermute | solution.py:412
  3.0 0.1 shard_map.73
  3.2 0.0 copy-done
  3.2 0.0 copy-start.1
  3.2 1.4 %shard_map.74 = (bf16[256,128]{1,0:T(8,128)(2,1)S(1)}, bf16[256,512]{1,0:T(8,128)(2,1)S(1)}) custom-call(s32[32]{0:T(128)} %sub_hbm.3, s32[8]{0:T(128)} %off_hbm.3, bf16[1,8,8192]{2,1,0:T(8,128)(2,1)S(1)} %copy-done, f32[256,128]{1,0:T(8,128)S(1)} %get-tuple-element.31.turn_ref.refs_10_, bf16[64,128]{1,0:T(8,128)(2,1)S(1)} %get-tuple-element.32.fwd_ref), custom_call_target="tpu_custom_call" | custom-call | tf_op jit(solution)/shard_map/pallas_call | solution.py:414
  4.6 0.1 collective-permute-start
  4.7 0.2 collective-permute-done.1.second_ref
  4.9 0.0 copy-done.1
  4.9 3.0 %collective-permute-start.2 = (f32[8,512]{1,0:T(8,128)S(1)}, f32[8,512]{1,0:T(8,128)S(1)}, u32[]{:S(2)}, u32[]{:S(2)}) collective-permute-start(f32[8,512]{1,0:T(8,128)S(1)} %shard_map.75.after_ref.first_ref), channel_id=1, source_target_pairs={{0,2},{1,3},{2,0},{3,1},{4,6},{5,7},{6,4},{7,5},{8,10},{9,11},{10,... | collective-permute-start | bytes 49160 | tf_op jit(solution)/shard_map/ppermute | solution.py:412
  7.9 0.0 copy-done.2
  7.9 1.3 %shard_map.76 = (f32[256,128]{1,0:T(8,128)S(1)}, f32[256,128]{1,0:T(8,128)S(1)}, bf16[512,128]{1,0:T(8,128)(2,1)S(1)}, bf16[512,128]{1,0:T(8,128)(2,1)S(1)}, bf1...) custom-call(s32[32]{0:T(128)} %sub_hbm.3, ...), custom_call_target="tpu_custom_call" | custom-call | flops 20000000000 | bytes 1048576 | tf_op jit(solution)/shard_map/pallas_call | solution.py:441
  9.2 0.0 collective-permute-done.passed_ref
  9.2 0.2 %shard_map.77 = (f32[256,128]{1,0:T(8,128)S(1)}, bf16[256,128]{1,0:T(8,128)(2,1)S(1)}, bf16[256,128]{1,0:T(8,128)(2,1)S(1)}, bf16[256,128]{1,0:T(8,128)(2,1)S(1)}) custom-call(bf16[256,128]{1,0:T(8,128)(2,1)S(1)} %get-tuple-element.33.windows_ref, bf16[256,128]{1,0:T(8,128)(2,1)S(1)} %collective-permute-done.passed_ref, ...), custom_call_target="tpu_custom_call" | custom-call | tf_op jit(solution)/shard_map/pallas_call | solution.py:471
  9.5 0.2 collective-permute-done.2.second_ref
  9.6 0.1 collective-permute-start.4
  9.7 2.8 %collective-permute-start.3 = (bf16[320,128]{1,0:T(8,128)(2,1)S(1)}, bf16[320,128]{1,0:T(8,128)(2,1)S(1)}, u32[]{:S(2)}, u32[]{:S(2)}) collective-permute-start(bf16[320,128]{1,0:T(8,128)(2,1)S(1)} %get-tuple-element.40), channel_id=1, source_target_pairs={{0,24},{4,28},{8,16},{12,20},{16,8},{20,12},{24,0},{28,4},{1,25},{... | collective-permute-start | bytes 245768 | tf_op jit(solution)/shard_map/ppermute | solution.py:397
  12.6 0.0 collective-permute-done.4.passed_ref.refs_3_
  12.6 0.1 shard_map.80
  12.7 0.6 %collective-permute-start.5 = (bf16[288,128]{1,0:T(8,128)(2,1)S(1)}, bf16[288,128]{1,0:T(8,128)(2,1)S(1)}, u32[]{:S(2)}, u32[]{:S(2)}) collective-permute-start(bf16[288,128]{1,0:T(8,128)(2,1)S(1)} %get-tuple-element.47), channel_id=1, source_target_pairs={{0,16},{4,20},{8,24},{12,28},{16,0},{20,4},{24,8},{28,12},{1,17},{... | collective-permute-start | bytes 221192 | tf_op jit(solution)/shard_map/ppermute | solution.py:397
  13.3 1.2 %collective-permute-start.6 = (bf16[288,128]{1,0:T(8,128)(2,1)S(1)}, bf16[288,128]{1,0:T(8,128)(2,1)S(1)}, u32[]{:S(2)}, u32[]{:S(2)}) collective-permute-start(bf16[288,128]{1,0:T(8,128)(2,1)S(1)} %get-tuple-element.48), channel_id=1, source_target_pairs={{0,8},{4,12},{8,0},{12,4},{16,24},{20,28},{24,16},{28,20},{1,9},{5... | collective-permute-start | bytes 221192 | tf_op jit(solution)/shard_map/ppermute | solution.py:397
  14.4 1.1 %collective-permute-done.3.block_ref = bf16[320,128]{1,0:T(8,128)(2,1)S(1)} collective-permute-done((bf16[320,128]{1,0:T(8,128)(2,1)S(1)}, bf16[320,128]{1,0:T(8,128)(2,1)S(1)}, u32[]{:S(2)}, u32[]{:S(2)}) %collective-permute-start.3) | collective-permute-done | bytes 81952 | tf_op jit(solution)/shard_map/ppermute | solution.py:397
  15.6 0.2 shard_map.79
  15.8 0.1 collective-permute-start.7
  15.8 1.2 %collective-permute-done.7.refs_3_ = bf16[16,128]{1,0:T(8,128)(2,1)S(1)} collective-permute-done((bf16[16,128]{1,0:T(8,128)(2,1)S(1)}, bf16[16,128]{1,0:T(8,128)(2,1)S(1)}, u32[]{:S(2)}, u32[]{:S(2)}) %collective-permute-start.7) | collective-permute-done | bytes 4128 | tf_op jit(solution)/shard_map/ppermute | solution.py:397
  17.0 0.2 collective-permute-done.5.refs_0_
  17.2 0.5 %collective-permute-done.6.refs_1_ = bf16[288,128]{1,0:T(8,128)(2,1)S(1)} collective-permute-done((bf16[288,128]{1,0:T(8,128)(2,1)S(1)}, bf16[288,128]{1,0:T(8,128)(2,1)S(1)}, u32[]{:S(2)}, u32[]{:S(2)}) %collective-permute-start.6) | collective-permute-done | bytes 73760 | tf_op jit(solution)/shard_map/ppermute | solution.py:397
  17.6 1.6 %shard_map.81 = f32[1,8,8192]{2,1,0:T(8,128)} custom-call(f32[256,128]{1,0:T(8,128)S(1)} %get-tuple-element.43.total_ref, bf16[288,128]{1,0:T(8,128)(2,1)S(1)} %collective-permute-done.5.refs_0_, bf16[288,128]{1,0:T(8,128)(2,1)S(1)} %collective-permute-done.6.refs_1_, bf16[48,128]{1,0:T(8,128)(2,1)S(1)} %get-tuple-element.49.refs_2_, ...), custom_call_target="tpu_custom_call" | custom-call | tf_op jit(solution)/shard_map/pallas_call | solution.py:511
  (2 shorter events, 0.0 us)
Async XLA Ops:
  0.0 3.2 %copy-start = (bf16[1,8,8192]{2,1,0:T(8,128)(2,1)S(1)}, bf16[1,8,8192]{2,1,0:T(8,128)(2,1)}, u32[]{:S(2)}) copy-start(bf16[1,8,8192]{2,1,0:T(8,128)(2,1)} %strips_ref.1) | copy-start | bytes 393220
  0.0 7.9 %copy-start.2 = (bf16[16,32,1024]{2,1,0:T(8,128)(2,1)S(1)}, bf16[16,32,1024]{2,1,0:T(8,128)(2,1)}, u32[]{:S(2)}) copy-start(bf16[16,32,1024]{2,1,0:T(8,128)(2,1)} %screens_ref.1) | copy-start | bytes 3145732
  0.0 4.9 %collective-permute-start.1 = (f32[4,512]{1,0:T(4,128)}, f32[4,512]{1,0:T(4,128)S(1)}, u32[]{:S(2)}, u32[]{:S(2)}) collective-permute-start(f32[4,512]{1,0:T(4,128)} %first_ref.1), channel_id=1, source_target_pairs={{0,1},{1,0},{2,3},{3,2},{4,5},{5,4},{6,7},{7,6},{8,9},{9,8},{10,11... | collective-permute-start | bytes 24584 | tf_op jit(solution)/shard_map/ppermute | solution.py:412
  3.2 1.7 %copy-start.1 = (f32[4,512]{1,0:T(4,128)S(1)}, f32[4,512]{1,0:T(4,128)}, u32[]{:S(2)}) copy-start(f32[4,512]{1,0:T(4,128)} %first_ref.1) | copy-start | bytes 24580
  4.6 4.6 %collective-permute-start = (bf16[256,128]{1,0:T(8,128)(2,1)S(1)}, bf16[256,128]{1,0:T(8,128)(2,1)S(1)}, u32[]{:S(2)}, u32[]{:S(2)}) collective-permute-start(bf16[256,128]{1,0:T(8,128)(2,1)S(1)} %get-tuple-element.33.windows_ref), channel_id=1, source_target_pairs={{0,4},{4,0},{8,12},{12,8},{16,20},{20,16},{24,28},{28,24},{1,5},{5... | collective-permute-start | bytes 196616 | tf_op jit(solution)/shard_map/ppermute | solution.py:397
  4.9 4.8 %collective-permute-start.2 = (f32[8,512]{1,0:T(8,128)S(1)}, f32[8,512]{1,0:T(8,128)S(1)}, u32[]{:S(2)}, u32[]{:S(2)}) collective-permute-start(f32[8,512]{1,0:T(8,128)S(1)} %shard_map.75.after_ref.first_ref), channel_id=1, source_target_pairs={{0,2},{1,3},{2,0},{3,1},{4,6},{5,7},{6,4},{7,5},{8,10},{9,11},{10,... | collective-permute-start | bytes 49160 | tf_op jit(solution)/shard_map/ppermute | solution.py:412
  9.6 2.9 %collective-permute-start.4 = (bf16[64,128]{1,0:T(8,128)(2,1)S(1)}, bf16[64,128]{1,0:T(8,128)(2,1)S(1)}, u32[]{:S(2)}, u32[]{:S(2)}) collective-permute-start(bf16[64,128]{1,0:T(8,128)(2,1)S(1)} %get-tuple-element.41.laid_ref.refs_2_), channel_id=1, source_target_pairs={{0,4},{4,0},{8,12},{12,8},{16,20},{20,16},{24,28},{28,24},{1,5},{5... | collective-permute-start | bytes 49160 | tf_op jit(solution)/shard_map/ppermute | solution.py:397
  9.7 5.9 %collective-permute-start.3 = (bf16[320,128]{1,0:T(8,128)(2,1)S(1)}, bf16[320,128]{1,0:T(8,128)(2,1)S(1)}, u32[]{:S(2)}, u32[]{:S(2)}) collective-permute-start(bf16[320,128]{1,0:T(8,128)(2,1)S(1)} %get-tuple-element.40), channel_id=1, source_target_pairs={{0,24},{4,28},{8,16},{12,20},{16,8},{20,12},{24,0},{28,4},{1,25},{... | collective-permute-start | bytes 245768 | tf_op jit(solution)/shard_map/ppermute | solution.py:397
  12.7 4.5 %collective-permute-start.5 = (bf16[288,128]{1,0:T(8,128)(2,1)S(1)}, bf16[288,128]{1,0:T(8,128)(2,1)S(1)}, u32[]{:S(2)}, u32[]{:S(2)}) collective-permute-start(bf16[288,128]{1,0:T(8,128)(2,1)S(1)} %get-tuple-element.47), channel_id=1, source_target_pairs={{0,16},{4,20},{8,24},{12,28},{16,0},{20,4},{24,8},{28,12},{1,17},{... | collective-permute-start | bytes 221192 | tf_op jit(solution)/shard_map/ppermute | solution.py:397
  13.3 4.4 %collective-permute-start.6 = (bf16[288,128]{1,0:T(8,128)(2,1)S(1)}, bf16[288,128]{1,0:T(8,128)(2,1)S(1)}, u32[]{:S(2)}, u32[]{:S(2)}) collective-permute-start(bf16[288,128]{1,0:T(8,128)(2,1)S(1)} %get-tuple-element.48), channel_id=1, source_target_pairs={{0,8},{4,12},{8,0},{12,4},{16,24},{20,28},{24,16},{28,20},{1,9},{5... | collective-permute-start | bytes 221192 | tf_op jit(solution)/shard_map/ppermute | solution.py:397
  15.8 1.2 %collective-permute-start.7 = (bf16[16,128]{1,0:T(8,128)(2,1)S(1)}, bf16[16,128]{1,0:T(8,128)(2,1)S(1)}, u32[]{:S(2)}, u32[]{:S(2)}) collective-permute-start(bf16[16,128]{1,0:T(8,128)(2,1)S(1)} %get-tuple-element.50), channel_id=1, source_target_pairs={{0,4},{4,0},{8,12},{12,8},{16,20},{20,16},{24,28},{28,24},{1,5},{5... | collective-permute-start | bytes 12296 | tf_op jit(solution)/shard_map/ppermute | solution.py:397

commit v10 on v8

--- a/solution.py
+++ b/solution.py
@@ -288,7 +288,10 @@
     block = jnp.where(facet_step < 2, facet_step, facet_step + 1)
     block = jnp.where(facet_step == facets - 2, 2, block)
     block = jnp.where(facet_step == facets - 1, facets - 1, block)
-    place = (block * subs + sub_step) * CAP + slot.astype(jnp.int32)
+    order = jnp.zeros_like(sub_step)
+    for n in range(bits):
+        order = order * 2 + ((sub_step >> n) & 1)
+    place = (block * subs + order) * CAP + slot.astype(jnp.int32)
     for at in range(0, rank_ref.shape[1], LANES):
         hit = iota((count, LANES), 1) + at == place
         rank_ref[:, at : at + LANES] = jnp.where(hit, 1.0, 0.0).astype(BF)
@@ -407,7 +410,7 @@
         cost_estimate=cost(10**11),
     )()
     held = grid_weight
-    steps = [1 << n for n in range(subs.bit_length() - 1)]
+    steps = [1 << n for n in reversed(range(subs.bit_length() - 1))]
     for step in steps:
         last, beside = held, lax.ppermute(held, "sub", [(k, k ^ step) for k in range(subs)])
         if step == steps[0]:

time: 19.4 us -> 19.4 us (level)
  no operation moved by 1% of the time
where the time goes in v10:
time: 19.4 us; the launch traced here: 19.2 us
  starting transfers between devices  10.7 us (55%)
  Pallas kernels  4.98 us (26%)
  waiting for transfers between devices  3.39 us (17%)
    ppermute x2, starting transfers between devices, local(): lax.ppermute(held, 'sub', [(k, k ^ step) for k in range(subs)])  5.95 us
    ppermute x6, starting transfers between devices, swap(): return lax.ppermute(x, 'facet', [(i, i ^ step) for i in range(facets)])  4.79 us
    ppermute x6, waiting for transfers between devices, swap(): return lax.ppermute(x, 'facet', [(i, i ^ step) for i in range(facets)])  2.95 us
    pallas_call x1, Pallas kernels, local(): pl.pallas_call(backward_kernel, out_shape=shaped((1, rows, 2 * length), F...  1.57 us
    pallas_call x1, Pallas kernels, local(): pl.pallas_call(forward_kernel, out_shape=[shaped((count * rows, LANES), B...  1.41 us
    pallas_call x1, Pallas kernels, local(): pl.pallas_call(functools.partial(prepare_kernel, subs, length), out_shape...  1.3 us
    ppermute x2, waiting for transfers between devices, local(): lax.ppermute(held, 'sub', [(k, k ^ step) for k in range(subs)])  0.44 us
  transfers between devices with their start and end apart: 8, of which 6 were waited for; matrix products, arithmetic and copies ran while one was open for 0% of the time, Pallas kernels for 18%

profile of v10, /device:TPU:0, one launch (start us, length us, event | category | flops | bytes accessed | tf_op | source)
XLA Modules:
  0.0 19.2 jit_solution(18007327261363320562)
XLA Ops:
  0.0 0.0 copy-start
  0.0 0.0 copy-start.2
  0.0 4.0 %collective-permute-start.1 = (f32[4,512]{1,0:T(4,128)}, f32[4,512]{1,0:T(4,128)S(1)}, u32[]{:S(2)}, u32[]{:S(2)}) collective-permute-start(f32[4,512]{1,0:T(4,128)} %first_ref.1), channel_id=1, source_target_pairs={{0,2},{1,3},{2,0},{3,1},{4,6},{5,7},{6,4},{7,5},{8,10},{9,11},{10,... | collective-permute-start | bytes 24584 | tf_op jit(solution)/shard_map/ppermute | solution.py:415
  4.0 0.1 shard_map.73
  4.2 0.0 copy-done
  4.2 0.0 copy-start.1
  4.2 1.4 %shard_map.74 = (bf16[256,128]{1,0:T(8,128)(2,1)S(1)}, bf16[256,512]{1,0:T(8,128)(2,1)S(1)}) custom-call(s32[32]{0:T(128)} %sub_hbm.3, s32[8]{0:T(128)} %off_hbm.3, bf16[1,8,8192]{2,1,0:T(8,128)(2,1)S(1)} %copy-done, f32[256,128]{1,0:T(8,128)S(1)} %get-tuple-element.31.turn_ref.refs_10_, bf16[64,128]{1,0:T(8,128)(2,1)S(1)} %get-tuple-element.32.fwd_ref), custom_call_target="tpu_custom_call" | custom-call | tf_op jit(solution)/shard_map/pallas_call | solution.py:417
  5.6 0.1 collective-permute-start
  5.7 0.2 collective-permute-done.1.second_ref
  5.9 0.0 copy-done.1
  5.9 1.9 %collective-permute-start.2 = (f32[8,512]{1,0:T(8,128)S(1)}, f32[8,512]{1,0:T(8,128)S(1)}, u32[]{:S(2)}, u32[]{:S(2)}) collective-permute-start(f32[8,512]{1,0:T(8,128)S(1)} %shard_map.75.after_ref.first_ref), channel_id=1, source_target_pairs={{0,1},{1,0},{2,3},{3,2},{4,5},{5,4},{6,7},{7,6},{8,9},{9,8},{10,11... | collective-permute-start | bytes 49160 | tf_op jit(solution)/shard_map/ppermute | solution.py:415
  7.8 0.0 copy-done.2
  7.8 1.3 %shard_map.76 = (f32[256,128]{1,0:T(8,128)S(1)}, f32[256,128]{1,0:T(8,128)S(1)}, bf16[512,128]{1,0:T(8,128)(2,1)S(1)}, bf16[512,128]{1,0:T(8,128)(2,1)S(1)}, bf1...) custom-call(s32[32]{0:T(128)} %sub_hbm.3, ...), custom_call_target="tpu_custom_call" | custom-call | flops 20000000000 | bytes 1048576 | tf_op jit(solution)/shard_map/pallas_call | solution.py:444
  9.1 0.0 collective-permute-done.passed_ref
  9.1 0.2 %shard_map.77 = (f32[256,128]{1,0:T(8,128)S(1)}, bf16[256,128]{1,0:T(8,128)(2,1)S(1)}, bf16[256,128]{1,0:T(8,128)(2,1)S(1)}, bf16[256,128]{1,0:T(8,128)(2,1)S(1)}) custom-call(bf16[256,128]{1,0:T(8,128)(2,1)S(1)} %get-tuple-element.33.windows_ref, bf16[256,128]{1,0:T(8,128)(2,1)S(1)} %collective-permute-done.passed_ref, ...), custom_call_target="tpu_custom_call" | custom-call | tf_op jit(solution)/shard_map/pallas_call | solution.py:474
  9.4 0.3 %collective-permute-done.2.second_ref = f32[8,512]{1,0:T(8,128)S(1)} collective-permute-done((f32[8,512]{1,0:T(8,128)S(1)}, f32[8,512]{1,0:T(8,128)S(1)}, u32[]{:S(2)}, u32[]{:S(2)}) %collective-permute-start.2) | collective-permute-done | bytes 16416 | tf_op jit(solution)/shard_map/ppermute | solution.py:415
  9.6 0.1 collective-permute-start.4
  9.7 2.8 %collective-permute-start.3 = (bf16[320,128]{1,0:T(8,128)(2,1)S(1)}, bf16[320,128]{1,0:T(8,128)(2,1)S(1)}, u32[]{:S(2)}, u32[]{:S(2)}) collective-permute-start(bf16[320,128]{1,0:T(8,128)(2,1)S(1)} %get-tuple-element.40), channel_id=1, source_target_pairs={{0,24},{4,28},{8,16},{12,20},{16,8},{20,12},{24,0},{28,4},{1,25},{... | collective-permute-start | bytes 245768 | tf_op jit(solution)/shard_map/ppermute | solution.py:400
  12.6 0.0 collective-permute-done.4.passed_ref.refs_3_
  12.6 0.1 shard_map.80
  12.7 0.6 %collective-permute-start.5 = (bf16[288,128]{1,0:T(8,128)(2,1)S(1)}, bf16[288,128]{1,0:T(8,128)(2,1)S(1)}, u32[]{:S(2)}, u32[]{:S(2)}) collective-permute-start(bf16[288,128]{1,0:T(8,128)(2,1)S(1)} %get-tuple-element.47), channel_id=1, source_target_pairs={{0,16},{4,20},{8,24},{12,28},{16,0},{20,4},{24,8},{28,12},{1,17},{... | collective-permute-start | bytes 221192 | tf_op jit(solution)/shard_map/ppermute | solution.py:400
  13.3 1.2 %collective-permute-start.6 = (bf16[288,128]{1,0:T(8,128)(2,1)S(1)}, bf16[288,128]{1,0:T(8,128)(2,1)S(1)}, u32[]{:S(2)}, u32[]{:S(2)}) collective-permute-start(bf16[288,128]{1,0:T(8,128)(2,1)S(1)} %get-tuple-element.48), channel_id=1, source_target_pairs={{0,8},{4,12},{8,0},{12,4},{16,24},{20,28},{24,16},{28,20},{1,9},{5... | collective-permute-start | bytes 221192 | tf_op jit(solution)/shard_map/ppermute | solution.py:400
  14.4 1.1 %collective-permute-done.3.block_ref = bf16[320,128]{1,0:T(8,128)(2,1)S(1)} collective-permute-done((bf16[320,128]{1,0:T(8,128)(2,1)S(1)}, bf16[320,128]{1,0:T(8,128)(2,1)S(1)}, u32[]{:S(2)}, u32[]{:S(2)}) %collective-permute-start.3) | collective-permute-done | bytes 81952 | tf_op jit(solution)/shard_map/ppermute | solution.py:400
  15.6 0.2 shard_map.79
  15.8 0.1 collective-permute-start.7
  15.8 1.2 %collective-permute-done.7.refs_3_ = bf16[16,128]{1,0:T(8,128)(2,1)S(1)} collective-permute-done((bf16[16,128]{1,0:T(8,128)(2,1)S(1)}, bf16[16,128]{1,0:T(8,128)(2,1)S(1)}, u32[]{:S(2)}, u32[]{:S(2)}) %collective-permute-start.7) | collective-permute-done | bytes 4128 | tf_op jit(solution)/shard_map/ppermute | solution.py:400
  17.0 0.2 collective-permute-done.5.refs_0_
  17.2 0.5 %collective-permute-done.6.refs_1_ = bf16[288,128]{1,0:T(8,128)(2,1)S(1)} collective-permute-done((bf16[288,128]{1,0:T(8,128)(2,1)S(1)}, bf16[288,128]{1,0:T(8,128)(2,1)S(1)}, u32[]{:S(2)}, u32[]{:S(2)}) %collective-permute-start.6) | collective-permute-done | bytes 73760 | tf_op jit(solution)/shard_map/ppermute | solution.py:400
  17.6 1.6 %shard_map.81 = f32[1,8,8192]{2,1,0:T(8,128)} custom-call(f32[256,128]{1,0:T(8,128)S(1)} %get-tuple-element.43.total_ref, bf16[288,128]{1,0:T(8,128)(2,1)S(1)} %collective-permute-done.5.refs_0_, bf16[288,128]{1,0:T(8,128)(2,1)S(1)} %collective-permute-done.6.refs_1_, bf16[48,128]{1,0:T(8,128)(2,1)S(1)} %get-tuple-element.49.refs_2_, ...), custom_call_target="tpu_custom_call" | custom-call | tf_op jit(solution)/shard_map/pallas_call | solution.py:514
  (2 shorter events, 0.0 us)
Async XLA Ops:
  0.0 4.2 %copy-start = (bf16[1,8,8192]{2,1,0:T(8,128)(2,1)S(1)}, bf16[1,8,8192]{2,1,0:T(8,128)(2,1)}, u32[]{:S(2)}) copy-start(bf16[1,8,8192]{2,1,0:T(8,128)(2,1)} %strips_ref.1) | copy-start | bytes 393220
  0.0 7.8 %copy-start.2 = (bf16[16,32,1024]{2,1,0:T(8,128)(2,1)S(1)}, bf16[16,32,1024]{2,1,0:T(8,128)(2,1)}, u32[]{:S(2)}) copy-start(bf16[16,32,1024]{2,1,0:T(8,128)(2,1)} %screens_ref.1) | copy-start | bytes 3145732
  0.0 5.9 %collective-permute-start.1 = (f32[4,512]{1,0:T(4,128)}, f32[4,512]{1,0:T(4,128)S(1)}, u32[]{:S(2)}, u32[]{:S(2)}) collective-permute-start(f32[4,512]{1,0:T(4,128)} %first_ref.1), channel_id=1, source_target_pairs={{0,2},{1,3},{2,0},{3,1},{4,6},{5,7},{6,4},{7,5},{8,10},{9,11},{10,... | collective-permute-start | bytes 24584 | tf_op jit(solution)/shard_map/ppermute | solution.py:415
  4.2 1.7 %copy-start.1 = (f32[4,512]{1,0:T(4,128)S(1)}, f32[4,512]{1,0:T(4,128)}, u32[]{:S(2)}) copy-start(f32[4,512]{1,0:T(4,128)} %first_ref.1) | copy-start | bytes 24580
  5.6 3.5 %collective-permute-start = (bf16[256,128]{1,0:T(8,128)(2,1)S(1)}, bf16[256,128]{1,0:T(8,128)(2,1)S(1)}, u32[]{:S(2)}, u32[]{:S(2)}) collective-permute-start(bf16[256,128]{1,0:T(8,128)(2,1)S(1)} %get-tuple-element.33.windows_ref), channel_id=1, source_target_pairs={{0,4},{4,0},{8,12},{12,8},{16,20},{20,16},{24,28},{28,24},{1,5},{5... | collective-permute-start | bytes 196616 | tf_op jit(solution)/shard_map/ppermute | solution.py:400
  5.9 3.7 %collective-permute-start.2 = (f32[8,512]{1,0:T(8,128)S(1)}, f32[8,512]{1,0:T(8,128)S(1)}, u32[]{:S(2)}, u32[]{:S(2)}) collective-permute-start(f32[8,512]{1,0:T(8,128)S(1)} %shard_map.75.after_ref.first_ref), channel_id=1, source_target_pairs={{0,1},{1,0},{2,3},{3,2},{4,5},{5,4},{6,7},{7,6},{8,9},{9,8},{10,11... | collective-permute-start | bytes 49160 | tf_op jit(solution)/shard_map/ppermute | solution.py:415
  9.6 2.9 %collective-permute-start.4 = (bf16[64,128]{1,0:T(8,128)(2,1)S(1)}, bf16[64,128]{1,0:T(8,128)(2,1)S(1)}, u32[]{:S(2)}, u32[]{:S(2)}) collective-permute-start(bf16[64,128]{1,0:T(8,128)(2,1)S(1)} %get-tuple-element.41.laid_ref.refs_2_), channel_id=1, source_target_pairs={{0,4},{4,0},{8,12},{12,8},{16,20},{20,16},{24,28},{28,24},{1,5},{5... | collective-permute-start | bytes 49160 | tf_op jit(solution)/shard_map/ppermute | solution.py:400
  9.7 5.9 %collective-permute-start.3 = (bf16[320,128]{1,0:T(8,128)(2,1)S(1)}, bf16[320,128]{1,0:T(8,128)(2,1)S(1)}, u32[]{:S(2)}, u32[]{:S(2)}) collective-permute-start(bf16[320,128]{1,0:T(8,128)(2,1)S(1)} %get-tuple-element.40), channel_id=1, source_target_pairs={{0,24},{4,28},{8,16},{12,20},{16,8},{20,12},{24,0},{28,4},{1,25},{... | collective-permute-start | bytes 245768 | tf_op jit(solution)/shard_map/ppermute | solution.py:400
  12.7 4.5 %collective-permute-start.5 = (bf16[288,128]{1,0:T(8,128)(2,1)S(1)}, bf16[288,128]{1,0:T(8,128)(2,1)S(1)}, u32[]{:S(2)}, u32[]{:S(2)}) collective-permute-start(bf16[288,128]{1,0:T(8,128)(2,1)S(1)} %get-tuple-element.47), channel_id=1, source_target_pairs={{0,16},{4,20},{8,24},{12,28},{16,0},{20,4},{24,8},{28,12},{1,17},{... | collective-permute-start | bytes 221192 | tf_op jit(solution)/shard_map/ppermute | solution.py:400
  13.3 4.4 %collective-permute-start.6 = (bf16[288,128]{1,0:T(8,128)(2,1)S(1)}, bf16[288,128]{1,0:T(8,128)(2,1)S(1)}, u32[]{:S(2)}, u32[]{:S(2)}) collective-permute-start(bf16[288,128]{1,0:T(8,128)(2,1)S(1)} %get-tuple-element.48), channel_id=1, source_target_pairs={{0,8},{4,12},{8,0},{12,4},{16,24},{20,28},{24,16},{28,20},{1,9},{5... | collective-permute-start | bytes 221192 | tf_op jit(solution)/shard_map/ppermute | solution.py:400
  15.8 1.2 %collective-permute-start.7 = (bf16[16,128]{1,0:T(8,128)(2,1)S(1)}, bf16[16,128]{1,0:T(8,128)(2,1)S(1)}, u32[]{:S(2)}, u32[]{:S(2)}) collective-permute-start(bf16[16,128]{1,0:T(8,128)(2,1)S(1)} %get-tuple-element.50), channel_id=1, source_target_pairs={{0,4},{4,0},{8,12},{12,8},{16,20},{20,16},{24,28},{28,24},{1,5},{5... | collective-permute-start | bytes 12296 | tf_op jit(solution)/shard_map/ppermute | solution.py:400
